TPU v7x, 32 devices: a whole 2x2x4 slice. The times are simulated.
32 devices in a mesh: au: 8 (over z, core), ia: 4 (over y, x).
Axes of the slice: x: 2, y: 2, z: 4, core: 2. Of those that a mesh axis runs over, the one named last changes fastest.
Arguments:
- user_emb: float32 [4096, 512], P('au'), may hold values from -6 to 6
- item_emb: float32 [8192, 512], P(('ia', 'au')), may hold values from -6 to 6
- tiles: bfloat16 [8, 48, 256, 256], P('au', 'ia'), may hold values from -0.15625 to 0.15625
- block_rows: int32 [8, 48], P('au', 'ia'), may hold values from 0 to 1
- block_cols: int32 [8, 48], P('au', 'ia'), may hold values from 0 to 7
- block_counts: int32 [8, 4], P('au', 'ia'), may hold values from 1 to 12, as said below
- w_self: float32 [512, 512], replicated, may hold values from -0.25 to 0.25
- w_inter: float32 [512, 512], replicated, may hold values from -0.25 to 0.25
Outputs:
- new_users: float32 [4096, 512], P(('au', 'ia'))
- new_items: float32 [8192, 512], P(('ia', 'au'))
Inputs may be any that keep to these rules, and one draw needn't show every extreme that they name: `block_counts`: slots at or after a device's count hold no block; within one device's first count slots the (row, column) pairs are distinct; some device lists 12 blocks.
All inputs are finite; a program needn't handle non-finite values.
Results may differ from a plain program's by a relative error of at most 0.0037.
Values may be sent and summed in bfloat16 or wider, within the bound.
No kernel may reach another device: no remote copies, remote signals or barrier semaphores. Data moves between devices by JAX's collectives and lax.ppermute only.
A program may use at most 64 MiB of HBM per device.

v0:
```python
import jax
import jax.numpy as jnp
from jax import lax
from jax.sharding import PartitionSpec as P


def update(side, emb, w_self, w_inter):
    mixed = jnp.dot(
        side + emb, w_self, precision=lax.Precision.HIGHEST, preferred_element_type=jnp.float32
    )
    mixed = mixed + jnp.dot(
        side * emb, w_inter, precision=lax.Precision.HIGHEST, preferred_element_type=jnp.float32
    )
    return jax.nn.leaky_relu(mixed, 0.2)


def local(user_emb, item_emb, tiles, block_rows, block_cols, block_counts, w_self, w_inter):
    local_tiles = tiles[0]
    rows = block_rows[0]
    cols = block_cols[0]
    count = block_counts[0, 0]
    width = item_emb.shape[1]
    edge = local_tiles.shape[1]
    item_rows = lax.all_gather(item_emb.astype(jnp.bfloat16), "au", axis=0, tiled=True)

    def user_turn(slot, partial_value):
        block = lax.dynamic_slice_in_dim(item_rows, cols[slot] * edge, edge, 0)
        term = jnp.dot(local_tiles[slot], block, preferred_element_type=jnp.float32)
        current = lax.dynamic_slice_in_dim(partial_value, rows[slot] * edge, edge, 0)
        return lax.dynamic_update_slice_in_dim(partial_value, current + term, rows[slot] * edge, 0)

    partial_value = lax.fori_loop(
        0, count, user_turn, jnp.zeros((user_emb.shape[0], width), jnp.float32)
    )
    own_rows = user_emb.shape[0] // lax.axis_size("ia")
    owned = lax.psum_scatter(partial_value, "ia", scatter_dimension=0, tiled=True)
    own_emb = lax.dynamic_slice_in_dim(user_emb, lax.axis_index("ia") * own_rows, own_rows, 0)
    new_users = update(owned, own_emb, w_self, w_inter)
    user_rows = lax.all_gather(new_users.astype(jnp.bfloat16), "ia", axis=0, tiled=True)

    def item_turn(slot, partial_items):
        block = lax.dynamic_slice_in_dim(user_rows, rows[slot] * edge, edge, 0)
        term = lax.dot_general(
            local_tiles[slot], block, (((0,), (0,)), ((), ())), preferred_element_type=jnp.float32
        )
        current = lax.dynamic_slice_in_dim(partial_items, cols[slot] * edge, edge, 0)
        return lax.dynamic_update_slice_in_dim(partial_items, current + term, cols[slot] * edge, 0)

    partial_items = lax.fori_loop(
        0, count, item_turn, jnp.zeros((item_rows.shape[0], width), jnp.float32)
    )
    owned_items = lax.psum_scatter(partial_items, "au", scatter_dimension=0, tiled=True)
    new_items = update(owned_items, item_emb, w_self, w_inter)
    return (new_users, new_items)


def solution(mesh):
    in_specs = (
        P("au", None),
        P(("ia", "au"), None),
        P("au", "ia", None, None),
        P("au", "ia"),
        P("au", "ia"),
        P("au", "ia"),
        P(),
        P(),
    )
    out_specs = (P(("au", "ia"), None), P(("ia", "au"), None))
    return jax.shard_map(local, mesh=mesh, in_specs=in_specs, out_specs=out_specs, check_vma=False)
```

profile of v0, /device:TPU:0, one launch (start us, length us, event | category | flops | bytes accessed | tf_op | source)
XLA Modules:
  0.0 266.9 jit_solution(4788696453053697507)
XLA Ops:
  7.2 1.9 convert_element_type.6
  9.2 32.9 %all-gather.2.cloned.1.call-done = bf16[2048,512]{1,0:T(8,128)(2,1)} async-done(((bf16[256,512]{1,0:T(8,128)(2,1)}), bf16[2048,512]{1,0:T(8,128)(2,1)}) %all-gather.2.cloned.1.call-update) | async-done | bytes 2097168 | tf_op jit(solution)/shard_map/all_gather | solution.py:24
  42.2 22.8 %while.20 = (s32[]{:T(128)}, f32[512,512]{1,0:T(8,128)S(1)}, s32[]{:T(128)}, s32[12]{0:T(128)S(1)}, bf16[12,256,256]{2,1,0:T(8,128)(2,1)}, /*index=5*/s32[12]{0:...) while((s32[]{:T(128)}, f32[512,512]{1,0:T(8,128)S(1)}, ...), condition=%wide.region_1.0_spmd, body=%wide.region_0.0_spmd.sunk | while | flops 67239952 | bytes 1442087 | solution.py:32
  45.4 1.3 fusion.33
  49.9 1.3 fusion.33
  54.3 1.3 fusion.33
  58.7 1.3 fusion.33
  63.1 1.3 fusion.33
  65.0 1.0 copy-done.1
  66.1 57.2 %reduce-scatter.3.cloned.1.call-done = f32[128,512]{1,0:T(8,128)} async-done(((f32[512,512]{1,0:T(8,128)}), f32[128,512]{1,0:T(8,128)}) %reduce-scatter.3.cloned.1.call-update) | async-done | bytes 262160 | tf_op jit(solution)/shard_map/reduce_scatter | solution.py:36
  123.3 1.7 fusion.14
  125.1 2.5 fusion.20
  127.5 9.9 %all_gather.7 = bf16[512,512]{1,0:T(8,128)(2,1)S(1)} all-gather(bf16[128,512]{1,0:T(8,128)(2,1)S(1)} %get-tuple-element.108), channel_id=1, replica_groups=mesh['au'=8,'ia'=4] {'ia'}, dimensions={0}, use_global_device_ids=true | all-gather | bytes 655360 | tf_op jit(solution)/shard_map/all_gather | solution.py:39
  137.5 2.5 broadcast_in_dim.7
  139.9 28.3 %while.21 = (s32[]{:T(128)}, f32[2048,512]{1,0:T(8,128)}, s32[]{:T(128)}, s32[12]{0:T(128)S(1)}, bf16[12,256,256]{2,1,0:T(8,128)(2,1)}, /*index=5*/s32[12]{0:T(1...) while((s32[]{:T(128)}, f32[2048,512]{1,0:T(8,128)}, ...), condition=%wide.region_4.5_spmd, body=%wide.region_3.4_spmd.sunk | while | flops 67239952 | bytes 1442087 | solution.py:49
  141.9 0.7 dynamic_slice.79
  143.3 2.2 fusion.36
  148.8 2.2 fusion.36
  154.3 2.2 fusion.36
  159.9 2.2 fusion.36
  165.4 2.2 fusion.36
  168.3 88.0 %reduce-scatter.5.cloned.1.call-done = f32[256,512]{1,0:T(8,128)} async-done(((f32[2048,512]{1,0:T(8,128)}), f32[256,512]{1,0:T(8,128)}) %reduce-scatter.5.cloned.1.call-update) | async-done | bytes 524304 | tf_op jit(solution)/shard_map/reduce_scatter | solution.py:52
  256.3 2.2 fusion.11
  258.5 1.9 compare_select_fusion
  (39 shorter events, 12.1 us)
Async XLA Ops:
  7.2 117.9 %copy-start = (f32[512,512]{1,0:T(8,128)S(1)}, f32[512,512]{1,0:T(8,128)}, u32[]{:S(2)}) copy-start(f32[512,512]{1,0:T(8,128)} %param.19) | copy-start | bytes 3145732
  7.2 35.0 %copy-start.6 = (s32[1,12]{1,0:T(1,128)S(1)}, s32[1,12]{1,0:T(1,128)}, u32[]{:S(2)}) copy-start(s32[1,12]{1,0:T(1,128)} %param.16) | copy-start | bytes 148
  7.2 35.0 %copy-start.5 = (s32[1,12]{1,0:T(1,128)S(1)}, s32[1,12]{1,0:T(1,128)}, u32[]{:S(2)}) copy-start(s32[1,12]{1,0:T(1,128)} %param.15) | copy-start | bytes 148
  7.2 34.8 %all-gather.2.cloned.1.call-start = ((), (), s32[]{:S(2)}) async-start(), calls=%async_computation.2 | async-start | bytes 2359296 | tf_op jit(solution)/shard_map/all_gather | solution.py:24
  9.1 114.2 %reduce-scatter.3.cloned.1.call-start = ((), (), s32[]{:S(2)}) async-start(), calls=%async_computation.3 | async-start | bytes 1310720 | tf_op jit(solution)/shard_map/reduce_scatter | solution.py:36
  42.2 81.1 %copy-start.3 = (f32[512,512]{1,0:T(8,128)S(1)}, f32[512,512]{1,0:T(8,128)}, u32[]{:S(2)}) copy-start(f32[512,512]{1,0:T(8,128)} %param.18) | copy-start | bytes 3145732
  65.0 1.0 copy-start.1
  66.0 190.3 %reduce-scatter.5.cloned.1.call-start = ((), (), s32[]{:S(2)}) async-start(), calls=%async_computation.4 | async-start | bytes 4718592 | tf_op jit(solution)/shard_map/reduce_scatter | solution.py:52
  168.3 88.1 %copy-start.2 = (f32[256,512]{1,0:T(8,128)S(1)}, f32[256,512]{1,0:T(8,128)}, u32[]{:S(2)}) copy-start(f32[256,512]{1,0:T(8,128)} %param.13) | copy-start | bytes 1572868
  256.3 2.2 copy-start.4
Sparse Core Ops, SparseCore 0:
  10.2 31.7 all-gather.1
  66.1 57.1 reduce-scatter.2
  168.4 87.8 reduce-scatter.4
where the time goes:
time: 269 us; the launch traced here: 267 us
  waiting for transfers between devices  178 us (66%)
  matrix products  25.5 us (9%)
  loops' own time  21.5 us (8%)
  local copies, waits for them, and re-layouts  16 us (6%)
  between operations  13.9 us (5%)
  blocking collectives  9.93 us (4%)
    reduce_scatter x1, waiting for transfers between devices, local(): lax.psum_scatter(partial_items, 'au', scatter_dimension=0, tiled=True)  88 us
    reduce_scatter x1, waiting for transfers between devices, local(): lax.psum_scatter(partial_value, 'ia', scatter_dimension=0, tiled=True)  57.2 us
    all_gather x1, waiting for transfers between devices, local(): lax.all_gather(item_emb.astype(jnp.bfloat16), 'au', axis=0, tiled=True)  32.9 us
    dot_general x5, matrix products, item_turn(): lax.dot_general(local_tiles[slot], block, (((0,), (0,)), ((), ())), prefe...  10.9 us
    another operation x1, loops' own time, local(): lax.fori_loop(0, count, item_turn, jnp.zeros((item_rows.shape[0], width),...  10.9 us
    another operation x1, loops' own time, local(): lax.fori_loop(0, count, user_turn, jnp.zeros((user_emb.shape[0], width),...  10.7 us
    all_gather x1, blocking collectives, local(): lax.all_gather(new_users.astype(jnp.bfloat16), 'ia', axis=0, tiled=True)  9.93 us
    dot_general x5, matrix products, user_turn(): term = jnp.dot(local_tiles[slot], block, preferred_element_type=jnp.float32)  6.28 us
  transfers between devices with their start and end apart: 3, of which 3 were waited for; matrix products, arithmetic and copies ran while one was open for 0% of the time, Pallas kernels for 0%

commit v1 on v0

v1 whole, which is shorter than its diff:
```python
import functools

import jax
import jax.numpy as jnp
from jax import lax
from jax.experimental import pallas as pl
from jax.experimental.pallas import tpu as pltpu
from jax.sharding import PartitionSpec as P

F32 = jnp.float32
BF16 = jnp.bfloat16
VMEM = pl.BlockSpec(memory_space=pltpu.VMEM)
SMEM = pl.BlockSpec(memory_space=pltpu.SMEM)
PARAMS = pltpu.CompilerParams(vmem_limit_bytes=40 * 1024 * 1024)


def call(kernel, out_shape, in_specs, flops=0, nbytes=0, scratch=()):
    return pl.pallas_call(
        kernel,
        out_shape=out_shape,
        in_specs=in_specs,
        out_specs=jax.tree.map(lambda _: VMEM, out_shape),
        scratch_shapes=scratch,
        compiler_params=PARAMS,
        cost_estimate=pl.CostEstimate(flops=flops, bytes_accessed=nbytes, transcendentals=0),
    )


def shape(*dims, dtype=BF16):
    return jax.ShapeDtypeStruct(dims, dtype)


def split(x):
    hi = x.astype(BF16)
    return hi, (x - hi.astype(F32)).astype(BF16)


def dot(a, b):
    return jnp.dot(a, b, preferred_element_type=F32)


def prepare(piece, direct, rows, cols, count, tiles, user_emb, w_self, w_inter, adj, adj_t, w_hi, w_lo, own):
    me_au = lax.axis_index("au") if direct[0] else 0
    me_ia = lax.axis_index("ia") if direct[1] else 0
    edge = tiles.shape[2]
    depth = w_self.shape[0]
    adj[...] = jnp.zeros_like(adj)
    adj_t[...] = jnp.zeros_like(adj_t)

    def place(slot, carry):
        col = pl.multiple_of((cols[0, slot] ^ me_au) * edge, edge)
        for part in range(edge // piece):
            at = (rows[0, slot] * (edge // piece) + part) ^ me_ia
            row = pl.multiple_of(at * piece, piece)
            block = tiles[0, slot, part * piece : (part + 1) * piece, :]
            adj[pl.ds(row, piece), pl.ds(col, edge)] = block
            adj_t[pl.ds(col, edge), pl.ds(row, piece)] = block.T
        return carry

    lax.fori_loop(0, count[0, 0], place, 0)
    for k, w in enumerate((w_self, w_inter)):
        w_hi[k * depth : (k + 1) * depth, :], w_lo[k * depth : (k + 1) * depth, :] = split(w[...])
    height = own.shape[0]
    own[...] = user_emb[pl.ds(pl.multiple_of(lax.axis_index("ia") * height, height), height), :]


def user_sums(n, adj, *refs):
    blocks, outs = refs[:n], refs[n:]
    total = None
    at = 0
    for block in blocks:
        term = dot(adj[:, at : at + block.shape[0]], block[...])
        total = term if total is None else total + term
        at += block.shape[0]
    height = outs[0].shape[0]
    for k, out in enumerate(outs):
        out[...] = total[k * height : (k + 1) * height].astype(out.dtype)


def item_sums(n, adj_t, *refs):
    shares, outs = refs[:n], refs[n:]
    users = jnp.concatenate([share[...] for share in shares], axis=0)
    height = outs[0].shape[0]
    for k, out in enumerate(outs):
        out[...] = dot(adj_t[k * height : (k + 1) * height, :], users).astype(out.dtype)


def update(n, emb, w_hi, w_lo, *refs):
    parts, outs = refs[:n], refs[n:]
    side = parts[0][...].astype(F32)
    for part in parts[1:]:
        side = side + part[...].astype(F32)
    own = emb[...]
    hi, lo = split(jnp.concatenate([side + own, side * own], axis=1))
    mixed = dot(hi, w_lo[...]) + dot(lo, w_hi[...]) + dot(hi, w_hi[...])
    mixed = jnp.where(mixed >= 0, mixed, 0.2 * mixed)
    for out in outs:
        out[...] = mixed.astype(out.dtype)


def chip_sums(n, *refs):
    mine, theirs, outs = refs[:n], refs[n : 2 * n], refs[2 * n :]
    for a, b, out in zip(mine, theirs, outs):
        out[...] = (a[...] + b[...].astype(F32)).astype(out.dtype)


def local(n_au, n_ia, user_emb, item_emb, tiles, block_rows, block_cols, block_counts, w_self, w_inter):
    edge = tiles.shape[2]
    depth = w_self.shape[0]
    users, held = user_emb.shape[0], item_emb.shape[0]
    items = held * n_au
    share = users // n_ia
    direct = (n_au == 8 and held == edge, n_ia == 4 and edge % share == 0)

    def swap(x, axis, n, by):
        return lax.ppermute(x, axis, [(i, i ^ by) for i in range(n)])

    item_half = item_emb.astype(BF16)
    if direct[0]:
        blocks = [None] * 8
        blocks[0] = item_half
        for k in (2, 4, 6):
            blocks[k] = swap(item_half, "au", 8, k)
        for k in (0, 2, 4, 6):
            blocks[k + 1] = swap(blocks[k], "au", 8, 1)
    else:
        blocks = [lax.all_gather(item_half, "au", axis=0, tiled=True)]

    adj, adj_t, w_hi, w_lo, own_emb = call(
        functools.partial(prepare, share if direct[1] else edge, direct),
        (shape(users, items), shape(items, users), shape(2 * depth, depth), shape(2 * depth, depth), shape(share, depth, dtype=F32)),
        [SMEM, SMEM, SMEM, VMEM, VMEM, VMEM, VMEM],
        nbytes=10 << 20,
    )(block_rows, block_cols, block_counts, tiles, user_emb, w_self, w_inter)

    work = 2 * users * items * depth
    if direct[1]:
        shares = (shape(share, depth, dtype=F32),) + (shape(share, depth),) * (n_ia - 1)
        sums = call(functools.partial(user_sums, len(blocks)), shares, [VMEM] * (1 + len(blocks)), work, 6 << 20)(adj, *blocks)
        sums = [sums[0]] + [swap(sums[k], "ia", n_ia, k) for k in range(1, n_ia)]
    else:
        (sums,) = call(functools.partial(user_sums, len(blocks)), (shape(users, depth, dtype=F32),), [VMEM] * (1 + len(blocks)), work, 6 << 20)(adj, *blocks)
        sums = [lax.psum_scatter(sums, "ia", scatter_dimension=0, tiled=True)]
    new_users, user_half = call(
        functools.partial(update, len(sums)),
        (shape(share, depth, dtype=F32), shape(share, depth)),
        [VMEM] * (3 + len(sums)),
        12 * share * depth * depth,
        3 << 20,
    )(own_emb, w_hi, w_lo, *sums)

    if direct[1]:
        halves = [user_half] + [swap(user_half, "ia", n_ia, k) for k in range(1, n_ia)]
    else:
        halves = [lax.all_gather(user_half, "ia", axis=0, tiled=True)]
    if direct[0]:
        shares = tuple(shape(held, depth, dtype=BF16 if k % 2 else F32) for k in range(8))
        sums = call(functools.partial(item_sums, len(halves)), shares, [VMEM] * (1 + len(halves)), work, 6 << 20)(adj_t, *halves)
        theirs = [swap(sums[k], "au", 8, 1) for k in (1, 3, 5, 7)]
        shares = (shape(held, depth, dtype=F32),) + (shape(held, depth),) * 3
        sums = call(functools.partial(chip_sums, 4), shares, [VMEM] * 8, 0, 6 << 20)(*sums[0::2], *theirs)
        sums = [sums[0]] + [swap(sums[k], "au", 8, 2 * k) for k in (1, 2, 3)]
    else:
        (sums,) = call(functools.partial(item_sums, len(halves)), (shape(items, depth, dtype=F32),), [VMEM] * (1 + len(halves)), work, 6 << 20)(adj_t, *halves)
        sums = [lax.psum_scatter(sums, "au", scatter_dimension=0, tiled=True)]
    (new_items,) = call(
        functools.partial(update, len(sums)),
        (shape(held, depth, dtype=F32),),
        [VMEM] * (3 + len(sums)),
        12 * held * depth * depth,
        4 << 20,
    )(item_emb, w_hi, w_lo, *sums)
    return (new_users, new_items)


def solution(mesh):
    in_specs = (
        P("au", None),
        P(("ia", "au"), None),
        P("au", "ia", None, None),
        P("au", "ia"),
        P("au", "ia"),
        P("au", "ia"),
        P(),
        P(),
    )
    out_specs = (P(("au", "ia"), None), P(("ia", "au"), None))
    return jax.shard_map(
        functools.partial(local, mesh.shape["au"], mesh.shape["ia"]),
        mesh=mesh,
        in_specs=in_specs,
        out_specs=out_specs,
        check_vma=False,
    )
```

time: 269 us -> 90 us (0.33)
  the two profiles are of different devices: /device:TPU:0 before, /device:TPU:8 now
where the time goes in v1:
time: 90 us; the launch traced here: 89.6 us
  waiting for transfers between devices  55.5 us (62%)
  starting transfers between devices  18.1 us (20%)
  Pallas kernels  7.21 us (8%)
  local copies, waits for them, and re-layouts  6.39 us (7%)
  between operations  1.39 us (2%)
  other arithmetic  1.08 us (1%)
    ppermute x20, waiting for transfers between devices, swap(): return lax.ppermute(x, axis, [(i, i ^ by) for i in range(n)])  55.5 us
    ppermute x20, starting transfers between devices, swap(): return lax.ppermute(x, axis, [(i, i ^ by) for i in range(n)])  18.1 us
    unnamed x14, local copies, waits for them, and re-layouts  6.39 us
    pallas_call x1, Pallas kernels, local(): call(functools.partial(update, len(sums)), (shape(held, depth, dtype=F32)...  1.81 us
  transfers between devices with their start and end apart: 20, of which 13 were waited for; matrix products, arithmetic and copies ran while one was open for 0% of the time, Pallas kernels for 2%

profile of v1, /device:TPU:8, one launch (start us, length us, event | category | flops | bytes accessed | tf_op | source)
XLA Modules:
  0.0 89.6 jit_solution(8768176287032142010)
XLA Ops:
  1.7 1.6 %collective-permute-start.5 = (bf16[256,512]{1,0:T(8,128)(2,1)S(1)}, bf16[256,512]{1,0:T(8,128)(2,1)S(1)}, u32[]{:S(2)}, u32[]{:S(2)}) collective-permute-start(bf16[256,512]{1,0:T(8,128)(2,1)S(1)} %convert_element_type.3.refs_0_), channel_id=1, source_target_pairs={{0,24},{4,28},{8,16},{12,20},{16,8},{20,12},{24,0},{28,4},{1,25},{... | collective-permute-start | bytes 786440 | tf_op jit(solution)/shard_map/ppermute | solution.py:116
  4.4 1.4 %collective-permute-start.1 = (bf16[256,512]{1,0:T(8,128)(2,1)S(1)}, bf16[256,512]{1,0:T(8,128)(2,1)S(1)}, u32[]{:S(2)}, u32[]{:S(2)}) collective-permute-start(bf16[256,512]{1,0:T(8,128)(2,1)S(1)} %convert_element_type.3.refs_0_), channel_id=1, source_target_pairs={{0,8},{4,12},{8,0},{12,4},{16,24},{20,28},{24,16},{28,20},{1,9},{5... | collective-permute-start | bytes 786440 | tf_op jit(solution)/shard_map/ppermute | solution.py:116
  5.8 16.2 %collective-permute-done.5.refs_6_ = bf16[256,512]{1,0:T(8,128)(2,1)S(1)} collective-permute-done((bf16[256,512]{1,0:T(8,128)(2,1)S(1)}, bf16[256,512]{1,0:T(8,128)(2,1)S(1)}, u32[]{:S(2)}, u32[]{:S(2)}) %collective-permute-start.5) | collective-permute-done | bytes 262176 | tf_op jit(solution)/shard_map/ppermute | solution.py:116
  22.0 3.7 %collective-permute-done.3.refs_4_ = bf16[256,512]{1,0:T(8,128)(2,1)S(1)} collective-permute-done((bf16[256,512]{1,0:T(8,128)(2,1)S(1)}, bf16[256,512]{1,0:T(8,128)(2,1)S(1)}, u32[]{:S(2)}, u32[]{:S(2)}) %collective-permute-start.3) | collective-permute-done | bytes 262176 | tf_op jit(solution)/shard_map/ppermute | solution.py:116
  26.9 1.4 %copy-done.1 = bf16[1,12,256,256]{3,2,1,0:T(8,128)(2,1)S(1)} copy-done((bf16[1,12,256,256]{3,2,1,0:T(8,128)(2,1)S(1)}, bf16[1,12,256,256]{3,2,1,0:T(8,128)(2,1)}, u32[]{:S(2)}) %copy-start.1) | copy-done | bytes 1572888
  28.3 1.2 %copy-done.2 = f32[512,512]{1,0:T(8,128)S(1)} copy-done((f32[512,512]{1,0:T(8,128)S(1)}, f32[512,512]{1,0:T(8,128)}, u32[]{:S(2)}) %copy-start.2) | copy-done | bytes 1048600
  29.6 1.2 %copy-done.3 = f32[512,512]{1,0:T(8,128)S(1)} copy-done((f32[512,512]{1,0:T(8,128)S(1)}, f32[512,512]{1,0:T(8,128)}, u32[]{:S(2)}) %copy-start.3) | copy-done | bytes 1048600
  30.8 1.2 %copy-done.4 = f32[512,512]{1,0:T(8,128)S(1)} copy-done((f32[512,512]{1,0:T(8,128)S(1)}, f32[512,512]{1,0:T(8,128)}, u32[]{:S(2)}) %copy-start.4) | copy-done | bytes 1048600
  33.3 1.4 %shard_map.95 = (bf16[512,2048]{1,0:T(8,128)(2,1)S(1)}, bf16[2048,512]{1,0:T(8,128)(2,1)S(1)}, bf16[1024,512]{1,0:T(8,128)(2,1)S(1)}, bf16[1024,512]{1,0:T(8,128)(2,1)S(1)}, f32[128,512]{1,0:T(8,128)S(1)}) custom-call(s32[1,12]{1,0:T(1,128)S(1)} %copy-done.5, s32[1,12]{1,0:T(1,128)S(1)} %copy-done.6, s32[1,1]{1,0:T(1,128)S(6)} %copy.10.count, ...), custom_call_target="tpu_custom_call" | custom-call | bytes 10485760 | tf_op jit(solution)/shard_map/pallas_call | solution.py:129
  34.8 1.2 %shard_map.96 = (f32[128,512]{1,0:T(8,128)S(1)}, bf16[128,512]{1,0:T(8,128)(2,1)S(1)}, bf16[128,512]{1,0:T(8,128)(2,1)S(1)}, bf16[128,512]{1,0:T(8,128)(2,1)S(1)}) custom-call(bf16[512,2048]{1,0:T(8,128)(2,1)S(1)} %get-tuple-element.28.adj, bf16[256,512]{1,0:T(8,128)(2,1)S(1)} %convert_element_type.3.refs_0_, ...), custom_call_target="tpu_custom_call" | custom-call | flops 1073741824 | bytes 6291456 | tf_op jit(solution)/shard_map/pallas_call | solution.py:139
  36.1 2.0 %collective-permute-start.7 = (bf16[128,512]{1,0:T(8,128)(2,1)S(1)}, bf16[128,512]{1,0:T(8,128)(2,1)S(1)}, u32[]{:S(2)}, u32[]{:S(2)}) collective-permute-start(bf16[128,512]{1,0:T(8,128)(2,1)S(1)} %get-tuple-element.30), channel_id=1, source_target_pairs={{0,1},{1,0},{2,3},{3,2},{4,5},{5,4},{6,7},{7,6},{8,9},{9,8},{10,11... | collective-permute-start | bytes 393224 | tf_op jit(solution)/shard_map/ppermute | solution.py:116
  39.7 2.8 %collective-permute-done.7.refs_1_ = bf16[128,512]{1,0:T(8,128)(2,1)S(1)} collective-permute-done((bf16[128,512]{1,0:T(8,128)(2,1)S(1)}, bf16[128,512]{1,0:T(8,128)(2,1)S(1)}, u32[]{:S(2)}, u32[]{:S(2)}) %collective-permute-start.7) | collective-permute-done | bytes 131104 | tf_op jit(solution)/shard_map/ppermute | solution.py:116
  42.5 3.4 %collective-permute-done.8.refs_2_ = bf16[128,512]{1,0:T(8,128)(2,1)S(1)} collective-permute-done((bf16[128,512]{1,0:T(8,128)(2,1)S(1)}, bf16[128,512]{1,0:T(8,128)(2,1)S(1)}, u32[]{:S(2)}, u32[]{:S(2)}) %collective-permute-start.8) | collective-permute-done | bytes 131104 | tf_op jit(solution)/shard_map/ppermute | solution.py:116
  45.9 1.3 %shard_map.97 = (f32[128,512]{1,0:T(8,128)}, bf16[128,512]{1,0:T(8,128)(2,1)S(1)}) custom-call(f32[128,512]{1,0:T(8,128)S(1)} %get-tuple-element.25.emb, bf16[1024,512]{1,0:T(8,128)(2,1)S(1)} %get-tuple-element.26.w_hi, bf16[1024,512]{1,0:T(8,128)(2,1)S(1)} %get-tuple-element.27.w_lo, f32[128,512]{1,0:T(8,128)S(1)} %get-tuple-element.29.refs_0_, ...), custom_call_target="tpu_custom_call" | custom-call | flops 402653184 | bytes 3145728 | tf_op jit(solution)/shard_map/pallas_call | solution.py:144
  47.2 1.5 %collective-permute-start.12 = (bf16[128,512]{1,0:T(8,128)(2,1)S(1)}, bf16[128,512]{1,0:T(8,128)(2,1)S(1)}, u32[]{:S(2)}, u32[]{:S(2)}) collective-permute-start(bf16[128,512]{1,0:T(8,128)(2,1)S(1)} %get-tuple-element.35.refs_0_), channel_id=1, source_target_pairs={{0,3},{1,2},{2,1},{3,0},{4,7},{5,6},{6,5},{7,4},{8,11},{9,10},{10,... | collective-permute-start | bytes 393224 | tf_op jit(solution)/shard_map/ppermute | solution.py:116
  50.7 3.1 %collective-permute-done.12.refs_3_ = bf16[128,512]{1,0:T(8,128)(2,1)S(1)} collective-permute-done((bf16[128,512]{1,0:T(8,128)(2,1)S(1)}, bf16[128,512]{1,0:T(8,128)(2,1)S(1)}, u32[]{:S(2)}, u32[]{:S(2)}) %collective-permute-start.12) | collective-permute-done | bytes 131104 | tf_op jit(solution)/shard_map/ppermute | solution.py:116
  53.9 1.3 %collective-permute-done.11.refs_2_ = bf16[128,512]{1,0:T(8,128)(2,1)S(1)} collective-permute-done((bf16[128,512]{1,0:T(8,128)(2,1)S(1)}, bf16[128,512]{1,0:T(8,128)(2,1)S(1)}, u32[]{:S(2)}, u32[]{:S(2)}) %collective-permute-start.11) | collective-permute-done | bytes 131104 | tf_op jit(solution)/shard_map/ppermute | solution.py:116
  55.2 1.3 %shard_map.98 = (f32[256,512]{1,0:T(8,128)S(1)}, bf16[256,512]{1,0:T(8,128)(2,1)S(1)}, f32[256,512]{1,0:T(8,128)S(1)}, bf16[256,512]{1,0:T(8,128)(2,1)S(1)}, f32...) custom-call(bf16[2048,512]{1,0:T(8,128)(2,1)S(1)} %get-tuple-element., ...), custom_call_target="tpu_custom_call" | custom-call | flops 1073741824 | bytes 6291456 | tf_op jit(solution)/shard_map/pallas_call | solution.py:158
  59.3 3.7 %collective-permute-start.17 = (bf16[256,512]{1,0:T(8,128)(2,1)S(1)}, bf16[256,512]{1,0:T(8,128)(2,1)S(1)}, u32[]{:S(2)}, u32[]{:S(2)}) collective-permute-start(bf16[256,512]{1,0:T(8,128)(2,1)S(1)} %get-tuple-element.45), channel_id=1, source_target_pairs={{0,8},{4,12},{8,0},{12,4},{16,24},{20,28},{24,16},{28,20},{1,9},{5... | collective-permute-start | bytes 786440 | tf_op jit(solution)/shard_map/ppermute | solution.py:116
  63.1 1.5 %collective-permute-start.19 = (bf16[256,512]{1,0:T(8,128)(2,1)S(1)}, bf16[256,512]{1,0:T(8,128)(2,1)S(1)}, u32[]{:S(2)}, u32[]{:S(2)}) collective-permute-start(bf16[256,512]{1,0:T(8,128)(2,1)S(1)} %get-tuple-element.47), channel_id=1, source_target_pairs={{0,24},{4,28},{8,16},{12,20},{16,8},{20,12},{24,0},{28,4},{1,25},{... | collective-permute-start | bytes 786440 | tf_op jit(solution)/shard_map/ppermute | solution.py:116
  64.6 8.5 %collective-permute-done.17.refs_1_ = bf16[256,512]{1,0:T(8,128)(2,1)S(1)} collective-permute-done((bf16[256,512]{1,0:T(8,128)(2,1)S(1)}, bf16[256,512]{1,0:T(8,128)(2,1)S(1)}, u32[]{:S(2)}, u32[]{:S(2)}) %collective-permute-start.17) | collective-permute-done | bytes 262176 | tf_op jit(solution)/shard_map/ppermute | solution.py:116
  73.1 7.9 %collective-permute-done.18.refs_2_ = bf16[256,512]{1,0:T(8,128)(2,1)S(1)} collective-permute-done((bf16[256,512]{1,0:T(8,128)(2,1)S(1)}, bf16[256,512]{1,0:T(8,128)(2,1)S(1)}, u32[]{:S(2)}, u32[]{:S(2)}) %collective-permute-start.18) | collective-permute-done | bytes 262176 | tf_op jit(solution)/shard_map/ppermute | solution.py:116
  81.0 6.8 %collective-permute-done.19.refs_3_ = bf16[256,512]{1,0:T(8,128)(2,1)S(1)} collective-permute-done((bf16[256,512]{1,0:T(8,128)(2,1)S(1)}, bf16[256,512]{1,0:T(8,128)(2,1)S(1)}, u32[]{:S(2)}, u32[]{:S(2)}) %collective-permute-start.19) | collective-permute-done | bytes 262176 | tf_op jit(solution)/shard_map/ppermute | solution.py:116
  87.8 1.8 %shard_map.100 = f32[256,512]{1,0:T(8,128)} custom-call(f32[256,512]{1,0:T(8,128)S(1)} %copy-done, bf16[1024,512]{1,0:T(8,128)(2,1)S(1)} %get-tuple-element.26.w_hi, bf16[1024,512]{1,0:T(8,128)(2,1)S(1)} %get-tuple-element.27.w_lo, f32[256,512]{1,0:T(8,128)S(1)} %get-tuple-element.44.refs_0_, bf16[256,512]{1,0:T(8,128)(2,1)S(1)} %collective-permute-done.17.refs_1_, ...), custom_call_target="tpu_custom_call" | custom-call | flops 805306368 | bytes 4194304 | tf_op jit(solution)/shard_map/pallas_call | solution.py:166
  (37 shorter events, 10.5 us)
Async XLA Ops:
  1.7 20.3 %collective-permute-start.5 = (bf16[256,512]{1,0:T(8,128)(2,1)S(1)}, bf16[256,512]{1,0:T(8,128)(2,1)S(1)}, u32[]{:S(2)}, u32[]{:S(2)}) collective-permute-start(bf16[256,512]{1,0:T(8,128)(2,1)S(1)} %convert_element_type.3.refs_0_), channel_id=1, source_target_pairs={{0,24},{4,28},{8,16},{12,20},{16,8},{20,12},{24,0},{28,4},{1,25},{... | collective-permute-start | bytes 786440 | tf_op jit(solution)/shard_map/ppermute | solution.py:116
  3.4 22.4 %collective-permute-start.3 = (bf16[256,512]{1,0:T(8,128)(2,1)S(1)}, bf16[256,512]{1,0:T(8,128)(2,1)S(1)}, u32[]{:S(2)}, u32[]{:S(2)}) collective-permute-start(bf16[256,512]{1,0:T(8,128)(2,1)S(1)} %convert_element_type.3.refs_0_), channel_id=1, source_target_pairs={{0,16},{4,20},{8,24},{12,28},{16,0},{20,4},{24,8},{28,12},{1,17},{... | collective-permute-start | bytes 786440 | tf_op jit(solution)/shard_map/ppermute | solution.py:116
  4.4 21.3 %collective-permute-start.1 = (bf16[256,512]{1,0:T(8,128)(2,1)S(1)}, bf16[256,512]{1,0:T(8,128)(2,1)S(1)}, u32[]{:S(2)}, u32[]{:S(2)}) collective-permute-start(bf16[256,512]{1,0:T(8,128)(2,1)S(1)} %convert_element_type.3.refs_0_), channel_id=1, source_target_pairs={{0,8},{4,12},{8,0},{12,4},{16,24},{20,28},{24,16},{28,20},{1,9},{5... | collective-permute-start | bytes 786440 | tf_op jit(solution)/shard_map/ppermute | solution.py:116
  5.8 28.9 %collective-permute-start = (bf16[256,512]{1,0:T(8,128)(2,1)S(1)}, bf16[256,512]{1,0:T(8,128)(2,1)S(1)}, u32[]{:S(2)}, u32[]{:S(2)}) collective-permute-start(bf16[256,512]{1,0:T(8,128)(2,1)S(1)} %convert_element_type.3.refs_0_), channel_id=1, source_target_pairs={{0,4},{4,0},{8,12},{12,8},{16,20},{20,16},{24,28},{28,24},{1,5},{5... | collective-permute-start | bytes 786440 | tf_op jit(solution)/shard_map/ppermute | solution.py:116
  22.0 12.8 %collective-permute-start.6 = (bf16[256,512]{1,0:T(8,128)(2,1)S(1)}, bf16[256,512]{1,0:T(8,128)(2,1)S(1)}, u32[]{:S(2)}, u32[]{:S(2)}) collective-permute-start(bf16[256,512]{1,0:T(8,128)(2,1)S(1)} %collective-permute-done.5.refs_6_), channel_id=1, source_target_pairs={{0,4},{4,0},{8,12},{12,8},{16,20},{20,16},{24,28},{28,24},{1,5},{5... | collective-permute-start | bytes 786440 | tf_op jit(solution)/shard_map/ppermute | solution.py:116
  25.8 9.0 %collective-permute-start.4 = (bf16[256,512]{1,0:T(8,128)(2,1)S(1)}, bf16[256,512]{1,0:T(8,128)(2,1)S(1)}, u32[]{:S(2)}, u32[]{:S(2)}) collective-permute-start(bf16[256,512]{1,0:T(8,128)(2,1)S(1)} %collective-permute-done.3.refs_4_), channel_id=1, source_target_pairs={{0,4},{4,0},{8,12},{12,8},{16,20},{20,16},{24,28},{28,24},{1,5},{5... | collective-permute-start | bytes 786440 | tf_op jit(solution)/shard_map/ppermute | solution.py:116
  25.8 9.0 %collective-permute-start.2 = (bf16[256,512]{1,0:T(8,128)(2,1)S(1)}, bf16[256,512]{1,0:T(8,128)(2,1)S(1)}, u32[]{:S(2)}, u32[]{:S(2)}) collective-permute-start(bf16[256,512]{1,0:T(8,128)(2,1)S(1)} %collective-permute-done.1.refs_2_), channel_id=1, source_target_pairs={{0,4},{4,0},{8,12},{12,8},{16,20},{20,16},{24,28},{28,24},{1,5},{5... | collective-permute-start | bytes 786440 | tf_op jit(solution)/shard_map/ppermute | solution.py:116
  26.9 1.4 %copy-start.1 = (bf16[1,12,256,256]{3,2,1,0:T(8,128)(2,1)S(1)}, bf16[1,12,256,256]{3,2,1,0:T(8,128)(2,1)}, u32[]{:S(2)}) copy-start(bf16[1,12,256,256]{3,2,1,0:T(8,128)(2,1)} %tiles.1) | copy-start | bytes 4718596
  29.6 1.2 %copy-start.3 = (f32[512,512]{1,0:T(8,128)S(1)}, f32[512,512]{1,0:T(8,128)}, u32[]{:S(2)}) copy-start(f32[512,512]{1,0:T(8,128)} %w_self.1) | copy-start | bytes 3145732
  30.8 1.2 %copy-start.4 = (f32[512,512]{1,0:T(8,128)S(1)}, f32[512,512]{1,0:T(8,128)}, u32[]{:S(2)}) copy-start(f32[512,512]{1,0:T(8,128)} %w_inter.1) | copy-start | bytes 3145732
  36.1 6.4 %collective-permute-start.7 = (bf16[128,512]{1,0:T(8,128)(2,1)S(1)}, bf16[128,512]{1,0:T(8,128)(2,1)S(1)}, u32[]{:S(2)}, u32[]{:S(2)}) collective-permute-start(bf16[128,512]{1,0:T(8,128)(2,1)S(1)} %get-tuple-element.30), channel_id=1, source_target_pairs={{0,1},{1,0},{2,3},{3,2},{4,5},{5,4},{6,7},{7,6},{8,9},{9,8},{10,11... | collective-permute-start | bytes 393224 | tf_op jit(solution)/shard_map/ppermute | solution.py:116
  38.1 7.8 %collective-permute-start.8 = (bf16[128,512]{1,0:T(8,128)(2,1)S(1)}, bf16[128,512]{1,0:T(8,128)(2,1)S(1)}, u32[]{:S(2)}, u32[]{:S(2)}) collective-permute-start(bf16[128,512]{1,0:T(8,128)(2,1)S(1)} %get-tuple-element.31), channel_id=1, source_target_pairs={{0,2},{1,3},{2,0},{3,1},{4,6},{5,7},{6,4},{7,5},{8,10},{9,11},{10,... | collective-permute-start | bytes 393224 | tf_op jit(solution)/shard_map/ppermute | solution.py:116
  38.9 7.0 %collective-permute-start.9 = (bf16[128,512]{1,0:T(8,128)(2,1)S(1)}, bf16[128,512]{1,0:T(8,128)(2,1)S(1)}, u32[]{:S(2)}, u32[]{:S(2)}) collective-permute-start(bf16[128,512]{1,0:T(8,128)(2,1)S(1)} %get-tuple-element.32), channel_id=1, source_target_pairs={{0,3},{1,2},{2,1},{3,0},{4,7},{5,6},{6,5},{7,4},{8,11},{9,10},{10,... | collective-permute-start | bytes 393224 | tf_op jit(solution)/shard_map/ppermute | solution.py:116
  47.2 6.6 %collective-permute-start.12 = (bf16[128,512]{1,0:T(8,128)(2,1)S(1)}, bf16[128,512]{1,0:T(8,128)(2,1)S(1)}, u32[]{:S(2)}, u32[]{:S(2)}) collective-permute-start(bf16[128,512]{1,0:T(8,128)(2,1)S(1)} %get-tuple-element.35.refs_0_), channel_id=1, source_target_pairs={{0,3},{1,2},{2,1},{3,0},{4,7},{5,6},{6,5},{7,4},{8,11},{9,10},{10,... | collective-permute-start | bytes 393224 | tf_op jit(solution)/shard_map/ppermute | solution.py:116
  48.8 6.4 %collective-permute-start.11 = (bf16[128,512]{1,0:T(8,128)(2,1)S(1)}, bf16[128,512]{1,0:T(8,128)(2,1)S(1)}, u32[]{:S(2)}, u32[]{:S(2)}) collective-permute-start(bf16[128,512]{1,0:T(8,128)(2,1)S(1)} %get-tuple-element.35.refs_0_), channel_id=1, source_target_pairs={{0,2},{1,3},{2,0},{3,1},{4,6},{5,7},{6,4},{7,5},{8,10},{9,11},{10,... | collective-permute-start | bytes 393224 | tf_op jit(solution)/shard_map/ppermute | solution.py:116
  49.6 5.6 %collective-permute-start.10 = (bf16[128,512]{1,0:T(8,128)(2,1)S(1)}, bf16[128,512]{1,0:T(8,128)(2,1)S(1)}, u32[]{:S(2)}, u32[]{:S(2)}) collective-permute-start(bf16[128,512]{1,0:T(8,128)(2,1)S(1)} %get-tuple-element.35.refs_0_), channel_id=1, source_target_pairs={{0,1},{1,0},{2,3},{3,2},{4,5},{5,4},{6,7},{7,6},{8,9},{9,8},{10,11... | collective-permute-start | bytes 393224 | tf_op jit(solution)/shard_map/ppermute | solution.py:116
  56.4 31.4 %copy-start = (f32[256,512]{1,0:T(8,128)S(1)}, f32[256,512]{1,0:T(8,128)}, u32[]{:S(2)}) copy-start(f32[256,512]{1,0:T(8,128)} %emb.1) | copy-start | bytes 1572868
  56.4 1.6 %collective-permute-start.13 = (bf16[256,512]{1,0:T(8,128)(2,1)S(1)}, bf16[256,512]{1,0:T(8,128)(2,1)S(1)}, u32[]{:S(2)}, u32[]{:S(2)}) collective-permute-start(bf16[256,512]{1,0:T(8,128)(2,1)S(1)} %get-tuple-element.40), channel_id=1, source_target_pairs={{0,4},{4,0},{8,12},{12,8},{16,20},{20,16},{24,28},{28,24},{1,5},{5... | collective-permute-start | bytes 786440 | tf_op jit(solution)/shard_map/ppermute | solution.py:116
  56.5 1.9 %collective-permute-start.14 = (bf16[256,512]{1,0:T(8,128)(2,1)S(1)}, bf16[256,512]{1,0:T(8,128)(2,1)S(1)}, u32[]{:S(2)}, u32[]{:S(2)}) collective-permute-start(bf16[256,512]{1,0:T(8,128)(2,1)S(1)} %get-tuple-element.41), channel_id=1, source_target_pairs={{0,4},{4,0},{8,12},{12,8},{16,20},{20,16},{24,28},{28,24},{1,5},{5... | collective-permute-start | bytes 786440 | tf_op jit(solution)/shard_map/ppermute | solution.py:116
  57.0 1.8 %collective-permute-start.15 = (bf16[256,512]{1,0:T(8,128)(2,1)S(1)}, bf16[256,512]{1,0:T(8,128)(2,1)S(1)}, u32[]{:S(2)}, u32[]{:S(2)}) collective-permute-start(bf16[256,512]{1,0:T(8,128)(2,1)S(1)} %get-tuple-element.42), channel_id=1, source_target_pairs={{0,4},{4,0},{8,12},{12,8},{16,20},{20,16},{24,28},{28,24},{1,5},{5... | collective-permute-start | bytes 786440 | tf_op jit(solution)/shard_map/ppermute | solution.py:116
  57.1 2.1 %collective-permute-start.16 = (bf16[256,512]{1,0:T(8,128)(2,1)S(1)}, bf16[256,512]{1,0:T(8,128)(2,1)S(1)}, u32[]{:S(2)}, u32[]{:S(2)}) collective-permute-start(bf16[256,512]{1,0:T(8,128)(2,1)S(1)} %get-tuple-element.43), channel_id=1, source_target_pairs={{0,4},{4,0},{8,12},{12,8},{16,20},{20,16},{24,28},{28,24},{1,5},{5... | collective-permute-start | bytes 786440 | tf_op jit(solution)/shard_map/ppermute | solution.py:116
  59.3 13.7 %collective-permute-start.17 = (bf16[256,512]{1,0:T(8,128)(2,1)S(1)}, bf16[256,512]{1,0:T(8,128)(2,1)S(1)}, u32[]{:S(2)}, u32[]{:S(2)}) collective-permute-start(bf16[256,512]{1,0:T(8,128)(2,1)S(1)} %get-tuple-element.45), channel_id=1, source_target_pairs={{0,8},{4,12},{8,0},{12,4},{16,24},{20,28},{24,16},{28,20},{1,9},{5... | collective-permute-start | bytes 786440 | tf_op jit(solution)/shard_map/ppermute | solution.py:116
  63.0 17.9 %collective-permute-start.18 = (bf16[256,512]{1,0:T(8,128)(2,1)S(1)}, bf16[256,512]{1,0:T(8,128)(2,1)S(1)}, u32[]{:S(2)}, u32[]{:S(2)}) collective-permute-start(bf16[256,512]{1,0:T(8,128)(2,1)S(1)} %get-tuple-element.46), channel_id=1, source_target_pairs={{0,16},{4,20},{8,24},{12,28},{16,0},{20,4},{24,8},{28,12},{1,17},{... | collective-permute-start | bytes 786440 | tf_op jit(solution)/shard_map/ppermute | solution.py:116
  63.1 24.8 %collective-permute-start.19 = (bf16[256,512]{1,0:T(8,128)(2,1)S(1)}, bf16[256,512]{1,0:T(8,128)(2,1)S(1)}, u32[]{:S(2)}, u32[]{:S(2)}) collective-permute-start(bf16[256,512]{1,0:T(8,128)(2,1)S(1)} %get-tuple-element.47), channel_id=1, source_target_pairs={{0,24},{4,28},{8,16},{12,20},{16,8},{20,12},{24,0},{28,4},{1,25},{... | collective-permute-start | bytes 786440 | tf_op jit(solution)/shard_map/ppermute | solution.py:116
  (3 other events, 2.5 us)

commit v2 on v1

--- a/solution.py
+++ b/solution.py
@@ -39,16 +39,19 @@
     return jnp.dot(a, b, preferred_element_type=F32)
 
 
-def prepare(piece, direct, rows, cols, count, tiles, user_emb, w_self, w_inter, adj, adj_t, w_hi, w_lo, own):
+def dense(piece, direct, rows, cols, count, item_half, tiles, adj, adj_t, again):
     me_au = lax.axis_index("au") if direct[0] else 0
     me_ia = lax.axis_index("ia") if direct[1] else 0
     edge = tiles.shape[2]
-    depth = w_self.shape[0]
+    again[...] = item_half[...]
     adj[...] = jnp.zeros_like(adj)
     adj_t[...] = jnp.zeros_like(adj_t)
 
     def place(slot, carry):
-        col = pl.multiple_of((cols[0, slot] ^ me_au) * edge, edge)
+        at = cols[0, slot]
+        if direct[0]:
+            at = slot_of(me_au, at)
+        col = pl.multiple_of(at * edge, edge)
         for part in range(edge // piece):
             at = (rows[0, slot] * (edge // piece) + part) ^ me_ia
             row = pl.multiple_of(at * piece, piece)
@@ -58,20 +61,48 @@
         return carry
 
     lax.fori_loop(0, count[0, 0], place, 0)
+
+
+def halves_of(item_half, user_emb, w_self, w_inter, w_hi, w_lo, own, again):
+    depth = w_self.shape[0]
+    again[...] = item_half[...]
     for k, w in enumerate((w_self, w_inter)):
         w_hi[k * depth : (k + 1) * depth, :], w_lo[k * depth : (k + 1) * depth, :] = split(w[...])
     height = own.shape[0]
     own[...] = user_emb[pl.ds(pl.multiple_of(lax.axis_index("ia") * height, height), height), :]
 
 
-def user_sums(n, adj, *refs):
-    blocks, outs = refs[:n], refs[n:]
+def slot_of(me, block):
+    apart = block ^ me
+    z, turn = me >> 1, apart >> 1
+    swapped = ((z == 1) | (z == 2)) & ((turn == 1) | (turn == 2))
+    return jnp.where(swapped, 3 - turn, turn) * 2 + (apart & 1)
+
+
+TURN_1 = ((0, 2), (3, 1), (1, 0), (2, 3))
+TURN_2 = ((0, 1), (3, 2), (1, 3), (2, 0))
+MIDDLE = ((1, 2), (2, 1))
+ENDS = ((2, 3), (1, 0))
+
+
+def back(pairs):
+    return tuple((b, a) for a, b in pairs)
+
+
+def send(x, pairs):
+    return lax.ppermute(x, "au", [(2 * a + core, 2 * b + core) for a, b in pairs for core in (0, 1)])
+
+
+def user_sums(sizes, adj, *refs):
+    blocks, outs = refs[: sum(sizes)], refs[sum(sizes) :]
     total = None
-    at = 0
-    for block in blocks:
-        term = dot(adj[:, at : at + block.shape[0]], block[...])
+    at = first = 0
+    for size in sizes:
+        block = sum((ref[...] for ref in blocks[first + 1 : first + size]), blocks[first][...])
+        term = dot(adj[:, at : at + block.shape[0]], block)
         total = term if total is None else total + term
         at += block.shape[0]
+        first += size
     height = outs[0].shape[0]
     for k, out in enumerate(outs):
         out[...] = total[k * height : (k + 1) * height].astype(out.dtype)
@@ -101,7 +132,7 @@
 def chip_sums(n, *refs):
     mine, theirs, outs = refs[:n], refs[n : 2 * n], refs[2 * n :]
     for a, b, out in zip(mine, theirs, outs):
-        out[...] = (a[...] + b[...].astype(F32)).astype(out.dtype)
+        out[...] = (a[...].astype(F32) + b[...].astype(F32)).astype(out.dtype)
 
 
 def local(n_au, n_ia, user_emb, item_emb, tiles, block_rows, block_cols, block_counts, w_self, w_inter):
@@ -117,29 +148,38 @@
 
     item_half = item_emb.astype(BF16)
     if direct[0]:
-        blocks = [None] * 8
-        blocks[0] = item_half
-        for k in (2, 4, 6):
-            blocks[k] = swap(item_half, "au", 8, k)
-        for k in (0, 2, 4, 6):
-            blocks[k + 1] = swap(blocks[k], "au", 8, 1)
-    else:
-        blocks = [lax.all_gather(item_half, "au", axis=0, tiled=True)]
-
-    adj, adj_t, w_hi, w_lo, own_emb = call(
-        functools.partial(prepare, share if direct[1] else edge, direct),
-        (shape(users, items), shape(items, users), shape(2 * depth, depth), shape(2 * depth, depth), shape(share, depth, dtype=F32)),
-        [SMEM, SMEM, SMEM, VMEM, VMEM, VMEM, VMEM],
-        nbytes=10 << 20,
-    )(block_rows, block_cols, block_counts, tiles, user_emb, w_self, w_inter)
+        first = send(item_half, TURN_1)
+
+    adj, adj_t, again = call(
+        functools.partial(dense, share if direct[1] else edge, direct),
+        (shape(users, items), shape(items, users), shape(held, depth)),
+        [SMEM, SMEM, SMEM, VMEM, VMEM],
+        nbytes=8 << 20,
+    )(block_rows, block_cols, block_counts, item_half, tiles)
+    w_hi, w_lo, own_emb, later = call(
+        halves_of,
+        (shape(2 * depth, depth), shape(2 * depth, depth), shape(share, depth, dtype=F32), shape(held, depth)),
+        [VMEM] * 4,
+        nbytes=5 << 20,
+    )(again, user_emb, w_self, w_inter)
+    if direct[0]:
+        second = send(again, TURN_2)
+        middle = send(later, MIDDLE)
+        ends = send(first, ENDS)
+        groups = ((item_half,), (first,), (second,), (middle, ends))
+        groups = tuple(g for group in groups for g in (group, tuple(swap(x, "au", 8, 1) for x in group)))
+    else:
+        groups = ((lax.all_gather(item_half, "au", axis=0, tiled=True),),)
+    blocks = [x for group in groups for x in group]
+    sizes = tuple(len(group) for group in groups)
 
     work = 2 * users * items * depth
     if direct[1]:
         shares = (shape(share, depth, dtype=F32),) + (shape(share, depth),) * (n_ia - 1)
-        sums = call(functools.partial(user_sums, len(blocks)), shares, [VMEM] * (1 + len(blocks)), work, 6 << 20)(adj, *blocks)
+        sums = call(functools.partial(user_sums, sizes), shares, [VMEM] * (1 + len(blocks)), work, 6 << 20)(adj, *blocks)
         sums = [sums[0]] + [swap(sums[k], "ia", n_ia, k) for k in range(1, n_ia)]
     else:
-        (sums,) = call(functools.partial(user_sums, len(blocks)), (shape(users, depth, dtype=F32),), [VMEM] * (1 + len(blocks)), work, 6 << 20)(adj, *blocks)
+        (sums,) = call(functools.partial(user_sums, sizes), (shape(users, depth, dtype=F32),), [VMEM] * (1 + len(blocks)), work, 6 << 20)(adj, *blocks)
         sums = [lax.psum_scatter(sums, "ia", scatter_dimension=0, tiled=True)]
     new_users, user_half = call(
         functools.partial(update, len(sums)),
@@ -159,7 +199,10 @@
         theirs = [swap(sums[k], "au", 8, 1) for k in (1, 3, 5, 7)]
         shares = (shape(held, depth, dtype=F32),) + (shape(held, depth),) * 3
         sums = call(functools.partial(chip_sums, 4), shares, [VMEM] * 8, 0, 6 << 20)(*sums[0::2], *theirs)
-        sums = [sums[0]] + [swap(sums[k], "au", 8, 2 * k) for k in (1, 2, 3)]
+        handed = send(sums[3], back(ENDS))
+        arrived = [send(sums[2], back(TURN_2)), send(sums[3], back(MIDDLE))]
+        (onward,) = call(functools.partial(chip_sums, 1), (shape(held, depth),), [VMEM] * 2, 0, 1 << 20)(sums[1], handed)
+        sums = [sums[0], send(onward, back(TURN_1))] + arrived
     else:
         (sums,) = call(functools.partial(item_sums, len(halves)), (shape(items, depth, dtype=F32),), [VMEM] * (1 + len(halves)), work, 6 << 20)(adj_t, *halves)
         sums = [lax.psum_scatter(sums, "au", scatter_dimension=0, tiled=True)]

time: 90 us -> 76.5 us (0.85)
  the two profiles are of different devices: /device:TPU:8 before, /device:TPU:0 now
where the time goes in v2:
time: 76.5 us; the launch traced here: 76.3 us
  waiting for transfers between devices  38.6 us (50%)
  starting transfers between devices  22.8 us (30%)
  Pallas kernels  7.06 us (9%)
  local copies, waits for them, and re-layouts  5.4 us (7%)
  between operations  1.43 us (2%)
  other arithmetic  1.08 us (1%)
    ppermute x8, waiting for transfers between devices, send(): lax.ppermute(x, 'au', [(2 * a + core, 2 * b + core) for a, b in pairs for...  24.5 us
    ppermute x15, waiting for transfers between devices, swap(): return lax.ppermute(x, axis, [(i, i ^ by) for i in range(n)])  14.1 us
    ppermute x8, starting transfers between devices, send(): lax.ppermute(x, 'au', [(2 * a + core, 2 * b + core) for a, b in pairs for...  13.6 us
    ppermute x15, starting transfers between devices, swap(): return lax.ppermute(x, axis, [(i, i ^ by) for i in range(n)])  9.21 us
    unnamed x14, local copies, waits for them, and re-layouts  5.4 us
    pallas_call x1, Pallas kernels, local(): call(functools.partial(update, len(sums)), (shape(held, depth, dtype=F32)...  1.81 us
  transfers between devices with their start and end apart: 23, of which 15 were waited for; matrix products, arithmetic and copies ran while one was open for 0% of the time, Pallas kernels for 2%

profile of v2, /device:TPU:0, one launch (start us, length us, event | category | flops | bytes accessed | tf_op | source)
XLA Modules:
  0.0 76.3 jit_solution(8273037141345296280)
XLA Ops:
  1.7 4.1 %collective-permute-start.1 = (bf16[256,512]{1,0:T(8,128)(2,1)S(1)}, bf16[256,512]{1,0:T(8,128)(2,1)S(1)}, u32[]{:S(2)}, u32[]{:S(2)}) collective-permute-start(bf16[256,512]{1,0:T(8,128)(2,1)S(1)} %convert_element_type.3.item_half.refs_0_), channel_id=1, source_target_pairs={{0,16},{4,20},{24,8},{28,12},{8,0},{12,4},{16,24},{20,28},{1,17},{... | collective-permute-start | bytes 786440 | tf_op jit(solution)/shard_map/ppermute | solution.py:93
  6.5 1.4 %copy-done.1 = bf16[1,12,256,256]{3,2,1,0:T(8,128)(2,1)S(1)} copy-done((bf16[1,12,256,256]{3,2,1,0:T(8,128)(2,1)S(1)}, bf16[1,12,256,256]{3,2,1,0:T(8,128)(2,1)}, u32[]{:S(2)}) %copy-start.1) | copy-done | bytes 1572888
  10.4 1.2 %copy-done.3 = f32[512,512]{1,0:T(8,128)S(1)} copy-done((f32[512,512]{1,0:T(8,128)S(1)}, f32[512,512]{1,0:T(8,128)}, u32[]{:S(2)}) %copy-start.3) | copy-done | bytes 1048600
  13.9 1.3 %collective-permute-start.6 = (bf16[256,512]{1,0:T(8,128)(2,1)S(1)}, bf16[256,512]{1,0:T(8,128)(2,1)S(1)}, u32[]{:S(2)}, u32[]{:S(2)}) collective-permute-start(bf16[256,512]{1,0:T(8,128)(2,1)S(1)} %collective-permute-done.1.refs_2_), channel_id=1, source_target_pairs={{16,24},{20,28},{8,0},{12,4},{17,25},{21,29},{9,1},{13,5},{18,26},... | collective-permute-start | bytes 786440 | tf_op jit(solution)/shard_map/ppermute | solution.py:93
  15.7 4.4 %collective-permute-done.3.refs_4_ = bf16[256,512]{1,0:T(8,128)(2,1)S(1)} collective-permute-done((bf16[256,512]{1,0:T(8,128)(2,1)S(1)}, bf16[256,512]{1,0:T(8,128)(2,1)S(1)}, u32[]{:S(2)}, u32[]{:S(2)}) %collective-permute-start.3) | collective-permute-done | bytes 262176 | tf_op jit(solution)/shard_map/ppermute | solution.py:93
  20.7 5.1 %collective-permute-done.6.refs_7_ = bf16[256,512]{1,0:T(8,128)(2,1)S(1)} collective-permute-done((bf16[256,512]{1,0:T(8,128)(2,1)S(1)}, bf16[256,512]{1,0:T(8,128)(2,1)S(1)}, u32[]{:S(2)}, u32[]{:S(2)}) %collective-permute-start.6) | collective-permute-done | bytes 262176 | tf_op jit(solution)/shard_map/ppermute | solution.py:93
  25.9 1.5 %collective-permute-done.8.refs_9_ = bf16[256,512]{1,0:T(8,128)(2,1)S(1)} collective-permute-done((bf16[256,512]{1,0:T(8,128)(2,1)S(1)}, bf16[256,512]{1,0:T(8,128)(2,1)S(1)}, u32[]{:S(2)}, u32[]{:S(2)}) %collective-permute-start.8) | collective-permute-done | bytes 262176 | tf_op jit(solution)/shard_map/ppermute | solution.py:147
  27.4 1.2 %shard_map.97 = (f32[128,512]{1,0:T(8,128)S(1)}, bf16[128,512]{1,0:T(8,128)(2,1)S(1)}, bf16[128,512]{1,0:T(8,128)(2,1)S(1)}, bf16[128,512]{1,0:T(8,128)(2,1)S(1)}) custom-call(bf16[512,2048]{1,0:T(8,128)(2,1)S(1)} %get-tuple-element.31.adj, bf16[256,512]{1,0:T(8,128)(2,1)S(1)} %convert_element_type.3.item_half.refs_0_, ...), custom_call_target="tpu_custom_call" | custom-call | flops 1073741824 | bytes 6291456 | tf_op jit(solution)/shard_map/pallas_call | solution.py:179
  28.6 1.4 %collective-permute-start.9 = (bf16[128,512]{1,0:T(8,128)(2,1)S(1)}, bf16[128,512]{1,0:T(8,128)(2,1)S(1)}, u32[]{:S(2)}, u32[]{:S(2)}) collective-permute-start(bf16[128,512]{1,0:T(8,128)(2,1)S(1)} %get-tuple-element.34), channel_id=1, source_target_pairs={{0,1},{1,0},{2,3},{3,2},{4,5},{5,4},{6,7},{7,6},{8,9},{9,8},{10,11... | collective-permute-start | bytes 393224 | tf_op jit(solution)/shard_map/ppermute | solution.py:147
  30.0 1.8 %collective-permute-start.10 = (bf16[128,512]{1,0:T(8,128)(2,1)S(1)}, bf16[128,512]{1,0:T(8,128)(2,1)S(1)}, u32[]{:S(2)}, u32[]{:S(2)}) collective-permute-start(bf16[128,512]{1,0:T(8,128)(2,1)S(1)} %get-tuple-element.35), channel_id=1, source_target_pairs={{0,2},{1,3},{2,0},{3,1},{4,6},{5,7},{6,4},{7,5},{8,10},{9,11},{10,... | collective-permute-start | bytes 393224 | tf_op jit(solution)/shard_map/ppermute | solution.py:147
  32.2 2.5 %collective-permute-done.9.refs_1_ = bf16[128,512]{1,0:T(8,128)(2,1)S(1)} collective-permute-done((bf16[128,512]{1,0:T(8,128)(2,1)S(1)}, bf16[128,512]{1,0:T(8,128)(2,1)S(1)}, u32[]{:S(2)}, u32[]{:S(2)}) %collective-permute-start.9) | collective-permute-done | bytes 131104 | tf_op jit(solution)/shard_map/ppermute | solution.py:147
  34.7 3.5 %collective-permute-done.10.refs_2_ = bf16[128,512]{1,0:T(8,128)(2,1)S(1)} collective-permute-done((bf16[128,512]{1,0:T(8,128)(2,1)S(1)}, bf16[128,512]{1,0:T(8,128)(2,1)S(1)}, u32[]{:S(2)}, u32[]{:S(2)}) %collective-permute-start.10) | collective-permute-done | bytes 131104 | tf_op jit(solution)/shard_map/ppermute | solution.py:147
  38.1 1.3 %shard_map.98 = (f32[128,512]{1,0:T(8,128)}, bf16[128,512]{1,0:T(8,128)(2,1)S(1)}) custom-call(f32[128,512]{1,0:T(8,128)S(1)} %get-tuple-element.28.emb, bf16[1024,512]{1,0:T(8,128)(2,1)S(1)} %get-tuple-element.29.w_hi, bf16[1024,512]{1,0:T(8,128)(2,1)S(1)} %get-tuple-element.30.w_lo, f32[128,512]{1,0:T(8,128)S(1)} %get-tuple-element.33.refs_0_, ...), custom_call_target="tpu_custom_call" | custom-call | flops 402653184 | bytes 3145728 | tf_op jit(solution)/shard_map/pallas_call | solution.py:184
  39.4 1.5 %collective-permute-start.14 = (bf16[128,512]{1,0:T(8,128)(2,1)S(1)}, bf16[128,512]{1,0:T(8,128)(2,1)S(1)}, u32[]{:S(2)}, u32[]{:S(2)}) collective-permute-start(bf16[128,512]{1,0:T(8,128)(2,1)S(1)} %get-tuple-element.39.refs_0_), channel_id=1, source_target_pairs={{0,3},{1,2},{2,1},{3,0},{4,7},{5,6},{6,5},{7,4},{8,11},{9,10},{10,... | collective-permute-start | bytes 393224 | tf_op jit(solution)/shard_map/ppermute | solution.py:147
  41.0 1.4 %collective-permute-start.13 = (bf16[128,512]{1,0:T(8,128)(2,1)S(1)}, bf16[128,512]{1,0:T(8,128)(2,1)S(1)}, u32[]{:S(2)}, u32[]{:S(2)}) collective-permute-start(bf16[128,512]{1,0:T(8,128)(2,1)S(1)} %get-tuple-element.39.refs_0_), channel_id=1, source_target_pairs={{0,2},{1,3},{2,0},{3,1},{4,6},{5,7},{6,4},{7,5},{8,10},{9,11},{10,... | collective-permute-start | bytes 393224 | tf_op jit(solution)/shard_map/ppermute | solution.py:147
  42.9 3.4 %collective-permute-done.14.refs_3_ = bf16[128,512]{1,0:T(8,128)(2,1)S(1)} collective-permute-done((bf16[128,512]{1,0:T(8,128)(2,1)S(1)}, bf16[128,512]{1,0:T(8,128)(2,1)S(1)}, u32[]{:S(2)}, u32[]{:S(2)}) %collective-permute-start.14) | collective-permute-done | bytes 131104 | tf_op jit(solution)/shard_map/ppermute | solution.py:147
  47.9 1.2 %shard_map.99 = (f32[256,512]{1,0:T(8,128)S(1)}, bf16[256,512]{1,0:T(8,128)(2,1)S(1)}, f32[256,512]{1,0:T(8,128)S(1)}, bf16[256,512]{1,0:T(8,128)(2,1)S(1)}, f32...) custom-call(bf16[2048,512]{1,0:T(8,128)(2,1)S(1)} %get-tuple-element., ...), custom_call_target="tpu_custom_call" | custom-call | flops 1073741824 | bytes 6291456 | tf_op jit(solution)/shard_map/pallas_call | solution.py:198
  52.1 2.1 %collective-permute-start.19 = (bf16[256,512]{1,0:T(8,128)(2,1)S(1)}, bf16[256,512]{1,0:T(8,128)(2,1)S(1)}, u32[]{:S(2)}, u32[]{:S(2)}) collective-permute-start(bf16[256,512]{1,0:T(8,128)(2,1)S(1)} %get-tuple-element.50), channel_id=1, source_target_pairs={{24,16},{28,20},{0,8},{4,12},{25,17},{29,21},{1,9},{5,13},{26,18},... | collective-permute-start | bytes 786440 | tf_op jit(solution)/shard_map/ppermute | solution.py:93
  54.9 2.1 %collective-permute-start.21 = (bf16[256,512]{1,0:T(8,128)(2,1)S(1)}, bf16[256,512]{1,0:T(8,128)(2,1)S(1)}, u32[]{:S(2)}, u32[]{:S(2)}) collective-permute-start(bf16[256,512]{1,0:T(8,128)(2,1)S(1)} %get-tuple-element.51), channel_id=1, source_target_pairs={{8,0},{12,4},{16,24},{20,28},{24,8},{28,12},{0,16},{4,20},{9,1},{1... | collective-permute-start | bytes 786440 | tf_op jit(solution)/shard_map/ppermute | solution.py:93
  57.0 3.8 %collective-permute-done.19.refs_1_ = bf16[256,512]{1,0:T(8,128)(2,1)S(1)} collective-permute-done((bf16[256,512]{1,0:T(8,128)(2,1)S(1)}, bf16[256,512]{1,0:T(8,128)(2,1)S(1)}, u32[]{:S(2)}, u32[]{:S(2)}) %collective-permute-start.19) | collective-permute-done | bytes 262176 | tf_op jit(solution)/shard_map/ppermute | solution.py:93
  60.9 2.5 %collective-permute-start.20 = (bf16[256,512]{1,0:T(8,128)(2,1)S(1)}, bf16[256,512]{1,0:T(8,128)(2,1)S(1)}, u32[]{:S(2)}, u32[]{:S(2)}) collective-permute-start(bf16[256,512]{1,0:T(8,128)(2,1)S(1)} %shard_map.101), channel_id=1, source_target_pairs={{16,0},{20,4},{8,24},{12,28},{0,8},{4,12},{24,16},{28,20},{17,1},{... | collective-permute-start | bytes 786440 | tf_op jit(solution)/shard_map/ppermute | solution.py:93
  63.4 3.1 %collective-permute-done.21.refs_2_ = bf16[256,512]{1,0:T(8,128)(2,1)S(1)} collective-permute-done((bf16[256,512]{1,0:T(8,128)(2,1)S(1)}, bf16[256,512]{1,0:T(8,128)(2,1)S(1)}, u32[]{:S(2)}, u32[]{:S(2)}) %collective-permute-start.21) | collective-permute-done | bytes 262176 | tf_op jit(solution)/shard_map/ppermute | solution.py:93
  66.5 8.0 %collective-permute-done.20.refs_1_ = bf16[256,512]{1,0:T(8,128)(2,1)S(1)} collective-permute-done((bf16[256,512]{1,0:T(8,128)(2,1)S(1)}, bf16[256,512]{1,0:T(8,128)(2,1)S(1)}, u32[]{:S(2)}, u32[]{:S(2)}) %collective-permute-start.20) | collective-permute-done | bytes 262176 | tf_op jit(solution)/shard_map/ppermute | solution.py:93
  74.5 1.8 %shard_map.102 = f32[256,512]{1,0:T(8,128)} custom-call(f32[256,512]{1,0:T(8,128)S(1)} %copy-done, bf16[1024,512]{1,0:T(8,128)(2,1)S(1)} %get-tuple-element.29.w_hi, bf16[1024,512]{1,0:T(8,128)(2,1)S(1)} %get-tuple-element.30.w_lo, f32[256,512]{1,0:T(8,128)S(1)} %get-tuple-element.48.refs_0_, bf16[256,512]{1,0:T(8,128)(2,1)S(1)} %collective-permute-done.20.refs_1_, ...), custom_call_target="tpu_custom_call" | custom-call | flops 805306368 | bytes 4194304 | tf_op jit(solution)/shard_map/pallas_call | solution.py:209
  (45 shorter events, 13.1 us)
Async XLA Ops:
  1.7 12.1 %collective-permute-start.1 = (bf16[256,512]{1,0:T(8,128)(2,1)S(1)}, bf16[256,512]{1,0:T(8,128)(2,1)S(1)}, u32[]{:S(2)}, u32[]{:S(2)}) collective-permute-start(bf16[256,512]{1,0:T(8,128)(2,1)S(1)} %convert_element_type.3.item_half.refs_0_), channel_id=1, source_target_pairs={{0,16},{4,20},{24,8},{28,12},{8,0},{12,4},{16,24},{20,28},{1,17},{... | collective-permute-start | bytes 786440 | tf_op jit(solution)/shard_map/ppermute | solution.py:93
  10.1 10.1 %collective-permute-start.3 = (bf16[256,512]{1,0:T(8,128)(2,1)S(1)}, bf16[256,512]{1,0:T(8,128)(2,1)S(1)}, u32[]{:S(2)}, u32[]{:S(2)}) collective-permute-start(bf16[256,512]{1,0:T(8,128)(2,1)S(1)} %get-tuple-element.27.item_half), channel_id=1, source_target_pairs={{0,8},{4,12},{24,16},{28,20},{8,24},{12,28},{16,0},{20,4},{1,9},{5... | collective-permute-start | bytes 786440 | tf_op jit(solution)/shard_map/ppermute | solution.py:93
  13.2 7.0 %collective-permute-start.5 = (bf16[256,512]{1,0:T(8,128)(2,1)S(1)}, bf16[256,512]{1,0:T(8,128)(2,1)S(1)}, u32[]{:S(2)}, u32[]{:S(2)}) collective-permute-start(bf16[256,512]{1,0:T(8,128)(2,1)S(1)} %get-tuple-element.32), channel_id=1, source_target_pairs={{8,16},{12,20},{16,8},{20,12},{9,17},{13,21},{17,9},{21,13},{10,18... | collective-permute-start | bytes 786440 | tf_op jit(solution)/shard_map/ppermute | solution.py:93
  13.9 12.0 %collective-permute-start.6 = (bf16[256,512]{1,0:T(8,128)(2,1)S(1)}, bf16[256,512]{1,0:T(8,128)(2,1)S(1)}, u32[]{:S(2)}, u32[]{:S(2)}) collective-permute-start(bf16[256,512]{1,0:T(8,128)(2,1)S(1)} %collective-permute-done.1.refs_2_), channel_id=1, source_target_pairs={{16,24},{20,28},{8,0},{12,4},{17,25},{21,29},{9,1},{13,5},{18,26},... | collective-permute-start | bytes 786440 | tf_op jit(solution)/shard_map/ppermute | solution.py:93
  15.2 10.7 %collective-permute-start = (bf16[256,512]{1,0:T(8,128)(2,1)S(1)}, bf16[256,512]{1,0:T(8,128)(2,1)S(1)}, u32[]{:S(2)}, u32[]{:S(2)}) collective-permute-start(bf16[256,512]{1,0:T(8,128)(2,1)S(1)} %convert_element_type.3.item_half.refs_0_), channel_id=1, source_target_pairs={{0,4},{4,0},{8,12},{12,8},{16,20},{20,16},{24,28},{28,24},{1,5},{5... | collective-permute-start | bytes 786440 | tf_op jit(solution)/shard_map/ppermute | solution.py:147
  15.3 10.5 %collective-permute-start.2 = (bf16[256,512]{1,0:T(8,128)(2,1)S(1)}, bf16[256,512]{1,0:T(8,128)(2,1)S(1)}, u32[]{:S(2)}, u32[]{:S(2)}) collective-permute-start(bf16[256,512]{1,0:T(8,128)(2,1)S(1)} %collective-permute-done.1.refs_2_), channel_id=1, source_target_pairs={{0,4},{4,0},{8,12},{12,8},{16,20},{20,16},{24,28},{28,24},{1,5},{5... | collective-permute-start | bytes 786440 | tf_op jit(solution)/shard_map/ppermute | solution.py:147
  20.2 5.7 %collective-permute-start.4 = (bf16[256,512]{1,0:T(8,128)(2,1)S(1)}, bf16[256,512]{1,0:T(8,128)(2,1)S(1)}, u32[]{:S(2)}, u32[]{:S(2)}) collective-permute-start(bf16[256,512]{1,0:T(8,128)(2,1)S(1)} %collective-permute-done.3.refs_4_), channel_id=1, source_target_pairs={{0,4},{4,0},{8,12},{12,8},{16,20},{20,16},{24,28},{28,24},{1,5},{5... | collective-permute-start | bytes 786440 | tf_op jit(solution)/shard_map/ppermute | solution.py:147
  20.2 5.7 %collective-permute-start.7 = (bf16[256,512]{1,0:T(8,128)(2,1)S(1)}, bf16[256,512]{1,0:T(8,128)(2,1)S(1)}, u32[]{:S(2)}, u32[]{:S(2)}) collective-permute-start(bf16[256,512]{1,0:T(8,128)(2,1)S(1)} %collective-permute-done.5.refs_6_), channel_id=1, source_target_pairs={{0,4},{4,0},{8,12},{12,8},{16,20},{20,16},{24,28},{28,24},{1,5},{5... | collective-permute-start | bytes 786440 | tf_op jit(solution)/shard_map/ppermute | solution.py:147
  25.8 1.5 %collective-permute-start.8 = (bf16[256,512]{1,0:T(8,128)(2,1)S(1)}, bf16[256,512]{1,0:T(8,128)(2,1)S(1)}, u32[]{:S(2)}, u32[]{:S(2)}) collective-permute-start(bf16[256,512]{1,0:T(8,128)(2,1)S(1)} %collective-permute-done.6.refs_7_), channel_id=1, source_target_pairs={{0,4},{4,0},{8,12},{12,8},{16,20},{20,16},{24,28},{28,24},{1,5},{5... | collective-permute-start | bytes 786440 | tf_op jit(solution)/shard_map/ppermute | solution.py:147
  28.6 6.1 %collective-permute-start.9 = (bf16[128,512]{1,0:T(8,128)(2,1)S(1)}, bf16[128,512]{1,0:T(8,128)(2,1)S(1)}, u32[]{:S(2)}, u32[]{:S(2)}) collective-permute-start(bf16[128,512]{1,0:T(8,128)(2,1)S(1)} %get-tuple-element.34), channel_id=1, source_target_pairs={{0,1},{1,0},{2,3},{3,2},{4,5},{5,4},{6,7},{7,6},{8,9},{9,8},{10,11... | collective-permute-start | bytes 393224 | tf_op jit(solution)/shard_map/ppermute | solution.py:147
  30.0 8.2 %collective-permute-start.10 = (bf16[128,512]{1,0:T(8,128)(2,1)S(1)}, bf16[128,512]{1,0:T(8,128)(2,1)S(1)}, u32[]{:S(2)}, u32[]{:S(2)}) collective-permute-start(bf16[128,512]{1,0:T(8,128)(2,1)S(1)} %get-tuple-element.35), channel_id=1, source_target_pairs={{0,2},{1,3},{2,0},{3,1},{4,6},{5,7},{6,4},{7,5},{8,10},{9,11},{10,... | collective-permute-start | bytes 393224 | tf_op jit(solution)/shard_map/ppermute | solution.py:147
  31.8 6.3 %collective-permute-start.11 = (bf16[128,512]{1,0:T(8,128)(2,1)S(1)}, bf16[128,512]{1,0:T(8,128)(2,1)S(1)}, u32[]{:S(2)}, u32[]{:S(2)}) collective-permute-start(bf16[128,512]{1,0:T(8,128)(2,1)S(1)} %get-tuple-element.36), channel_id=1, source_target_pairs={{0,3},{1,2},{2,1},{3,0},{4,7},{5,6},{6,5},{7,4},{8,11},{9,10},{10,... | collective-permute-start | bytes 393224 | tf_op jit(solution)/shard_map/ppermute | solution.py:147
  39.4 6.9 %collective-permute-start.14 = (bf16[128,512]{1,0:T(8,128)(2,1)S(1)}, bf16[128,512]{1,0:T(8,128)(2,1)S(1)}, u32[]{:S(2)}, u32[]{:S(2)}) collective-permute-start(bf16[128,512]{1,0:T(8,128)(2,1)S(1)} %get-tuple-element.39.refs_0_), channel_id=1, source_target_pairs={{0,3},{1,2},{2,1},{3,0},{4,7},{5,6},{6,5},{7,4},{8,11},{9,10},{10,... | collective-permute-start | bytes 393224 | tf_op jit(solution)/shard_map/ppermute | solution.py:147
  41.0 6.2 %collective-permute-start.13 = (bf16[128,512]{1,0:T(8,128)(2,1)S(1)}, bf16[128,512]{1,0:T(8,128)(2,1)S(1)}, u32[]{:S(2)}, u32[]{:S(2)}) collective-permute-start(bf16[128,512]{1,0:T(8,128)(2,1)S(1)} %get-tuple-element.39.refs_0_), channel_id=1, source_target_pairs={{0,2},{1,3},{2,0},{3,1},{4,6},{5,7},{6,4},{7,5},{8,10},{9,11},{10,... | collective-permute-start | bytes 393224 | tf_op jit(solution)/shard_map/ppermute | solution.py:147
  42.4 5.6 %collective-permute-start.12 = (bf16[128,512]{1,0:T(8,128)(2,1)S(1)}, bf16[128,512]{1,0:T(8,128)(2,1)S(1)}, u32[]{:S(2)}, u32[]{:S(2)}) collective-permute-start(bf16[128,512]{1,0:T(8,128)(2,1)S(1)} %get-tuple-element.39.refs_0_), channel_id=1, source_target_pairs={{0,1},{1,0},{2,3},{3,2},{4,5},{5,4},{6,7},{7,6},{8,9},{9,8},{10,11... | collective-permute-start | bytes 393224 | tf_op jit(solution)/shard_map/ppermute | solution.py:147
  49.2 25.3 %copy-start = (f32[256,512]{1,0:T(8,128)S(1)}, f32[256,512]{1,0:T(8,128)}, u32[]{:S(2)}) copy-start(f32[256,512]{1,0:T(8,128)} %emb.1) | copy-start | bytes 1572868
  49.2 1.6 %collective-permute-start.15 = (bf16[256,512]{1,0:T(8,128)(2,1)S(1)}, bf16[256,512]{1,0:T(8,128)(2,1)S(1)}, u32[]{:S(2)}, u32[]{:S(2)}) collective-permute-start(bf16[256,512]{1,0:T(8,128)(2,1)S(1)} %get-tuple-element.44), channel_id=1, source_target_pairs={{0,4},{4,0},{8,12},{12,8},{16,20},{20,16},{24,28},{28,24},{1,5},{5... | collective-permute-start | bytes 786440 | tf_op jit(solution)/shard_map/ppermute | solution.py:147
  49.3 1.9 %collective-permute-start.16 = (bf16[256,512]{1,0:T(8,128)(2,1)S(1)}, bf16[256,512]{1,0:T(8,128)(2,1)S(1)}, u32[]{:S(2)}, u32[]{:S(2)}) collective-permute-start(bf16[256,512]{1,0:T(8,128)(2,1)S(1)} %get-tuple-element.45), channel_id=1, source_target_pairs={{0,4},{4,0},{8,12},{12,8},{16,20},{20,16},{24,28},{28,24},{1,5},{5... | collective-permute-start | bytes 786440 | tf_op jit(solution)/shard_map/ppermute | solution.py:147
  49.8 1.8 %collective-permute-start.17 = (bf16[256,512]{1,0:T(8,128)(2,1)S(1)}, bf16[256,512]{1,0:T(8,128)(2,1)S(1)}, u32[]{:S(2)}, u32[]{:S(2)}) collective-permute-start(bf16[256,512]{1,0:T(8,128)(2,1)S(1)} %get-tuple-element.46), channel_id=1, source_target_pairs={{0,4},{4,0},{8,12},{12,8},{16,20},{20,16},{24,28},{28,24},{1,5},{5... | collective-permute-start | bytes 786440 | tf_op jit(solution)/shard_map/ppermute | solution.py:147
  49.8 2.1 %collective-permute-start.18 = (bf16[256,512]{1,0:T(8,128)(2,1)S(1)}, bf16[256,512]{1,0:T(8,128)(2,1)S(1)}, u32[]{:S(2)}, u32[]{:S(2)}) collective-permute-start(bf16[256,512]{1,0:T(8,128)(2,1)S(1)} %get-tuple-element.47), channel_id=1, source_target_pairs={{0,4},{4,0},{8,12},{12,8},{16,20},{20,16},{24,28},{28,24},{1,5},{5... | collective-permute-start | bytes 786440 | tf_op jit(solution)/shard_map/ppermute | solution.py:147
  52.1 8.7 %collective-permute-start.19 = (bf16[256,512]{1,0:T(8,128)(2,1)S(1)}, bf16[256,512]{1,0:T(8,128)(2,1)S(1)}, u32[]{:S(2)}, u32[]{:S(2)}) collective-permute-start(bf16[256,512]{1,0:T(8,128)(2,1)S(1)} %get-tuple-element.50), channel_id=1, source_target_pairs={{24,16},{28,20},{0,8},{4,12},{25,17},{29,21},{1,9},{5,13},{26,18},... | collective-permute-start | bytes 786440 | tf_op jit(solution)/shard_map/ppermute | solution.py:93
  54.2 12.3 %collective-permute-start.22 = (bf16[256,512]{1,0:T(8,128)(2,1)S(1)}, bf16[256,512]{1,0:T(8,128)(2,1)S(1)}, u32[]{:S(2)}, u32[]{:S(2)}) collective-permute-start(bf16[256,512]{1,0:T(8,128)(2,1)S(1)} %get-tuple-element.50), channel_id=1, source_target_pairs={{16,8},{20,12},{8,16},{12,20},{17,9},{21,13},{9,17},{13,21},{18,10... | collective-permute-start | bytes 786440 | tf_op jit(solution)/shard_map/ppermute | solution.py:93
  54.9 11.6 %collective-permute-start.21 = (bf16[256,512]{1,0:T(8,128)(2,1)S(1)}, bf16[256,512]{1,0:T(8,128)(2,1)S(1)}, u32[]{:S(2)}, u32[]{:S(2)}) collective-permute-start(bf16[256,512]{1,0:T(8,128)(2,1)S(1)} %get-tuple-element.51), channel_id=1, source_target_pairs={{8,0},{12,4},{16,24},{20,28},{24,8},{28,12},{0,16},{4,20},{9,1},{1... | collective-permute-start | bytes 786440 | tf_op jit(solution)/shard_map/ppermute | solution.py:93
  60.9 13.6 %collective-permute-start.20 = (bf16[256,512]{1,0:T(8,128)(2,1)S(1)}, bf16[256,512]{1,0:T(8,128)(2,1)S(1)}, u32[]{:S(2)}, u32[]{:S(2)}) collective-permute-start(bf16[256,512]{1,0:T(8,128)(2,1)S(1)} %shard_map.101), channel_id=1, source_target_pairs={{16,0},{20,4},{8,24},{12,28},{0,8},{4,12},{24,16},{28,20},{17,1},{... | collective-permute-start | bytes 786440 | tf_op jit(solution)/shard_map/ppermute | solution.py:93
  (6 other events, 6.4 us)

commit v3 on v0

v3 whole, which is shorter than its diff:
```python
import functools

import jax
import jax.numpy as jnp
from jax import lax
from jax.experimental import pallas as pl
from jax.experimental.pallas import tpu as pltpu
from jax.sharding import PartitionSpec as P

F32 = jnp.float32
BF16 = jnp.bfloat16
VMEM = pl.BlockSpec(memory_space=pltpu.VMEM)
SMEM = pl.BlockSpec(memory_space=pltpu.SMEM)
PARAMS = pltpu.CompilerParams(vmem_limit_bytes=40 * 1024 * 1024)

TURN_1 = ((0, 2), (3, 1), (1, 0), (2, 3))
TURN_2 = ((0, 1), (3, 2), (1, 3), (2, 0))
MIDDLE = ((1, 2), (2, 1), (0, 0), (3, 3))
HANDED = ((2, 3), (1, 0), (3, 2), (0, 1))


def back(pairs):
    return tuple((b, a) for a, b in pairs)


def send(x, pairs):
    return lax.ppermute(x, "au", [(2 * a + core, 2 * b + core) for a, b in pairs for core in (0, 1)])


def swap(x, axis, n, by):
    return lax.ppermute(x, axis, [(i, i ^ by) for i in range(n)])


def slot_of(me, block):
    apart = block ^ me
    turn = apart >> 1
    swapped = in_middle() & ((turn == 1) | (turn == 2))
    return jnp.where(swapped, 3 - turn, turn) * 2 + (apart & 1)


def in_middle():
    z = lax.axis_index("au") >> 1
    return (z == 1) | (z == 2)


def call(kernel, out_shape, operands, smem=0, flops=0, nbytes=0):
    return pl.pallas_call(
        kernel,
        out_shape=out_shape,
        in_specs=[SMEM] * smem + [VMEM] * (len(operands) - smem),
        out_specs=jax.tree.map(lambda _: VMEM, out_shape),
        compiler_params=PARAMS,
        cost_estimate=pl.CostEstimate(flops=flops, bytes_accessed=nbytes, transcendentals=0),
    )(*operands)


def shape(*dims, dtype=BF16):
    return jax.ShapeDtypeStruct(dims, dtype)


def split(x):
    hi = x.astype(BF16)
    return hi, (x - hi.astype(F32)).astype(BF16)


def dot(a, b):
    return jnp.dot(a, b, preferred_element_type=F32)


def total(refs):
    value = refs[0][...].astype(F32)
    for ref in refs[1:]:
        value = value + ref[...].astype(F32)
    return value


def dense(piece, turns, rows, cols, count, tiles, adj):
    edge = tiles.shape[2]
    adj[...] = jnp.zeros_like(adj)

    def place(slot, carry):
        at = cols[0, slot]
        if turns:
            at = slot_of(lax.axis_index("au"), at)
        col = pl.multiple_of(at * edge, edge)
        for part in range(edge // piece):
            row = rows[0, slot] * (edge // piece) + part
            if turns:
                row = row ^ lax.axis_index("ia")
            row = pl.multiple_of(row * piece, piece)
            adj[pl.ds(row, piece), pl.ds(col, edge)] = tiles[0, slot, part * piece : (part + 1) * piece, :]
        return carry

    lax.fori_loop(0, count[0, 0], place, 0)


def flip(edge, adj, *outs):
    n = len(outs)
    for k in range(adj.shape[1] // edge):
        out = outs[k % n]
        out[k // n * edge : (k // n + 1) * edge, :] = adj[:, k * edge : (k + 1) * edge].T


def ready(edge, adj, user_emb, w_self, w_inter, w_hi, w_lo, own, *adj_t):
    weights(user_emb, w_self, w_inter, w_hi, w_lo, own)
    flip(edge, adj, *adj_t)


def weights(user_emb, w_self, w_inter, w_hi, w_lo, own):
    depth = w_self.shape[0]
    for k, w in enumerate((w_self, w_inter)):
        w_hi[k * depth : (k + 1) * depth, :], w_lo[k * depth : (k + 1) * depth, :] = split(w[...])
    height = own.shape[0]
    own[...] = user_emb[pl.ds(pl.multiple_of(lax.axis_index("ia") * height, height), height), :]


def block_sums(adj, first, blocks):
    edge = blocks[0].shape[0]
    return sum(dot(adj[:, (first + k) * edge : (first + k + 1) * edge], block) for k, block in enumerate(blocks))


def early_sums(adj, *refs):
    *blocks, sums = refs
    sums[...] = block_sums(adj, 0, [block[...] for block in blocks])


def late_sums(adj, early, second, second_other, middle, ends, middle_other, ends_other, *outs):
    inner = in_middle()
    blocks = [second[...], second_other[...]]
    blocks += [jnp.where(inner, a[...], b[...]) for a, b in ((middle, ends), (middle_other, ends_other))]
    sums = early[...] + block_sums(adj, 4, blocks)
    height = outs[0].shape[0]
    for k, out in enumerate(outs):
        out[...] = sums[k * height : (k + 1) * height].astype(out.dtype)


def user_sums(adj, items, out):
    out[...] = dot(adj[...], items[...])


def item_sums(slots, n, *refs):
    adj_t, shares, outs = refs[:2], refs[2 : 2 + 2 * n], refs[-len(slots) :]
    users = [jnp.concatenate([share[...] for share in shares[core * n : core * n + n]], axis=0) for core in (0, 1)]
    edge = outs[0].shape[0]
    for slot, out in zip(slots, outs):
        rows = slice(slot * edge, (slot + 1) * edge)
        out[...] = (dot(adj_t[0][rows, :], users[0]) + dot(adj_t[1][rows, :], users[1])).astype(out.dtype)


def all_sums(adj_t, users, out):
    out[...] = dot(adj_t[...], users[...])


def pass_on(sums, handed, out):
    given = jnp.where(in_middle(), handed[...].astype(F32), 0)
    out[...] = (sums[...] + given).astype(out.dtype)


def update(n, emb, w_hi, w_lo, *refs, inner=0):
    parts, outs = refs[:n], refs[n:]
    side = total(parts[inner:])
    if inner:
        side = side + jnp.where(in_middle(), total(parts[:inner]), 0)
    own = emb[...]
    height = own.shape[0]
    hi, lo = split(jnp.concatenate([side + own, side * own], axis=1))
    both = dot(jnp.concatenate([hi, lo], axis=0), w_hi[...])
    mixed = both[:height] + (both[height:] + dot(hi, w_lo[...]))
    mixed = jnp.where(mixed >= 0, mixed, 0.2 * mixed)
    for out in outs:
        out[...] = mixed.astype(out.dtype)


def in_turns(user_emb, item_emb, tiles, block_rows, block_cols, block_counts, w_self, w_inter):
    depth = w_self.shape[0]
    users, held = user_emb.shape[0], item_emb.shape[0]
    items = held * 8
    share = users // 4
    work = 2 * users * items * depth

    def other(x):
        return swap(x, "au", 8, 1)

    def after(x, *done):
        return lax.optimization_barrier((x, *done))[0]

    mine = item_emb.astype(BF16)
    first = send(mine, TURN_1)
    (adj,) = call(
        functools.partial(dense, share, True),
        (shape(users, items),),
        (block_rows, block_cols, block_counts, tiles),
        smem=3,
        nbytes=8 << 20,
    )
    second = send(after(mine, adj), TURN_2)
    w_hi, w_lo, own_emb, adj_t, others_t = call(
        functools.partial(ready, held),
        (shape(2 * depth, depth), shape(2 * depth, depth), shape(share, depth, dtype=F32))
        + (shape(items // 2, users), shape(items // 2, users)),
        (adj, user_emb, w_self, w_inter),
        nbytes=9 << 20,
    )
    middle = send(after(mine, w_hi), MIDDLE)
    first = after(first, w_hi)
    ends = send(first, HANDED)
    (early,) = call(
        early_sums,
        (shape(users, depth, dtype=F32),),
        (adj, mine, other(mine), first, other(first)),
        flops=work // 2,
        nbytes=4 << 20,
    )
    own, *others = call(
        late_sums,
        (shape(share, depth, dtype=F32),) + (shape(share, depth),) * 3,
        (adj, early, second, other(second), middle, ends, other(middle), other(ends)),
        flops=work // 2,
        nbytes=4 << 20,
    )
    new_users, user_half = call(
        functools.partial(update, 4),
        (shape(share, depth, dtype=F32), shape(share, depth)),
        (own_emb, w_hi, w_lo, *(swap(others[k - 1], "ia", 4, k) for k in (3, 2, 1)), own),
        flops=12 * share * depth * depth,
        nbytes=3 << 20,
    )

    others_t = other(after(others_t, user_half))
    shares = [user_half] + [swap(user_half, "ia", 4, k) for k in (1, 2, 3)]
    shares += [other(x) for x in shares]
    (far,) = call(
        functools.partial(item_sums, (3,), 4),
        (shape(held, depth),),
        (adj_t, others_t, *shares),
        flops=work // 4,
        nbytes=2 << 20,
    )
    middle = send(far, back(MIDDLE))
    handed = send(far, back(HANDED))
    own, onward, near = call(
        functools.partial(item_sums, (0, 1, 2), 4),
        (shape(held, depth, dtype=F32), shape(held, depth, dtype=F32), shape(held, depth)),
        (adj_t, others_t, *shares, far),
        flops=3 * work // 4,
        nbytes=6 << 20,
    )
    near = send(near, back(TURN_2))
    (onward,) = call(pass_on, (shape(held, depth),), (onward, handed), nbytes=1 << 19)
    (new_items,) = call(
        functools.partial(update, 4, inner=1),
        (shape(held, depth, dtype=F32),),
        (item_emb, w_hi, w_lo, middle, own, near, send(onward, back(TURN_1))),
        flops=12 * held * depth * depth,
        nbytes=4 << 20,
    )
    return (new_users, new_items)


def gathered(n_au, n_ia, user_emb, item_emb, tiles, block_rows, block_cols, block_counts, w_self, w_inter):
    depth = w_self.shape[0]
    users, held = user_emb.shape[0], item_emb.shape[0]
    items = held * n_au
    share = users // n_ia
    work = 2 * users * items * depth

    blocks = lax.all_gather(item_emb.astype(BF16), "au", axis=0, tiled=True)
    (adj,) = call(
        functools.partial(dense, tiles.shape[2], False),
        (shape(users, items),),
        (block_rows, block_cols, block_counts, tiles),
        smem=3,
        nbytes=4 << 20,
    )
    (adj_t,) = call(functools.partial(flip, tiles.shape[2]), (shape(items, users),), (adj,), nbytes=4 << 20)
    w_hi, w_lo, own_emb = call(
        weights,
        (shape(2 * depth, depth), shape(2 * depth, depth), shape(share, depth, dtype=F32)),
        (user_emb, w_self, w_inter),
        nbytes=5 << 20,
    )
    (sums,) = call(
        user_sums, (shape(users, depth, dtype=F32),), (adj, blocks), flops=work, nbytes=6 << 20
    )
    sums = lax.psum_scatter(sums, "ia", scatter_dimension=0, tiled=True)
    new_users, user_half = call(
        functools.partial(update, 1),
        (shape(share, depth, dtype=F32), shape(share, depth)),
        (own_emb, w_hi, w_lo, sums),
        flops=12 * share * depth * depth,
        nbytes=3 << 20,
    )
    shares = lax.all_gather(user_half, "ia", axis=0, tiled=True)
    (sums,) = call(
        all_sums, (shape(items, depth, dtype=F32),), (adj_t, shares), flops=work, nbytes=6 << 20
    )
    sums = lax.psum_scatter(sums, "au", scatter_dimension=0, tiled=True)
    (new_items,) = call(
        functools.partial(update, 1),
        (shape(held, depth, dtype=F32),),
        (item_emb, w_hi, w_lo, sums),
        flops=12 * held * depth * depth,
        nbytes=4 << 20,
    )
    return (new_users, new_items)


def local(n_au, n_ia, user_emb, item_emb, tiles, *rest):
    edge = tiles.shape[2]
    if (n_au, n_ia) == (8, 4) and item_emb.shape[0] == edge and edge % (user_emb.shape[0] // n_ia) == 0:
        return in_turns(user_emb, item_emb, tiles, *rest)
    return gathered(n_au, n_ia, user_emb, item_emb, tiles, *rest)


def solution(mesh):
    in_specs = (
        P("au", None),
        P(("ia", "au"), None),
        P("au", "ia", None, None),
        P("au", "ia"),
        P("au", "ia"),
        P("au", "ia"),
        P(),
        P(),
    )
    out_specs = (P(("au", "ia"), None), P(("ia", "au"), None))
    return jax.shard_map(
        functools.partial(local, mesh.shape["au"], mesh.shape["ia"]),
        mesh=mesh,
        in_specs=in_specs,
        out_specs=out_specs,
        check_vma=False,
    )
```

time: 269 us -> 73.9 us (0.27)
  waiting for transfers between devices: 178 us -> 35.8 us
  matrix products: 25.5 us -> 0 us
  starting transfers between devices: 0.12 us -> 23.8 us
  loops' own time: 21.5 us -> 0 us
  between operations: 13.9 us -> 1.43 us
  local copies, waits for them, and re-layouts: 16 us -> 3.63 us
  blocking collectives: 9.93 us -> 0 us
  Pallas kernels: 0 us -> 7.99 us
    reduce_scatter x2 -> x0, waiting for transfers between devices: 145 us -> none  [the longest x1 88 us: local(): lax.psum_scatter(partial_items, 'au', scatter_dimension=0, tiled=True)]
    ppermute x0 -> x24, waiting for transfers between devices: none -> 35.8 us  [the longest x8 22.1 us: send(): lax.ppermute(x, 'au', [(2 * a + core, 2 * b + core) for a, b in pairs for...]
    all_gather x1 -> x0, waiting for transfers between devices: 32.9 us -> none  [local(): lax.all_gather(item_emb.astype(jnp.bfloat16), 'au', axis=0, tiled=True)]
    dot_general x14 -> x0, matrix products: 25.5 us -> none  [the longest x5 10.9 us: item_turn(): lax.dot_general(local_tiles[slot], block, (((0,), (0,)), ((), ())), prefe...]
    ppermute x0 -> x24, starting transfers between devices: none -> 23.8 us  [the longest x8 15.2 us: send(): lax.ppermute(x, 'au', [(2 * a + core, 2 * b + core) for a, b in pairs for...]
    another operation x2 -> x0, loops' own time: 21.5 us -> none  [the longest x1 10.9 us: local(): lax.fori_loop(0, count, item_turn, jnp.zeros((item_rows.shape[0], width),...]
    dynamic_slice x20 -> x0, local copies, waits for them, and re-layouts: 12.4 us -> none  [the longest x5 3.27 us: item_turn(): block = lax.dynamic_slice_in_dim(user_rows, rows[slot] * edge, edge, 0)]
    all_gather x1 -> x0, blocking collectives: 9.93 us -> none  [local(): lax.all_gather(new_users.astype(jnp.bfloat16), 'ia', axis=0, tiled=True)]
  transfers between devices with their start and end apart: 3 -> 24, of which waited for: 3 -> 12; matrix products, arithmetic and copies ran while one was open for 0% -> 0% of each run, Pallas kernels for 0% -> 5%
where the time goes in v3:
time: 73.9 us; the launch traced here: 73.7 us
  waiting for transfers between devices  35.8 us (48%)
  starting transfers between devices  23.8 us (32%)
  Pallas kernels  7.99 us (11%)
  local copies, waits for them, and re-layouts  3.63 us (5%)
  between operations  1.43 us (2%)
  other arithmetic  1.08 us (1%)
    ppermute x8, waiting for transfers between devices, send(): lax.ppermute(x, 'au', [(2 * a + core, 2 * b + core) for a, b in pairs for...  22.1 us
    ppermute x8, starting transfers between devices, send(): lax.ppermute(x, 'au', [(2 * a + core, 2 * b + core) for a, b in pairs for...  15.2 us
    ppermute x16, waiting for transfers between devices, swap(): return lax.ppermute(x, axis, [(i, i ^ by) for i in range(n)])  13.7 us
    ppermute x16, starting transfers between devices, swap(): return lax.ppermute(x, axis, [(i, i ^ by) for i in range(n)])  8.59 us
    pallas_call x9, Pallas kernels, call(): pl.pallas_call(kernel, out_shape=out_shape, in_specs=[SMEM] * smem + [VME...  7.99 us
    unnamed x14, local copies, waits for them, and re-layouts  3.63 us
  transfers between devices with their start and end apart: 24, of which 12 were waited for; matrix products, arithmetic and copies ran while one was open for 0% of the time, Pallas kernels for 5%

profile of v3, /device:TPU:0, one launch (start us, length us, event | category | flops | bytes accessed | tf_op | source)
XLA Modules:
  0.0 73.7 jit_solution(5683810831022638857)
XLA Ops:
  0.6 1.1 %convert_element_type.3.refs_0_ = bf16[256,512]{1,0:T(8,128)(2,1)S(1)} convert(f32[256,512]{1,0:T(8,128)} %emb.1) | non-fusion elementwise | flops 131072 | bytes 786432 | tf_op jit(solution)/shard_map/convert_element_type | solution.py:187
  1.7 4.1 %collective-permute-start.1 = (bf16[256,512]{1,0:T(8,128)(2,1)S(1)}, bf16[256,512]{1,0:T(8,128)(2,1)S(1)}, u32[]{:S(2)}, u32[]{:S(2)}) collective-permute-start(bf16[256,512]{1,0:T(8,128)(2,1)S(1)} %convert_element_type.3.refs_0_), channel_id=1, source_target_pairs={{0,16},{4,20},{24,8},{28,12},{8,0},{12,4},{16,24},{20,28},{1,17},{... | collective-permute-start | bytes 786440 | tf_op jit(solution)/shard_map/ppermute | solution.py:27
  6.5 1.4 %copy-done.1 = bf16[1,12,256,256]{3,2,1,0:T(8,128)(2,1)S(1)} copy-done((bf16[1,12,256,256]{3,2,1,0:T(8,128)(2,1)S(1)}, bf16[1,12,256,256]{3,2,1,0:T(8,128)(2,1)}, u32[]{:S(2)}) %copy-start.1) | copy-done | bytes 1572888
  9.2 0.9 %shard_map.95.adj = bf16[512,2048]{1,0:T(8,128)(2,1)S(1)} custom-call(s32[1,12]{1,0:T(1,128)S(1)} %copy-done.5, s32[1,12]{1,0:T(1,128)S(1)} %copy-done.6, s32[1,1]{1,0:T(1,128)S(6)} %copy.10.count, bf16[1,12,256,256]{3,2,1,0:T(8,128)(2,1)S(1)} %copy-done.1), custom_call_target="tpu_custom_call" | custom-call | bytes 8388608 | tf_op jit(solution)/shard_map/pallas_call | solution.py:47
  11.0 1.2 %shard_map.96 = (bf16[1024,512]{1,0:T(8,128)(2,1)S(1)}, bf16[1024,512]{1,0:T(8,128)(2,1)S(1)}, f32[128,512]{1,0:T(8,128)S(1)}, bf16[1024,512]{1,0:T(8,128)(2,1)S(1)}, bf16[1024,512]{1,0:T(8,128)(2,1)S(1)}) custom-call(bf16[512,2048]{1,0:T(8,128)(2,1)S(1)} %shard_map.95.adj, f32[512,512]{1,0:T(8,128)S(1)} %copy-done.2, f32[512,512]{1,0:T(8,128)S(1)} %copy-done.3, ...), custom_call_target="tpu_custom_call" | custom-call | bytes 9437184 | tf_op jit(solution)/shard_map/pallas_call | solution.py:47
  12.9 3.9 %collective-permute-start.6 = (bf16[256,512]{1,0:T(8,128)(2,1)S(1)}, bf16[256,512]{1,0:T(8,128)(2,1)S(1)}, u32[]{:S(2)}, u32[]{:S(2)}) collective-permute-start(bf16[256,512]{1,0:T(8,128)(2,1)S(1)} %collective-permute-done.1.refs_2_), channel_id=1, source_target_pairs={{16,24},{20,28},{8,0},{12,4},{24,16},{28,20},{0,8},{4,12},{17,25},... | collective-permute-start | bytes 786440 | tf_op jit(solution)/shard_map/ppermute | solution.py:27
  17.3 3.0 %collective-permute-done.3.second = bf16[256,512]{1,0:T(8,128)(2,1)S(1)} collective-permute-done((bf16[256,512]{1,0:T(8,128)(2,1)S(1)}, bf16[256,512]{1,0:T(8,128)(2,1)S(1)}, u32[]{:S(2)}, u32[]{:S(2)}) %collective-permute-start.3) | collective-permute-done | bytes 262176 | tf_op jit(solution)/shard_map/ppermute | solution.py:27
  20.7 3.8 %collective-permute-done.6.ends = bf16[256,512]{1,0:T(8,128)(2,1)S(1)} collective-permute-done((bf16[256,512]{1,0:T(8,128)(2,1)S(1)}, bf16[256,512]{1,0:T(8,128)(2,1)S(1)}, u32[]{:S(2)}, u32[]{:S(2)}) %collective-permute-start.6) | collective-permute-done | bytes 262176 | tf_op jit(solution)/shard_map/ppermute | solution.py:27
  26.8 2.5 %collective-permute-start.9 = (bf16[128,512]{1,0:T(8,128)(2,1)S(1)}, bf16[128,512]{1,0:T(8,128)(2,1)S(1)}, u32[]{:S(2)}, u32[]{:S(2)}) collective-permute-start(bf16[128,512]{1,0:T(8,128)(2,1)S(1)} %get-tuple-element.26), channel_id=1, source_target_pairs={{0,3},{1,2},{2,1},{3,0},{4,7},{5,6},{6,5},{7,4},{8,11},{9,10},{10,... | collective-permute-start | bytes 393224 | tf_op jit(solution)/shard_map/ppermute | solution.py:31
  30.3 3.3 %collective-permute-done.9.refs_0_ = bf16[128,512]{1,0:T(8,128)(2,1)S(1)} collective-permute-done((bf16[128,512]{1,0:T(8,128)(2,1)S(1)}, bf16[128,512]{1,0:T(8,128)(2,1)S(1)}, u32[]{:S(2)}, u32[]{:S(2)}) %collective-permute-start.9) | collective-permute-done | bytes 131104 | tf_op jit(solution)/shard_map/ppermute | solution.py:31
  33.6 2.5 %collective-permute-done.10.refs_1_ = bf16[128,512]{1,0:T(8,128)(2,1)S(1)} collective-permute-done((bf16[128,512]{1,0:T(8,128)(2,1)S(1)}, bf16[128,512]{1,0:T(8,128)(2,1)S(1)}, u32[]{:S(2)}, u32[]{:S(2)}) %collective-permute-start.10) | collective-permute-done | bytes 131104 | tf_op jit(solution)/shard_map/ppermute | solution.py:31
  36.1 1.3 %shard_map.99 = (f32[128,512]{1,0:T(8,128)}, bf16[128,512]{1,0:T(8,128)(2,1)S(1)}) custom-call(f32[128,512]{1,0:T(8,128)S(1)} %get-tuple-element.20.emb, bf16[1024,512]{1,0:T(8,128)(2,1)S(1)} %get-tuple-element.21.w_hi, bf16[1024,512]{1,0:T(8,128)(2,1)S(1)} %get-tuple-element.22.w_lo, bf16[128,512]{1,0:T(8,128)(2,1)S(1)} %collective-permute-done.9.refs_0_, ...), custom_call_target="tpu_custom_call" | custom-call | flops 402653184 | bytes 3145728 | tf_op jit(solution)/shard_map/pallas_call | solution.py:47
  37.4 1.7 %collective-permute-start.15 = (bf16[128,512]{1,0:T(8,128)(2,1)S(1)}, bf16[128,512]{1,0:T(8,128)(2,1)S(1)}, u32[]{:S(2)}, u32[]{:S(2)}) collective-permute-start(bf16[128,512]{1,0:T(8,128)(2,1)S(1)} %get-tuple-element.33.refs_2_), channel_id=1, source_target_pairs={{0,3},{1,2},{2,1},{3,0},{4,7},{5,6},{6,5},{7,4},{8,11},{9,10},{10,... | collective-permute-start | bytes 393224 | tf_op jit(solution)/shard_map/ppermute | solution.py:31
  39.1 1.3 %collective-permute-start.14 = (bf16[128,512]{1,0:T(8,128)(2,1)S(1)}, bf16[128,512]{1,0:T(8,128)(2,1)S(1)}, u32[]{:S(2)}, u32[]{:S(2)}) collective-permute-start(bf16[128,512]{1,0:T(8,128)(2,1)S(1)} %get-tuple-element.33.refs_2_), channel_id=1, source_target_pairs={{0,2},{1,3},{2,0},{3,1},{4,6},{5,7},{6,4},{7,5},{8,10},{9,11},{10,... | collective-permute-start | bytes 393224 | tf_op jit(solution)/shard_map/ppermute | solution.py:31
  40.9 3.7 %collective-permute-done.15.refs_5_ = bf16[128,512]{1,0:T(8,128)(2,1)S(1)} collective-permute-done((bf16[128,512]{1,0:T(8,128)(2,1)S(1)}, bf16[128,512]{1,0:T(8,128)(2,1)S(1)}, u32[]{:S(2)}, u32[]{:S(2)}) %collective-permute-start.15) | collective-permute-done | bytes 131104 | tf_op jit(solution)/shard_map/ppermute | solution.py:31
  44.6 2.4 %collective-permute-done.14.refs_4_ = bf16[128,512]{1,0:T(8,128)(2,1)S(1)} collective-permute-done((bf16[128,512]{1,0:T(8,128)(2,1)S(1)}, bf16[128,512]{1,0:T(8,128)(2,1)S(1)}, u32[]{:S(2)}, u32[]{:S(2)}) %collective-permute-start.14) | collective-permute-done | bytes 131104 | tf_op jit(solution)/shard_map/ppermute | solution.py:31
  49.0 1.0 %collective-permute-start.22 = (bf16[256,512]{1,0:T(8,128)(2,1)S(1)}, bf16[256,512]{1,0:T(8,128)(2,1)S(1)}, u32[]{:S(2)}, u32[]{:S(2)}) collective-permute-start(bf16[256,512]{1,0:T(8,128)(2,1)S(1)} %shard_map.100.refs_10_), channel_id=1, source_target_pairs={{24,16},{28,20},{0,8},{4,12},{16,24},{20,28},{8,0},{12,4},{25,17},... | collective-permute-start | bytes 786440 | tf_op jit(solution)/shard_map/ppermute | solution.py:27
  50.7 1.0 %shard_map.101 = (f32[256,512]{1,0:T(8,128)S(1)}, f32[256,512]{1,0:T(8,128)S(1)}, bf16[256,512]{1,0:T(8,128)(2,1)S(1)}) custom-call(bf16[1024,512]{1,0:T(8,128)(2,1)S(1)} %get-tuple-element.31.refs_0_, bf16[1024,512]{1,0:T(8,128)(2,1)S(1)} %collective-permute-done.12.refs_1_, bf16[128,512]{1,0:T(8,128)(2,1)S(1)} %get-tuple-element.33.refs_2_, ...), custom_call_target="tpu_custom_call" | custom-call | flops 805306368 | bytes 6291456 | tf_op jit(solution)/shard_map/pallas_call | solution.py:47
  51.7 3.8 %collective-permute-start.21 = (bf16[256,512]{1,0:T(8,128)(2,1)S(1)}, bf16[256,512]{1,0:T(8,128)(2,1)S(1)}, u32[]{:S(2)}, u32[]{:S(2)}) collective-permute-start(bf16[256,512]{1,0:T(8,128)(2,1)S(1)} %get-tuple-element.36), channel_id=1, source_target_pairs={{8,0},{12,4},{16,24},{20,28},{24,8},{28,12},{0,16},{4,20},{9,1},{1... | collective-permute-start | bytes 786440 | tf_op jit(solution)/shard_map/ppermute | solution.py:27
  55.5 2.7 %collective-permute-done.22.handed = bf16[256,512]{1,0:T(8,128)(2,1)S(1)} collective-permute-done((bf16[256,512]{1,0:T(8,128)(2,1)S(1)}, bf16[256,512]{1,0:T(8,128)(2,1)S(1)}, u32[]{:S(2)}, u32[]{:S(2)}) %collective-permute-start.22) | collective-permute-done | bytes 262176 | tf_op jit(solution)/shard_map/ppermute | solution.py:27
  58.3 1.0 %collective-permute-start.23 = (bf16[256,512]{1,0:T(8,128)(2,1)S(1)}, bf16[256,512]{1,0:T(8,128)(2,1)S(1)}, u32[]{:S(2)}, u32[]{:S(2)}) collective-permute-start(bf16[256,512]{1,0:T(8,128)(2,1)S(1)} %shard_map.102), channel_id=1, source_target_pairs={{16,0},{20,4},{8,24},{12,28},{0,8},{4,12},{24,16},{28,20},{17,1},{... | collective-permute-start | bytes 786440 | tf_op jit(solution)/shard_map/ppermute | solution.py:27
  59.3 4.0 %collective-permute-done.21.refs_2_ = bf16[256,512]{1,0:T(8,128)(2,1)S(1)} collective-permute-done((bf16[256,512]{1,0:T(8,128)(2,1)S(1)}, bf16[256,512]{1,0:T(8,128)(2,1)S(1)}, u32[]{:S(2)}, u32[]{:S(2)}) %collective-permute-start.21) | collective-permute-done | bytes 262176 | tf_op jit(solution)/shard_map/ppermute | solution.py:27
  63.2 8.7 %collective-permute-done.23.refs_3_ = bf16[256,512]{1,0:T(8,128)(2,1)S(1)} collective-permute-done((bf16[256,512]{1,0:T(8,128)(2,1)S(1)}, bf16[256,512]{1,0:T(8,128)(2,1)S(1)}, u32[]{:S(2)}, u32[]{:S(2)}) %collective-permute-start.23) | collective-permute-done | bytes 262176 | tf_op jit(solution)/shard_map/ppermute | solution.py:27
  71.9 1.8 %shard_map.103 = f32[256,512]{1,0:T(8,128)} custom-call(f32[256,512]{1,0:T(8,128)S(1)} %copy-done, bf16[1024,512]{1,0:T(8,128)(2,1)S(1)} %get-tuple-element.21.w_hi, bf16[1024,512]{1,0:T(8,128)(2,1)S(1)} %get-tuple-element.22.w_lo, bf16[256,512]{1,0:T(8,128)(2,1)S(1)} %collective-permute-done.20.refs_0_, f32[256,512]{1,0:T(8,128)S(1)} %get-tuple-element.35.refs_1_, ...), custom_call_target="tpu_custom_call" | custom-call | flops 805306368 | bytes 4194304 | tf_op jit(solution)/shard_map/pallas_call | solution.py:47
  (48 shorter events, 10.5 us)
Async XLA Ops:
  1.7 11.2 %collective-permute-start.1 = (bf16[256,512]{1,0:T(8,128)(2,1)S(1)}, bf16[256,512]{1,0:T(8,128)(2,1)S(1)}, u32[]{:S(2)}, u32[]{:S(2)}) collective-permute-start(bf16[256,512]{1,0:T(8,128)(2,1)S(1)} %convert_element_type.3.refs_0_), channel_id=1, source_target_pairs={{0,16},{4,20},{24,8},{28,12},{8,0},{12,4},{16,24},{20,28},{1,17},{... | collective-permute-start | bytes 786440 | tf_op jit(solution)/shard_map/ppermute | solution.py:27
  10.1 10.2 %collective-permute-start.3 = (bf16[256,512]{1,0:T(8,128)(2,1)S(1)}, bf16[256,512]{1,0:T(8,128)(2,1)S(1)}, u32[]{:S(2)}, u32[]{:S(2)}) collective-permute-start(bf16[256,512]{1,0:T(8,128)(2,1)S(1)} %convert_element_type.3.refs_0_), channel_id=1, source_target_pairs={{0,8},{4,12},{24,16},{28,20},{8,24},{12,28},{16,0},{20,4},{1,9},{5... | collective-permute-start | bytes 786440 | tf_op jit(solution)/shard_map/ppermute | solution.py:27
  12.2 8.0 %collective-permute-start.5 = (bf16[256,512]{1,0:T(8,128)(2,1)S(1)}, bf16[256,512]{1,0:T(8,128)(2,1)S(1)}, u32[]{:S(2)}, u32[]{:S(2)}) collective-permute-start(bf16[256,512]{1,0:T(8,128)(2,1)S(1)} %convert_element_type.3.refs_0_), channel_id=1, source_target_pairs={{8,16},{12,20},{16,8},{20,12},{0,0},{4,4},{24,24},{28,28},{9,17},{... | collective-permute-start | bytes 786440 | tf_op jit(solution)/shard_map/ppermute | solution.py:27
  12.9 11.6 %collective-permute-start.6 = (bf16[256,512]{1,0:T(8,128)(2,1)S(1)}, bf16[256,512]{1,0:T(8,128)(2,1)S(1)}, u32[]{:S(2)}, u32[]{:S(2)}) collective-permute-start(bf16[256,512]{1,0:T(8,128)(2,1)S(1)} %collective-permute-done.1.refs_2_), channel_id=1, source_target_pairs={{16,24},{20,28},{8,0},{12,4},{24,16},{28,20},{0,8},{4,12},{17,25},... | collective-permute-start | bytes 786440 | tf_op jit(solution)/shard_map/ppermute | solution.py:27
  16.8 7.8 %collective-permute-start = (bf16[256,512]{1,0:T(8,128)(2,1)S(1)}, bf16[256,512]{1,0:T(8,128)(2,1)S(1)}, u32[]{:S(2)}, u32[]{:S(2)}) collective-permute-start(bf16[256,512]{1,0:T(8,128)(2,1)S(1)} %convert_element_type.3.refs_0_), channel_id=1, source_target_pairs={{0,4},{4,0},{8,12},{12,8},{16,20},{20,16},{24,28},{28,24},{1,5},{5... | collective-permute-start | bytes 786440 | tf_op jit(solution)/shard_map/ppermute | solution.py:31
  16.8 7.8 %collective-permute-start.2 = (bf16[256,512]{1,0:T(8,128)(2,1)S(1)}, bf16[256,512]{1,0:T(8,128)(2,1)S(1)}, u32[]{:S(2)}, u32[]{:S(2)}) collective-permute-start(bf16[256,512]{1,0:T(8,128)(2,1)S(1)} %collective-permute-done.1.refs_2_), channel_id=1, source_target_pairs={{0,4},{4,0},{8,12},{12,8},{16,20},{20,16},{24,28},{28,24},{1,5},{5... | collective-permute-start | bytes 786440 | tf_op jit(solution)/shard_map/ppermute | solution.py:31
  20.2 5.0 %collective-permute-start.4 = (bf16[256,512]{1,0:T(8,128)(2,1)S(1)}, bf16[256,512]{1,0:T(8,128)(2,1)S(1)}, u32[]{:S(2)}, u32[]{:S(2)}) collective-permute-start(bf16[256,512]{1,0:T(8,128)(2,1)S(1)} %collective-permute-done.3.second), channel_id=1, source_target_pairs={{0,4},{4,0},{8,12},{12,8},{16,20},{20,16},{24,28},{28,24},{1,5},{5... | collective-permute-start | bytes 786440 | tf_op jit(solution)/shard_map/ppermute | solution.py:31
  20.2 5.0 %collective-permute-start.7 = (bf16[256,512]{1,0:T(8,128)(2,1)S(1)}, bf16[256,512]{1,0:T(8,128)(2,1)S(1)}, u32[]{:S(2)}, u32[]{:S(2)}) collective-permute-start(bf16[256,512]{1,0:T(8,128)(2,1)S(1)} %collective-permute-done.5.middle), channel_id=1, source_target_pairs={{0,4},{4,0},{8,12},{12,8},{16,20},{20,16},{24,28},{28,24},{1,5},{5... | collective-permute-start | bytes 786440 | tf_op jit(solution)/shard_map/ppermute | solution.py:31
  24.5 1.5 %collective-permute-start.8 = (bf16[256,512]{1,0:T(8,128)(2,1)S(1)}, bf16[256,512]{1,0:T(8,128)(2,1)S(1)}, u32[]{:S(2)}, u32[]{:S(2)}) collective-permute-start(bf16[256,512]{1,0:T(8,128)(2,1)S(1)} %collective-permute-done.6.ends), channel_id=1, source_target_pairs={{0,4},{4,0},{8,12},{12,8},{16,20},{20,16},{24,28},{28,24},{1,5},{5... | collective-permute-start | bytes 786440 | tf_op jit(solution)/shard_map/ppermute | solution.py:31
  26.8 6.8 %collective-permute-start.9 = (bf16[128,512]{1,0:T(8,128)(2,1)S(1)}, bf16[128,512]{1,0:T(8,128)(2,1)S(1)}, u32[]{:S(2)}, u32[]{:S(2)}) collective-permute-start(bf16[128,512]{1,0:T(8,128)(2,1)S(1)} %get-tuple-element.26), channel_id=1, source_target_pairs={{0,3},{1,2},{2,1},{3,0},{4,7},{5,6},{6,5},{7,4},{8,11},{9,10},{10,... | collective-permute-start | bytes 393224 | tf_op jit(solution)/shard_map/ppermute | solution.py:31
  29.3 6.8 %collective-permute-start.10 = (bf16[128,512]{1,0:T(8,128)(2,1)S(1)}, bf16[128,512]{1,0:T(8,128)(2,1)S(1)}, u32[]{:S(2)}, u32[]{:S(2)}) collective-permute-start(bf16[128,512]{1,0:T(8,128)(2,1)S(1)} %get-tuple-element.27), channel_id=1, source_target_pairs={{0,2},{1,3},{2,0},{3,1},{4,6},{5,7},{6,4},{7,5},{8,10},{9,11},{10,... | collective-permute-start | bytes 393224 | tf_op jit(solution)/shard_map/ppermute | solution.py:31
  29.8 6.3 %collective-permute-start.11 = (bf16[128,512]{1,0:T(8,128)(2,1)S(1)}, bf16[128,512]{1,0:T(8,128)(2,1)S(1)}, u32[]{:S(2)}, u32[]{:S(2)}) collective-permute-start(bf16[128,512]{1,0:T(8,128)(2,1)S(1)} %get-tuple-element.28), channel_id=1, source_target_pairs={{0,1},{1,0},{2,3},{3,2},{4,5},{5,4},{6,7},{7,6},{8,9},{9,8},{10,11... | collective-permute-start | bytes 393224 | tf_op jit(solution)/shard_map/ppermute | solution.py:31
  37.4 11.2 %collective-permute-start.12 = (bf16[1024,512]{1,0:T(8,128)(2,1)S(1)}, bf16[1024,512]{1,0:T(8,128)(2,1)S(1)}, u32[]{:S(2)}, u32[]{:S(2)}) collective-permute-start(bf16[1024,512]{1,0:T(8,128)(2,1)S(1)} %get-tuple-element.34), channel_id=1, source_target_pairs={{0,4},{4,0},{8,12},{12,8},{16,20},{20,16},{24,28},{28,24},{1,5},{5... | collective-permute-start | bytes 3145736 | tf_op jit(solution)/shard_map/ppermute | solution.py:31
  37.4 7.2 %collective-permute-start.15 = (bf16[128,512]{1,0:T(8,128)(2,1)S(1)}, bf16[128,512]{1,0:T(8,128)(2,1)S(1)}, u32[]{:S(2)}, u32[]{:S(2)}) collective-permute-start(bf16[128,512]{1,0:T(8,128)(2,1)S(1)} %get-tuple-element.33.refs_2_), channel_id=1, source_target_pairs={{0,3},{1,2},{2,1},{3,0},{4,7},{5,6},{6,5},{7,4},{8,11},{9,10},{10,... | collective-permute-start | bytes 393224 | tf_op jit(solution)/shard_map/ppermute | solution.py:31
  39.1 7.9 %collective-permute-start.14 = (bf16[128,512]{1,0:T(8,128)(2,1)S(1)}, bf16[128,512]{1,0:T(8,128)(2,1)S(1)}, u32[]{:S(2)}, u32[]{:S(2)}) collective-permute-start(bf16[128,512]{1,0:T(8,128)(2,1)S(1)} %get-tuple-element.33.refs_2_), channel_id=1, source_target_pairs={{0,2},{1,3},{2,0},{3,1},{4,6},{5,7},{6,4},{7,5},{8,10},{9,11},{10,... | collective-permute-start | bytes 393224 | tf_op jit(solution)/shard_map/ppermute | solution.py:31
  40.4 6.6 %collective-permute-start.13 = (bf16[128,512]{1,0:T(8,128)(2,1)S(1)}, bf16[128,512]{1,0:T(8,128)(2,1)S(1)}, u32[]{:S(2)}, u32[]{:S(2)}) collective-permute-start(bf16[128,512]{1,0:T(8,128)(2,1)S(1)} %get-tuple-element.33.refs_2_), channel_id=1, source_target_pairs={{0,1},{1,0},{2,3},{3,2},{4,5},{5,4},{6,7},{7,6},{8,9},{9,8},{10,11... | collective-permute-start | bytes 393224 | tf_op jit(solution)/shard_map/ppermute | solution.py:31
  40.9 6.6 %collective-permute-start.16 = (bf16[128,512]{1,0:T(8,128)(2,1)S(1)}, bf16[128,512]{1,0:T(8,128)(2,1)S(1)}, u32[]{:S(2)}, u32[]{:S(2)}) collective-permute-start(bf16[128,512]{1,0:T(8,128)(2,1)S(1)} %get-tuple-element.33.refs_2_), channel_id=1, source_target_pairs={{0,4},{4,0},{8,12},{12,8},{16,20},{20,16},{24,28},{28,24},{1,5},{5... | collective-permute-start | bytes 393224 | tf_op jit(solution)/shard_map/ppermute | solution.py:31
  44.6 2.9 %collective-permute-start.19 = (bf16[128,512]{1,0:T(8,128)(2,1)S(1)}, bf16[128,512]{1,0:T(8,128)(2,1)S(1)}, u32[]{:S(2)}, u32[]{:S(2)}) collective-permute-start(bf16[128,512]{1,0:T(8,128)(2,1)S(1)} %collective-permute-done.15.refs_5_), channel_id=1, source_target_pairs={{0,4},{4,0},{8,12},{12,8},{16,20},{20,16},{24,28},{28,24},{1,5},{5... | collective-permute-start | bytes 393224 | tf_op jit(solution)/shard_map/ppermute | solution.py:31
  47.0 1.3 %collective-permute-start.18 = (bf16[128,512]{1,0:T(8,128)(2,1)S(1)}, bf16[128,512]{1,0:T(8,128)(2,1)S(1)}, u32[]{:S(2)}, u32[]{:S(2)}) collective-permute-start(bf16[128,512]{1,0:T(8,128)(2,1)S(1)} %collective-permute-done.14.refs_4_), channel_id=1, source_target_pairs={{0,4},{4,0},{8,12},{12,8},{16,20},{20,16},{24,28},{28,24},{1,5},{5... | collective-permute-start | bytes 393224 | tf_op jit(solution)/shard_map/ppermute | solution.py:31
  47.1 1.5 %collective-permute-start.17 = (bf16[128,512]{1,0:T(8,128)(2,1)S(1)}, bf16[128,512]{1,0:T(8,128)(2,1)S(1)}, u32[]{:S(2)}, u32[]{:S(2)}) collective-permute-start(bf16[128,512]{1,0:T(8,128)(2,1)S(1)} %collective-permute-done.13.refs_3_), channel_id=1, source_target_pairs={{0,4},{4,0},{8,12},{12,8},{16,20},{20,16},{24,28},{28,24},{1,5},{5... | collective-permute-start | bytes 393224 | tf_op jit(solution)/shard_map/ppermute | solution.py:31
  49.0 9.2 %collective-permute-start.22 = (bf16[256,512]{1,0:T(8,128)(2,1)S(1)}, bf16[256,512]{1,0:T(8,128)(2,1)S(1)}, u32[]{:S(2)}, u32[]{:S(2)}) collective-permute-start(bf16[256,512]{1,0:T(8,128)(2,1)S(1)} %shard_map.100.refs_10_), channel_id=1, source_target_pairs={{24,16},{28,20},{0,8},{4,12},{16,24},{20,28},{8,0},{12,4},{25,17},... | collective-permute-start | bytes 786440 | tf_op jit(solution)/shard_map/ppermute | solution.py:27
  50.0 13.2 %collective-permute-start.20 = (bf16[256,512]{1,0:T(8,128)(2,1)S(1)}, bf16[256,512]{1,0:T(8,128)(2,1)S(1)}, u32[]{:S(2)}, u32[]{:S(2)}) collective-permute-start(bf16[256,512]{1,0:T(8,128)(2,1)S(1)} %shard_map.100.refs_10_), channel_id=1, source_target_pairs={{16,8},{20,12},{8,16},{12,20},{0,0},{4,4},{24,24},{28,28},{17,9},{... | collective-permute-start | bytes 786440 | tf_op jit(solution)/shard_map/ppermute | solution.py:27
  51.7 11.6 %collective-permute-start.21 = (bf16[256,512]{1,0:T(8,128)(2,1)S(1)}, bf16[256,512]{1,0:T(8,128)(2,1)S(1)}, u32[]{:S(2)}, u32[]{:S(2)}) collective-permute-start(bf16[256,512]{1,0:T(8,128)(2,1)S(1)} %get-tuple-element.36), channel_id=1, source_target_pairs={{8,0},{12,4},{16,24},{20,28},{24,8},{28,12},{0,16},{4,20},{9,1},{1... | collective-permute-start | bytes 786440 | tf_op jit(solution)/shard_map/ppermute | solution.py:27
  58.3 13.6 %collective-permute-start.23 = (bf16[256,512]{1,0:T(8,128)(2,1)S(1)}, bf16[256,512]{1,0:T(8,128)(2,1)S(1)}, u32[]{:S(2)}, u32[]{:S(2)}) collective-permute-start(bf16[256,512]{1,0:T(8,128)(2,1)S(1)} %shard_map.102), channel_id=1, source_target_pairs={{16,0},{20,4},{8,24},{12,28},{0,8},{4,12},{24,16},{28,20},{17,1},{... | collective-permute-start | bytes 786440 | tf_op jit(solution)/shard_map/ppermute | solution.py:27
  (7 other events, 30.3 us)

commit v4 on v3

--- a/solution.py
+++ b/solution.py
@@ -17,6 +17,7 @@
 TURN_2 = ((0, 1), (3, 2), (1, 3), (2, 0))
 MIDDLE = ((1, 2), (2, 1), (0, 0), (3, 3))
 HANDED = ((2, 3), (1, 0), (3, 2), (0, 1))
+FAR = ((0, 3), (3, 0), (1, 2), (2, 1))
 
 
 def back(pairs):
@@ -124,11 +125,10 @@
     sums[...] = block_sums(adj, 0, [block[...] for block in blocks])
 
 
-def late_sums(adj, early, second, second_other, middle, ends, middle_other, ends_other, *outs):
+def late_sums(adj, early, middle, ends, middle_other, ends_other, *outs):
     inner = in_middle()
-    blocks = [second[...], second_other[...]]
-    blocks += [jnp.where(inner, a[...], b[...]) for a, b in ((middle, ends), (middle_other, ends_other))]
-    sums = early[...] + block_sums(adj, 4, blocks)
+    blocks = [jnp.where(inner, a[...], b[...]) for a, b in ((middle, ends), (middle_other, ends_other))]
+    sums = early[...] + block_sums(adj, 6, blocks)
     height = outs[0].shape[0]
     for k, out in enumerate(outs):
         out[...] = sums[k * height : (k + 1) * height].astype(out.dtype)
@@ -138,12 +138,11 @@
     out[...] = dot(adj[...], items[...])
 
 
-def item_sums(slots, n, *refs):
-    adj_t, shares, outs = refs[:2], refs[2 : 2 + 2 * n], refs[-len(slots) :]
+def item_sums(starts, n, *refs):
+    adj_t, shares, outs = refs[:2], refs[2 : 2 + 2 * n], refs[-len(starts) :]
     users = [jnp.concatenate([share[...] for share in shares[core * n : core * n + n]], axis=0) for core in (0, 1)]
-    edge = outs[0].shape[0]
-    for slot, out in zip(slots, outs):
-        rows = slice(slot * edge, (slot + 1) * edge)
+    for start, out in zip(starts, outs):
+        rows = slice(start, start + out.shape[0])
         out[...] = (dot(adj_t[0][rows, :], users[0]) + dot(adj_t[1][rows, :], users[1])).astype(out.dtype)
 
 
@@ -152,23 +151,33 @@
 
 
 def pass_on(sums, handed, out):
-    given = jnp.where(in_middle(), handed[...].astype(F32), 0)
-    out[...] = (sums[...] + given).astype(out.dtype)
-
-
-def update(n, emb, w_hi, w_lo, *refs, inner=0):
-    parts, outs = refs[:n], refs[n:]
-    side = total(parts[inner:])
-    if inner:
-        side = side + jnp.where(in_middle(), total(parts[:inner]), 0)
-    own = emb[...]
+    direct = out.shape[0] - handed.shape[0]
+    out[:direct, :] = sums[:direct, :].astype(out.dtype)
+    out[direct:, :] = (sums[direct:, :] + jnp.where(in_middle(), handed[...].astype(F32), 0)).astype(out.dtype)
+
+
+def mix(side, own, w_hi, w_lo):
     height = own.shape[0]
     hi, lo = split(jnp.concatenate([side + own, side * own], axis=1))
-    both = dot(jnp.concatenate([hi, lo], axis=0), w_hi[...])
-    mixed = both[:height] + (both[height:] + dot(hi, w_lo[...]))
-    mixed = jnp.where(mixed >= 0, mixed, 0.2 * mixed)
-    for out in outs:
+    both = dot(jnp.concatenate([hi, lo], axis=0), w_hi)
+    mixed = both[:height] + (both[height:] + dot(hi, w_lo))
+    return jnp.where(mixed >= 0, mixed, 0.2 * mixed)
+
+
+def update(n, emb, w_hi, w_lo, *refs):
+    mixed = mix(total(refs[:n]), emb[...], w_hi[...], w_lo[...])
+    for out in refs[n:]:
         out[...] = mixed.astype(out.dtype)
+
+
+def last_update(emb, w_hi, w_lo, own, near, onward, far, middle, new_users, out, new_users_out, sem):
+    copy = pltpu.make_async_copy(new_users, new_users_out, sem)
+    copy.start()
+    side = total((own, near, onward))
+    rest = jnp.where(in_middle(), middle[...].astype(F32), 0)
+    side = side + jnp.concatenate([far[...].astype(F32), rest], axis=0)
+    out[...] = mix(side, emb[...], w_hi[...], w_lo[...])
+    copy.wait()
 
 
 def in_turns(user_emb, item_emb, tiles, block_rows, block_cols, block_counts, w_self, w_inter):
@@ -207,17 +216,19 @@
     (early,) = call(
         early_sums,
         (shape(users, depth, dtype=F32),),
-        (adj, mine, other(mine), first, other(first)),
+        (adj, mine, other(mine), first, other(first), second, other(second)),
         flops=work // 2,
         nbytes=4 << 20,
     )
     own, *others = call(
         late_sums,
         (shape(share, depth, dtype=F32),) + (shape(share, depth),) * 3,
-        (adj, early, second, other(second), middle, ends, other(middle), other(ends)),
+        (adj, early, middle, ends, other(middle), other(ends)),
         flops=work // 2,
         nbytes=4 << 20,
     )
+    others_t = other(after(others_t, own))
+    own = after(own, others_t)
     new_users, user_half = call(
         functools.partial(update, 4),
         (shape(share, depth, dtype=F32), shape(share, depth)),
@@ -226,34 +237,38 @@
         nbytes=3 << 20,
     )
 
-    others_t = other(after(others_t, user_half))
     shares = [user_half] + [swap(user_half, "ia", 4, k) for k in (1, 2, 3)]
     shares += [other(x) for x in shares]
-    (far,) = call(
-        functools.partial(item_sums, (3,), 4),
-        (shape(held, depth),),
+    direct = 160
+    far, handed = call(
+        functools.partial(item_sums, (3 * held, 3 * held + direct), 4),
+        (shape(direct, depth), shape(held - direct, depth)),
         (adj_t, others_t, *shares),
         flops=work // 4,
         nbytes=2 << 20,
     )
-    middle = send(far, back(MIDDLE))
-    handed = send(far, back(HANDED))
+    middle_in = handed
+    handed = send(handed, back(HANDED))
+    far = send(far, FAR)
     own, onward, near = call(
-        functools.partial(item_sums, (0, 1, 2), 4),
+        functools.partial(item_sums, (0, held, 2 * held), 4),
         (shape(held, depth, dtype=F32), shape(held, depth, dtype=F32), shape(held, depth)),
-        (adj_t, others_t, *shares, far),
+        (adj_t, others_t, *shares),
         flops=3 * work // 4,
         nbytes=6 << 20,
     )
+    middle = send(middle_in, back(MIDDLE))
     near = send(near, back(TURN_2))
-    (onward,) = call(pass_on, (shape(held, depth),), (onward, handed), nbytes=1 << 19)
-    (new_items,) = call(
-        functools.partial(update, 4, inner=1),
-        (shape(held, depth, dtype=F32),),
-        (item_emb, w_hi, w_lo, middle, own, near, send(onward, back(TURN_1))),
-        flops=12 * held * depth * depth,
-        nbytes=4 << 20,
-    )
+    (onward,) = call(pass_on, (shape(held, depth),), (after(onward, far), handed), nbytes=1 << 19)
+    new_items, new_users = pl.pallas_call(
+        last_update,
+        out_shape=(shape(held, depth, dtype=F32), shape(share, depth, dtype=F32)),
+        in_specs=[VMEM] * 9,
+        out_specs=(VMEM, pl.BlockSpec(memory_space=pl.ANY)),
+        scratch_shapes=(pltpu.SemaphoreType.DMA,),
+        compiler_params=PARAMS,
+        cost_estimate=pl.CostEstimate(flops=12 * held * depth * depth, bytes_accessed=4 << 20, transcendentals=0),
+    )(item_emb, w_hi, w_lo, own, near, send(onward, back(TURN_1)), far, middle, new_users)
     return (new_users, new_items)
 
 

time: 73.9 us -> 72.1 us (0.976)
  waiting for transfers between devices: 35.8 us -> 34.5 us
    pallas_call x9 -> x8, Pallas kernels: 7.99 us -> 5.63 us  [call(): pl.pallas_call(kernel, out_shape=out_shape, in_specs=[SMEM] * smem + [VME...]
    pallas_call x0 -> x1, Pallas kernels: none -> 1.79 us  [in_turns(): pl.pallas_call(last_update, out_shape=(shape(held, depth, dtype=F32), sha...]
    ppermute x8 -> x9, waiting for transfers between devices: 22.1 us -> 21 us  [send(): lax.ppermute(x, 'au', [(2 * a + core, 2 * b + core) for a, b in pairs for...]
    ppermute x8 -> x9, starting transfers between devices: 15.2 us -> 15.1 us  [send(): lax.ppermute(x, 'au', [(2 * a + core, 2 * b + core) for a, b in pairs for...]
  transfers between devices with their start and end apart: 24 -> 25, of which waited for: 12 -> 14; matrix products, arithmetic and copies ran while one was open for 0% -> 0% of each run, Pallas kernels for 5% -> 6%
where the time goes in v4:
time: 72.1 us; the launch traced here: 71.9 us
  waiting for transfers between devices  34.5 us (48%)
  starting transfers between devices  23.9 us (33%)
  Pallas kernels  7.43 us (10%)
  local copies, waits for them, and re-layouts  3.52 us (5%)
  between operations  1.44 us (2%)
  other arithmetic  1.08 us (1%)
    ppermute x9, waiting for transfers between devices, send(): lax.ppermute(x, 'au', [(2 * a + core, 2 * b + core) for a, b in pairs for...  21 us
    ppermute x9, starting transfers between devices, send(): lax.ppermute(x, 'au', [(2 * a + core, 2 * b + core) for a, b in pairs for...  15.1 us
    ppermute x16, waiting for transfers between devices, swap(): return lax.ppermute(x, axis, [(i, i ^ by) for i in range(n)])  13.5 us
    ppermute x16, starting transfers between devices, swap(): return lax.ppermute(x, axis, [(i, i ^ by) for i in range(n)])  8.8 us
    pallas_call x8, Pallas kernels, call(): pl.pallas_call(kernel, out_shape=out_shape, in_specs=[SMEM] * smem + [VME...  5.63 us
    unnamed x14, local copies, waits for them, and re-layouts  3.52 us
    pallas_call x1, Pallas kernels, in_turns(): pl.pallas_call(last_update, out_shape=(shape(held, depth, dtype=F32), sha...  1.79 us
  transfers between devices with their start and end apart: 25, of which 14 were waited for; matrix products, arithmetic and copies ran while one was open for 0% of the time, Pallas kernels for 6%

profile of v4, /device:TPU:0, one launch (start us, length us, event | category | flops | bytes accessed | tf_op | source)
XLA Modules:
  0.0 71.9 jit_solution(10578851828961040428)
XLA Ops:
  0.6 1.1 %convert_element_type.3.refs_0_ = bf16[256,512]{1,0:T(8,128)(2,1)S(1)} convert(f32[256,512]{1,0:T(8,128)} %emb.1) | non-fusion elementwise | flops 131072 | bytes 786432 | tf_op jit(solution)/shard_map/convert_element_type | solution.py:196
  1.7 4.1 %collective-permute-start.1 = (bf16[256,512]{1,0:T(8,128)(2,1)S(1)}, bf16[256,512]{1,0:T(8,128)(2,1)S(1)}, u32[]{:S(2)}, u32[]{:S(2)}) collective-permute-start(bf16[256,512]{1,0:T(8,128)(2,1)S(1)} %convert_element_type.3.refs_0_), channel_id=1, source_target_pairs={{0,16},{4,20},{24,8},{28,12},{8,0},{12,4},{16,24},{20,28},{1,17},{... | collective-permute-start | bytes 786440 | tf_op jit(solution)/shard_map/ppermute | solution.py:28
  6.5 1.4 %copy-done.1 = bf16[1,12,256,256]{3,2,1,0:T(8,128)(2,1)S(1)} copy-done((bf16[1,12,256,256]{3,2,1,0:T(8,128)(2,1)S(1)}, bf16[1,12,256,256]{3,2,1,0:T(8,128)(2,1)}, u32[]{:S(2)}) %copy-start.1) | copy-done | bytes 1572888
  9.2 1.0 %shard_map.95.adj = bf16[512,2048]{1,0:T(8,128)(2,1)S(1)} custom-call(s32[1,12]{1,0:T(1,128)S(1)} %copy-done.5, s32[1,12]{1,0:T(1,128)S(1)} %copy-done.6, s32[1,1]{1,0:T(1,128)S(6)} %copy.10.count, bf16[1,12,256,256]{3,2,1,0:T(8,128)(2,1)S(1)} %copy-done.1), custom_call_target="tpu_custom_call" | custom-call | bytes 8388608 | tf_op jit(solution)/shard_map/pallas_call | solution.py:48
  11.0 1.2 %shard_map.96 = (bf16[1024,512]{1,0:T(8,128)(2,1)S(1)}, bf16[1024,512]{1,0:T(8,128)(2,1)S(1)}, f32[128,512]{1,0:T(8,128)S(1)}, bf16[1024,512]{1,0:T(8,128)(2,1)S(1)}, bf16[1024,512]{1,0:T(8,128)(2,1)S(1)}) custom-call(bf16[512,2048]{1,0:T(8,128)(2,1)S(1)} %shard_map.95.adj, f32[512,512]{1,0:T(8,128)S(1)} %copy-done.2, f32[512,512]{1,0:T(8,128)S(1)} %copy-done.3, ...), custom_call_target="tpu_custom_call" | custom-call | bytes 9437184 | tf_op jit(solution)/shard_map/pallas_call | solution.py:48
  12.9 4.0 %collective-permute-start.6 = (bf16[256,512]{1,0:T(8,128)(2,1)S(1)}, bf16[256,512]{1,0:T(8,128)(2,1)S(1)}, u32[]{:S(2)}, u32[]{:S(2)}) collective-permute-start(bf16[256,512]{1,0:T(8,128)(2,1)S(1)} %collective-permute-done.1.refs_2_), channel_id=1, source_target_pairs={{16,24},{20,28},{8,0},{12,4},{24,16},{28,20},{0,8},{4,12},{17,25},... | collective-permute-start | bytes 786440 | tf_op jit(solution)/shard_map/ppermute | solution.py:28
  17.4 3.0 %collective-permute-done.3.refs_4_ = bf16[256,512]{1,0:T(8,128)(2,1)S(1)} collective-permute-done((bf16[256,512]{1,0:T(8,128)(2,1)S(1)}, bf16[256,512]{1,0:T(8,128)(2,1)S(1)}, u32[]{:S(2)}, u32[]{:S(2)}) %collective-permute-start.3) | collective-permute-done | bytes 262176 | tf_op jit(solution)/shard_map/ppermute | solution.py:28
  20.9 3.5 %collective-permute-done.6.ends = bf16[256,512]{1,0:T(8,128)(2,1)S(1)} collective-permute-done((bf16[256,512]{1,0:T(8,128)(2,1)S(1)}, bf16[256,512]{1,0:T(8,128)(2,1)S(1)}, u32[]{:S(2)}, u32[]{:S(2)}) %collective-permute-start.6) | collective-permute-done | bytes 262176 | tf_op jit(solution)/shard_map/ppermute | solution.py:28
  24.4 1.0 %shard_map.97.early = f32[512,512]{1,0:T(8,128)S(1)} custom-call(bf16[512,2048]{1,0:T(8,128)(2,1)S(1)} %shard_map.95.adj, bf16[256,512]{1,0:T(8,128)(2,1)S(1)} %convert_element_type.3.refs_0_, bf16[256,512]{1,0:T(8,128)(2,1)S(1)} %collective-permute-done.refs_1_, bf16[256,512]{1,0:T(8,128)(2,1)S(1)} %collective-permute-done.1.refs_2_, ...), custom_call_target="tpu_custom_call" | custom-call | flops 536870912 | bytes 4194304 | tf_op jit(solution)/shard_map/pallas_call | solution.py:48
  26.6 2.6 %collective-permute-start.10 = (bf16[128,512]{1,0:T(8,128)(2,1)S(1)}, bf16[128,512]{1,0:T(8,128)(2,1)S(1)}, u32[]{:S(2)}, u32[]{:S(2)}) collective-permute-start(bf16[128,512]{1,0:T(8,128)(2,1)S(1)} %get-tuple-element.36), channel_id=1, source_target_pairs={{0,3},{1,2},{2,1},{3,0},{4,7},{5,6},{6,5},{7,4},{8,11},{9,10},{10,... | collective-permute-start | bytes 393224 | tf_op jit(solution)/shard_map/ppermute | solution.py:32
  30.1 3.3 %collective-permute-done.10.refs_0_ = bf16[128,512]{1,0:T(8,128)(2,1)S(1)} collective-permute-done((bf16[128,512]{1,0:T(8,128)(2,1)S(1)}, bf16[128,512]{1,0:T(8,128)(2,1)S(1)}, u32[]{:S(2)}, u32[]{:S(2)}) %collective-permute-start.10) | collective-permute-done | bytes 131104 | tf_op jit(solution)/shard_map/ppermute | solution.py:32
  33.4 2.6 %collective-permute-done.11.refs_1_ = bf16[128,512]{1,0:T(8,128)(2,1)S(1)} collective-permute-done((bf16[128,512]{1,0:T(8,128)(2,1)S(1)}, bf16[128,512]{1,0:T(8,128)(2,1)S(1)}, u32[]{:S(2)}, u32[]{:S(2)}) %collective-permute-start.11) | collective-permute-done | bytes 131104 | tf_op jit(solution)/shard_map/ppermute | solution.py:32
  36.8 1.6 %collective-permute-start.13 = (bf16[128,512]{1,0:T(8,128)(2,1)S(1)}, bf16[128,512]{1,0:T(8,128)(2,1)S(1)}, u32[]{:S(2)}, u32[]{:S(2)}) collective-permute-start(bf16[128,512]{1,0:T(8,128)(2,1)S(1)} %get-tuple-element.40.refs_2_), channel_id=1, source_target_pairs={{0,1},{1,0},{2,3},{3,2},{4,5},{5,4},{6,7},{7,6},{8,9},{9,8},{10,11... | collective-permute-start | bytes 393224 | tf_op jit(solution)/shard_map/ppermute | solution.py:32
  39.0 1.3 %collective-permute-start.15 = (bf16[128,512]{1,0:T(8,128)(2,1)S(1)}, bf16[128,512]{1,0:T(8,128)(2,1)S(1)}, u32[]{:S(2)}, u32[]{:S(2)}) collective-permute-start(bf16[128,512]{1,0:T(8,128)(2,1)S(1)} %get-tuple-element.40.refs_2_), channel_id=1, source_target_pairs={{0,3},{1,2},{2,1},{3,0},{4,7},{5,6},{6,5},{7,4},{8,11},{9,10},{10,... | collective-permute-start | bytes 393224 | tf_op jit(solution)/shard_map/ppermute | solution.py:32
  40.4 2.2 %collective-permute-done.13.refs_3_ = bf16[128,512]{1,0:T(8,128)(2,1)S(1)} collective-permute-done((bf16[128,512]{1,0:T(8,128)(2,1)S(1)}, bf16[128,512]{1,0:T(8,128)(2,1)S(1)}, u32[]{:S(2)}, u32[]{:S(2)}) %collective-permute-start.13) | collective-permute-done | bytes 131104 | tf_op jit(solution)/shard_map/ppermute | solution.py:32
  42.6 3.7 %collective-permute-done.14.refs_4_ = bf16[128,512]{1,0:T(8,128)(2,1)S(1)} collective-permute-done((bf16[128,512]{1,0:T(8,128)(2,1)S(1)}, bf16[128,512]{1,0:T(8,128)(2,1)S(1)}, u32[]{:S(2)}, u32[]{:S(2)}) %collective-permute-start.14) | collective-permute-done | bytes 131104 | tf_op jit(solution)/shard_map/ppermute | solution.py:32
  48.3 2.5 %collective-permute-start.21 = (bf16[160,512]{1,0:T(8,128)(2,1)S(1)}, bf16[160,512]{1,0:T(8,128)(2,1)S(1)}, u32[]{:S(2)}, u32[]{:S(2)}) collective-permute-start(bf16[160,512]{1,0:T(8,128)(2,1)S(1)} %get-tuple-element.44), channel_id=1, source_target_pairs={{0,24},{4,28},{24,0},{28,4},{8,16},{12,20},{16,8},{20,12},{1,25},{... | collective-permute-start | bytes 491528 | tf_op jit(solution)/shard_map/ppermute | solution.py:28
  51.8 1.9 %collective-permute-start.20 = (bf16[256,512]{1,0:T(8,128)(2,1)S(1)}, bf16[256,512]{1,0:T(8,128)(2,1)S(1)}, u32[]{:S(2)}, u32[]{:S(2)}) collective-permute-start(bf16[256,512]{1,0:T(8,128)(2,1)S(1)} %get-tuple-element.42), channel_id=1, source_target_pairs={{8,0},{12,4},{16,24},{20,28},{24,8},{28,12},{0,16},{4,20},{9,1},{1... | collective-permute-start | bytes 786440 | tf_op jit(solution)/shard_map/ppermute | solution.py:28
  53.8 3.5 %collective-permute-done.21.far = bf16[160,512]{1,0:T(8,128)(2,1)S(1)} collective-permute-done((bf16[160,512]{1,0:T(8,128)(2,1)S(1)}, bf16[160,512]{1,0:T(8,128)(2,1)S(1)}, u32[]{:S(2)}, u32[]{:S(2)}) %collective-permute-start.21) | collective-permute-done | bytes 163872 | tf_op jit(solution)/shard_map/ppermute | solution.py:28
  57.2 1.6 %collective-permute-done.22.handed = bf16[96,512]{1,0:T(8,128)(2,1)S(1)} collective-permute-done((bf16[96,512]{1,0:T(8,128)(2,1)S(1)}, bf16[96,512]{1,0:T(8,128)(2,1)S(1)}, u32[]{:S(2)}, u32[]{:S(2)}) %collective-permute-start.22) | collective-permute-done | bytes 98336 | tf_op jit(solution)/shard_map/ppermute | solution.py:28
  58.9 1.1 %collective-permute-start.23 = (bf16[256,512]{1,0:T(8,128)(2,1)S(1)}, bf16[256,512]{1,0:T(8,128)(2,1)S(1)}, u32[]{:S(2)}, u32[]{:S(2)}) collective-permute-start(bf16[256,512]{1,0:T(8,128)(2,1)S(1)} %shard_map.102), channel_id=1, source_target_pairs={{16,0},{20,4},{8,24},{12,28},{0,8},{4,12},{24,16},{28,20},{17,1},{... | collective-permute-start | bytes 786440 | tf_op jit(solution)/shard_map/ppermute | solution.py:28
  60.7 4.3 %collective-permute-done.20.near = bf16[256,512]{1,0:T(8,128)(2,1)S(1)} collective-permute-done((bf16[256,512]{1,0:T(8,128)(2,1)S(1)}, bf16[256,512]{1,0:T(8,128)(2,1)S(1)}, u32[]{:S(2)}, u32[]{:S(2)}) %collective-permute-start.20) | collective-permute-done | bytes 262176 | tf_op jit(solution)/shard_map/ppermute | solution.py:28
  65.0 5.1 %collective-permute-done.23.onward = bf16[256,512]{1,0:T(8,128)(2,1)S(1)} collective-permute-done((bf16[256,512]{1,0:T(8,128)(2,1)S(1)}, bf16[256,512]{1,0:T(8,128)(2,1)S(1)}, u32[]{:S(2)}, u32[]{:S(2)}) %collective-permute-start.23) | collective-permute-done | bytes 262176 | tf_op jit(solution)/shard_map/ppermute | solution.py:28
  70.1 1.8 %shard_map.103 = (f32[256,512]{1,0:T(8,128)}, f32[128,512]{1,0:T(8,128)}) custom-call(f32[256,512]{1,0:T(8,128)S(1)} %copy-done, bf16[1024,512]{1,0:T(8,128)(2,1)S(1)} %get-tuple-element.26.w_hi, bf16[1024,512]{1,0:T(8,128)(2,1)S(1)} %get-tuple-element.27.w_lo, f32[256,512]{1,0:T(8,128)S(1)} %get-tuple-element.41.own, ...), custom_call_target="tpu_custom_call" | custom-call | flops 805306368 | bytes 4194304 | tf_op jit(solution)/shard_map/pallas_call | solution.py:263
  (50 shorter events, 11.1 us)
Async XLA Ops:
  1.7 11.2 %collective-permute-start.1 = (bf16[256,512]{1,0:T(8,128)(2,1)S(1)}, bf16[256,512]{1,0:T(8,128)(2,1)S(1)}, u32[]{:S(2)}, u32[]{:S(2)}) collective-permute-start(bf16[256,512]{1,0:T(8,128)(2,1)S(1)} %convert_element_type.3.refs_0_), channel_id=1, source_target_pairs={{0,16},{4,20},{24,8},{28,12},{8,0},{12,4},{16,24},{20,28},{1,17},{... | collective-permute-start | bytes 786440 | tf_op jit(solution)/shard_map/ppermute | solution.py:28
  10.2 10.2 %collective-permute-start.3 = (bf16[256,512]{1,0:T(8,128)(2,1)S(1)}, bf16[256,512]{1,0:T(8,128)(2,1)S(1)}, u32[]{:S(2)}, u32[]{:S(2)}) collective-permute-start(bf16[256,512]{1,0:T(8,128)(2,1)S(1)} %convert_element_type.3.refs_0_), channel_id=1, source_target_pairs={{0,8},{4,12},{24,16},{28,20},{8,24},{12,28},{16,0},{20,4},{1,9},{5... | collective-permute-start | bytes 786440 | tf_op jit(solution)/shard_map/ppermute | solution.py:28
  12.2 8.2 %collective-permute-start.5 = (bf16[256,512]{1,0:T(8,128)(2,1)S(1)}, bf16[256,512]{1,0:T(8,128)(2,1)S(1)}, u32[]{:S(2)}, u32[]{:S(2)}) collective-permute-start(bf16[256,512]{1,0:T(8,128)(2,1)S(1)} %convert_element_type.3.refs_0_), channel_id=1, source_target_pairs={{8,16},{12,20},{16,8},{20,12},{0,0},{4,4},{24,24},{28,28},{9,17},{... | collective-permute-start | bytes 786440 | tf_op jit(solution)/shard_map/ppermute | solution.py:28
  12.9 11.5 %collective-permute-start.6 = (bf16[256,512]{1,0:T(8,128)(2,1)S(1)}, bf16[256,512]{1,0:T(8,128)(2,1)S(1)}, u32[]{:S(2)}, u32[]{:S(2)}) collective-permute-start(bf16[256,512]{1,0:T(8,128)(2,1)S(1)} %collective-permute-done.1.refs_2_), channel_id=1, source_target_pairs={{16,24},{20,28},{8,0},{12,4},{24,16},{28,20},{0,8},{4,12},{17,25},... | collective-permute-start | bytes 786440 | tf_op jit(solution)/shard_map/ppermute | solution.py:28
  16.9 7.5 %collective-permute-start = (bf16[256,512]{1,0:T(8,128)(2,1)S(1)}, bf16[256,512]{1,0:T(8,128)(2,1)S(1)}, u32[]{:S(2)}, u32[]{:S(2)}) collective-permute-start(bf16[256,512]{1,0:T(8,128)(2,1)S(1)} %convert_element_type.3.refs_0_), channel_id=1, source_target_pairs={{0,4},{4,0},{8,12},{12,8},{16,20},{20,16},{24,28},{28,24},{1,5},{5... | collective-permute-start | bytes 786440 | tf_op jit(solution)/shard_map/ppermute | solution.py:32
  16.9 7.5 %collective-permute-start.2 = (bf16[256,512]{1,0:T(8,128)(2,1)S(1)}, bf16[256,512]{1,0:T(8,128)(2,1)S(1)}, u32[]{:S(2)}, u32[]{:S(2)}) collective-permute-start(bf16[256,512]{1,0:T(8,128)(2,1)S(1)} %collective-permute-done.1.refs_2_), channel_id=1, source_target_pairs={{0,4},{4,0},{8,12},{12,8},{16,20},{20,16},{24,28},{28,24},{1,5},{5... | collective-permute-start | bytes 786440 | tf_op jit(solution)/shard_map/ppermute | solution.py:32
  20.4 4.1 %collective-permute-start.4 = (bf16[256,512]{1,0:T(8,128)(2,1)S(1)}, bf16[256,512]{1,0:T(8,128)(2,1)S(1)}, u32[]{:S(2)}, u32[]{:S(2)}) collective-permute-start(bf16[256,512]{1,0:T(8,128)(2,1)S(1)} %collective-permute-done.3.refs_4_), channel_id=1, source_target_pairs={{0,4},{4,0},{8,12},{12,8},{16,20},{20,16},{24,28},{28,24},{1,5},{5... | collective-permute-start | bytes 786440 | tf_op jit(solution)/shard_map/ppermute | solution.py:32
  20.4 5.0 %collective-permute-start.7 = (bf16[256,512]{1,0:T(8,128)(2,1)S(1)}, bf16[256,512]{1,0:T(8,128)(2,1)S(1)}, u32[]{:S(2)}, u32[]{:S(2)}) collective-permute-start(bf16[256,512]{1,0:T(8,128)(2,1)S(1)} %collective-permute-done.5.middle), channel_id=1, source_target_pairs={{0,4},{4,0},{8,12},{12,8},{16,20},{20,16},{24,28},{28,24},{1,5},{5... | collective-permute-start | bytes 786440 | tf_op jit(solution)/shard_map/ppermute | solution.py:32
  24.4 1.5 %collective-permute-start.8 = (bf16[256,512]{1,0:T(8,128)(2,1)S(1)}, bf16[256,512]{1,0:T(8,128)(2,1)S(1)}, u32[]{:S(2)}, u32[]{:S(2)}) collective-permute-start(bf16[256,512]{1,0:T(8,128)(2,1)S(1)} %collective-permute-done.6.ends), channel_id=1, source_target_pairs={{0,4},{4,0},{8,12},{12,8},{16,20},{20,16},{24,28},{28,24},{1,5},{5... | collective-permute-start | bytes 786440 | tf_op jit(solution)/shard_map/ppermute | solution.py:32
  26.4 3.7 %collective-permute-start.9 = (bf16[1024,512]{1,0:T(8,128)(2,1)S(1)}, bf16[1024,512]{1,0:T(8,128)(2,1)S(1)}, u32[]{:S(2)}, u32[]{:S(2)}) collective-permute-start(bf16[1024,512]{1,0:T(8,128)(2,1)S(1)} %get-tuple-element.34), channel_id=1, source_target_pairs={{0,4},{4,0},{8,12},{12,8},{16,20},{20,16},{24,28},{28,24},{1,5},{5... | collective-permute-start | bytes 3145736 | tf_op jit(solution)/shard_map/ppermute | solution.py:32
  26.6 6.8 %collective-permute-start.10 = (bf16[128,512]{1,0:T(8,128)(2,1)S(1)}, bf16[128,512]{1,0:T(8,128)(2,1)S(1)}, u32[]{:S(2)}, u32[]{:S(2)}) collective-permute-start(bf16[128,512]{1,0:T(8,128)(2,1)S(1)} %get-tuple-element.36), channel_id=1, source_target_pairs={{0,3},{1,2},{2,1},{3,0},{4,7},{5,6},{6,5},{7,4},{8,11},{9,10},{10,... | collective-permute-start | bytes 393224 | tf_op jit(solution)/shard_map/ppermute | solution.py:32
  29.2 6.9 %collective-permute-start.11 = (bf16[128,512]{1,0:T(8,128)(2,1)S(1)}, bf16[128,512]{1,0:T(8,128)(2,1)S(1)}, u32[]{:S(2)}, u32[]{:S(2)}) collective-permute-start(bf16[128,512]{1,0:T(8,128)(2,1)S(1)} %get-tuple-element.37), channel_id=1, source_target_pairs={{0,2},{1,3},{2,0},{3,1},{4,6},{5,7},{6,4},{7,5},{8,10},{9,11},{10,... | collective-permute-start | bytes 393224 | tf_op jit(solution)/shard_map/ppermute | solution.py:32
  29.6 6.7 %collective-permute-start.12 = (bf16[128,512]{1,0:T(8,128)(2,1)S(1)}, bf16[128,512]{1,0:T(8,128)(2,1)S(1)}, u32[]{:S(2)}, u32[]{:S(2)}) collective-permute-start(bf16[128,512]{1,0:T(8,128)(2,1)S(1)} %get-tuple-element.38), channel_id=1, source_target_pairs={{0,1},{1,0},{2,3},{3,2},{4,5},{5,4},{6,7},{7,6},{8,9},{9,8},{10,11... | collective-permute-start | bytes 393224 | tf_op jit(solution)/shard_map/ppermute | solution.py:32
  36.8 5.7 %collective-permute-start.13 = (bf16[128,512]{1,0:T(8,128)(2,1)S(1)}, bf16[128,512]{1,0:T(8,128)(2,1)S(1)}, u32[]{:S(2)}, u32[]{:S(2)}) collective-permute-start(bf16[128,512]{1,0:T(8,128)(2,1)S(1)} %get-tuple-element.40.refs_2_), channel_id=1, source_target_pairs={{0,1},{1,0},{2,3},{3,2},{4,5},{5,4},{6,7},{7,6},{8,9},{9,8},{10,11... | collective-permute-start | bytes 393224 | tf_op jit(solution)/shard_map/ppermute | solution.py:32
  38.5 7.8 %collective-permute-start.14 = (bf16[128,512]{1,0:T(8,128)(2,1)S(1)}, bf16[128,512]{1,0:T(8,128)(2,1)S(1)}, u32[]{:S(2)}, u32[]{:S(2)}) collective-permute-start(bf16[128,512]{1,0:T(8,128)(2,1)S(1)} %get-tuple-element.40.refs_2_), channel_id=1, source_target_pairs={{0,2},{1,3},{2,0},{3,1},{4,6},{5,7},{6,4},{7,5},{8,10},{9,11},{10,... | collective-permute-start | bytes 393224 | tf_op jit(solution)/shard_map/ppermute | solution.py:32
  39.0 7.2 %collective-permute-start.15 = (bf16[128,512]{1,0:T(8,128)(2,1)S(1)}, bf16[128,512]{1,0:T(8,128)(2,1)S(1)}, u32[]{:S(2)}, u32[]{:S(2)}) collective-permute-start(bf16[128,512]{1,0:T(8,128)(2,1)S(1)} %get-tuple-element.40.refs_2_), channel_id=1, source_target_pairs={{0,3},{1,2},{2,1},{3,0},{4,7},{5,6},{6,5},{7,4},{8,11},{9,10},{10,... | collective-permute-start | bytes 393224 | tf_op jit(solution)/shard_map/ppermute | solution.py:32
  40.4 6.4 %collective-permute-start.16 = (bf16[128,512]{1,0:T(8,128)(2,1)S(1)}, bf16[128,512]{1,0:T(8,128)(2,1)S(1)}, u32[]{:S(2)}, u32[]{:S(2)}) collective-permute-start(bf16[128,512]{1,0:T(8,128)(2,1)S(1)} %get-tuple-element.40.refs_2_), channel_id=1, source_target_pairs={{0,4},{4,0},{8,12},{12,8},{16,20},{20,16},{24,28},{28,24},{1,5},{5... | collective-permute-start | bytes 393224 | tf_op jit(solution)/shard_map/ppermute | solution.py:32
  42.5 4.2 %collective-permute-start.17 = (bf16[128,512]{1,0:T(8,128)(2,1)S(1)}, bf16[128,512]{1,0:T(8,128)(2,1)S(1)}, u32[]{:S(2)}, u32[]{:S(2)}) collective-permute-start(bf16[128,512]{1,0:T(8,128)(2,1)S(1)} %collective-permute-done.13.refs_3_), channel_id=1, source_target_pairs={{0,4},{4,0},{8,12},{12,8},{16,20},{20,16},{24,28},{28,24},{1,5},{5... | collective-permute-start | bytes 393224 | tf_op jit(solution)/shard_map/ppermute | solution.py:32
  46.2 1.3 %collective-permute-start.18 = (bf16[128,512]{1,0:T(8,128)(2,1)S(1)}, bf16[128,512]{1,0:T(8,128)(2,1)S(1)}, u32[]{:S(2)}, u32[]{:S(2)}) collective-permute-start(bf16[128,512]{1,0:T(8,128)(2,1)S(1)} %collective-permute-done.14.refs_4_), channel_id=1, source_target_pairs={{0,4},{4,0},{8,12},{12,8},{16,20},{20,16},{24,28},{28,24},{1,5},{5... | collective-permute-start | bytes 393224 | tf_op jit(solution)/shard_map/ppermute | solution.py:32
  46.2 1.5 %collective-permute-start.19 = (bf16[128,512]{1,0:T(8,128)(2,1)S(1)}, bf16[128,512]{1,0:T(8,128)(2,1)S(1)}, u32[]{:S(2)}, u32[]{:S(2)}) collective-permute-start(bf16[128,512]{1,0:T(8,128)(2,1)S(1)} %collective-permute-done.15.refs_5_), channel_id=1, source_target_pairs={{0,4},{4,0},{8,12},{12,8},{16,20},{20,16},{24,28},{28,24},{1,5},{5... | collective-permute-start | bytes 393224 | tf_op jit(solution)/shard_map/ppermute | solution.py:32
  48.3 9.0 %collective-permute-start.21 = (bf16[160,512]{1,0:T(8,128)(2,1)S(1)}, bf16[160,512]{1,0:T(8,128)(2,1)S(1)}, u32[]{:S(2)}, u32[]{:S(2)}) collective-permute-start(bf16[160,512]{1,0:T(8,128)(2,1)S(1)} %get-tuple-element.44), channel_id=1, source_target_pairs={{0,24},{4,28},{24,0},{28,4},{8,16},{12,20},{16,8},{20,12},{1,25},{... | collective-permute-start | bytes 491528 | tf_op jit(solution)/shard_map/ppermute | solution.py:28
  50.8 8.1 %collective-permute-start.22 = (bf16[96,512]{1,0:T(8,128)(2,1)S(1)}, bf16[96,512]{1,0:T(8,128)(2,1)S(1)}, u32[]{:S(2)}, u32[]{:S(2)}) collective-permute-start(bf16[96,512]{1,0:T(8,128)(2,1)S(1)} %get-tuple-element.46), channel_id=1, source_target_pairs={{24,16},{28,20},{0,8},{4,12},{16,24},{20,28},{8,0},{12,4},{25,17},... | collective-permute-start | bytes 294920 | tf_op jit(solution)/shard_map/ppermute | solution.py:28
  51.8 13.2 %collective-permute-start.20 = (bf16[256,512]{1,0:T(8,128)(2,1)S(1)}, bf16[256,512]{1,0:T(8,128)(2,1)S(1)}, u32[]{:S(2)}, u32[]{:S(2)}) collective-permute-start(bf16[256,512]{1,0:T(8,128)(2,1)S(1)} %get-tuple-element.42), channel_id=1, source_target_pairs={{8,0},{12,4},{16,24},{20,28},{24,8},{28,12},{0,16},{4,20},{9,1},{1... | collective-permute-start | bytes 786440 | tf_op jit(solution)/shard_map/ppermute | solution.py:28
  58.9 11.2 %collective-permute-start.23 = (bf16[256,512]{1,0:T(8,128)(2,1)S(1)}, bf16[256,512]{1,0:T(8,128)(2,1)S(1)}, u32[]{:S(2)}, u32[]{:S(2)}) collective-permute-start(bf16[256,512]{1,0:T(8,128)(2,1)S(1)} %shard_map.102), channel_id=1, source_target_pairs={{16,0},{20,4},{8,24},{12,28},{0,8},{4,12},{24,16},{28,20},{17,1},{... | collective-permute-start | bytes 786440 | tf_op jit(solution)/shard_map/ppermute | solution.py:28
  (8 other events, 29.8 us)

commit v5 on v3

--- a/solution.py
+++ b/solution.py
@@ -15,7 +15,7 @@
 
 TURN_1 = ((0, 2), (3, 1), (1, 0), (2, 3))
 TURN_2 = ((0, 1), (3, 2), (1, 3), (2, 0))
-MIDDLE = ((1, 2), (2, 1), (0, 0), (3, 3))
+MIDDLE = ((1, 2), (2, 1))
 HANDED = ((2, 3), (1, 0), (3, 2), (0, 1))
 
 
@@ -24,7 +24,9 @@
 
 
 def send(x, pairs):
-    return lax.ppermute(x, "au", [(2 * a + core, 2 * b + core) for a, b in pairs for core in (0, 1)])
+    perm = [(2 * a + core, 2 * b + core) for a, b in pairs for core in (0, 1)]
+    perm += [(i, i ^ 1) for i in range(8) if i // 2 not in [a for a, _ in pairs]]
+    return lax.ppermute(x, "au", perm)
 
 
 def swap(x, axis, n, by):
@@ -124,11 +126,10 @@
     sums[...] = block_sums(adj, 0, [block[...] for block in blocks])
 
 
-def late_sums(adj, early, second, second_other, middle, ends, middle_other, ends_other, *outs):
+def late_sums(adj, early, middle, ends, middle_other, ends_other, *outs):
     inner = in_middle()
-    blocks = [second[...], second_other[...]]
-    blocks += [jnp.where(inner, a[...], b[...]) for a, b in ((middle, ends), (middle_other, ends_other))]
-    sums = early[...] + block_sums(adj, 4, blocks)
+    blocks = [jnp.where(inner, a[...], b[...]) for a, b in ((middle, ends), (middle_other, ends_other))]
+    sums = early[...] + block_sums(adj, 6, blocks)
     height = outs[0].shape[0]
     for k, out in enumerate(outs):
         out[...] = sums[k * height : (k + 1) * height].astype(out.dtype)
@@ -147,6 +148,11 @@
         out[...] = (dot(adj_t[0][rows, :], users[0]) + dot(adj_t[1][rows, :], users[1])).astype(out.dtype)
 
 
+def item_sums_and(starts, n, *refs):
+    refs[-1][...] = refs[-len(starts) - 2][...]
+    item_sums(starts, n, *refs[: -len(starts) - 2], *refs[-len(starts) - 1 : -1])
+
+
 def all_sums(adj_t, users, out):
     out[...] = dot(adj_t[...], users[...])
 
@@ -156,19 +162,33 @@
     out[...] = (sums[...] + given).astype(out.dtype)
 
 
-def update(n, emb, w_hi, w_lo, *refs, inner=0):
-    parts, outs = refs[:n], refs[n:]
-    side = total(parts[inner:])
-    if inner:
-        side = side + jnp.where(in_middle(), total(parts[:inner]), 0)
-    own = emb[...]
+def mix(side, own, w_hi, w_lo):
     height = own.shape[0]
     hi, lo = split(jnp.concatenate([side + own, side * own], axis=1))
-    both = dot(jnp.concatenate([hi, lo], axis=0), w_hi[...])
-    mixed = both[:height] + (both[height:] + dot(hi, w_lo[...]))
-    mixed = jnp.where(mixed >= 0, mixed, 0.2 * mixed)
-    for out in outs:
+    both = dot(jnp.concatenate([hi, lo], axis=0), w_hi)
+    mixed = both[:height] + (both[height:] + dot(hi, w_lo))
+    return jnp.where(mixed >= 0, mixed, 0.2 * mixed)
+
+
+def update(n, emb, w_hi, w_lo, *refs):
+    mixed = mix(total(refs[:n]), emb[...], w_hi[...], w_lo[...])
+    for out in refs[n:]:
         out[...] = mixed.astype(out.dtype)
+
+
+def last_update(emb, w_hi, w_lo, middle, own, near, onward, out, ready, sems):
+    inner = in_middle()
+    n = sems.shape[0]
+    copies = []
+    for k in range(n):
+        rows = slice(k * (out.shape[0] // n), (k + 1) * (out.shape[0] // n))
+        side = own[rows, :] + near[rows, :].astype(F32) + onward[rows, :].astype(F32)
+        side = side + jnp.where(inner, middle[rows, :].astype(F32), 0)
+        ready[rows, :] = mix(side, emb[rows, :], w_hi[...], w_lo[...])
+        copies.append(pltpu.make_async_copy(ready.at[rows, :], out.at[rows, :], sems.at[k]))
+        copies[k].start()
+    for copy in copies:
+        copy.wait()
 
 
 def in_turns(user_emb, item_emb, tiles, block_rows, block_cols, block_counts, w_self, w_inter):
@@ -207,17 +227,19 @@
     (early,) = call(
         early_sums,
         (shape(users, depth, dtype=F32),),
-        (adj, mine, other(mine), first, other(first)),
+        (adj, mine, other(mine), first, other(first), second, other(second)),
         flops=work // 2,
         nbytes=4 << 20,
     )
     own, *others = call(
         late_sums,
         (shape(share, depth, dtype=F32),) + (shape(share, depth),) * 3,
-        (adj, early, second, other(second), middle, ends, other(middle), other(ends)),
+        (adj, early, middle, ends, other(middle), other(ends)),
         flops=work // 2,
         nbytes=4 << 20,
     )
+    others_t = other(after(others_t, own))
+    own = after(own, others_t)
     new_users, user_half = call(
         functools.partial(update, 4),
         (shape(share, depth, dtype=F32), shape(share, depth)),
@@ -226,7 +248,6 @@
         nbytes=3 << 20,
     )
 
-    others_t = other(after(others_t, user_half))
     shares = [user_half] + [swap(user_half, "ia", 4, k) for k in (1, 2, 3)]
     shares += [other(x) for x in shares]
     (far,) = call(
@@ -238,22 +259,31 @@
     )
     middle = send(far, back(MIDDLE))
     handed = send(far, back(HANDED))
-    own, onward, near = call(
-        functools.partial(item_sums, (0, 1, 2), 4),
-        (shape(held, depth, dtype=F32), shape(held, depth, dtype=F32), shape(held, depth)),
+    own, onward = call(
+        functools.partial(item_sums, (0, 1), 4),
+        (shape(held, depth, dtype=F32), shape(held, depth, dtype=F32)),
         (adj_t, others_t, *shares, far),
         flops=3 * work // 4,
         nbytes=6 << 20,
     )
+    near, new_users = call(
+        functools.partial(item_sums_and, (2,), 4),
+        (shape(held, depth), shape(share, depth, dtype=F32)),
+        (adj_t, others_t, *shares, own, new_users),
+        flops=work // 4,
+        nbytes=2 << 20,
+    )
     near = send(near, back(TURN_2))
     (onward,) = call(pass_on, (shape(held, depth),), (onward, handed), nbytes=1 << 19)
-    (new_items,) = call(
-        functools.partial(update, 4, inner=1),
-        (shape(held, depth, dtype=F32),),
-        (item_emb, w_hi, w_lo, middle, own, near, send(onward, back(TURN_1))),
-        flops=12 * held * depth * depth,
-        nbytes=4 << 20,
-    )
+    new_items = pl.pallas_call(
+        last_update,
+        out_shape=shape(held, depth, dtype=F32),
+        in_specs=[VMEM] * 7,
+        out_specs=pl.BlockSpec(memory_space=pl.ANY),
+        scratch_shapes=(pltpu.VMEM((held, depth), F32), pltpu.SemaphoreType.DMA((2,))),
+        compiler_params=PARAMS,
+        cost_estimate=pl.CostEstimate(flops=12 * held * depth * depth, bytes_accessed=4 << 20, transcendentals=0),
+    )(item_emb, w_hi, w_lo, middle, own, near, send(onward, back(TURN_1)))
     return (new_users, new_items)
 
 

time: 73.9 us -> 71.4 us (0.966)
  starting transfers between devices: 23.8 us -> 19.9 us
  waiting for transfers between devices: 35.8 us -> 37.2 us
    ppermute x8, starting transfers between devices: 15.2 us -> 11.1 us  [send(): return lax.ppermute(x, 'au', perm)]
    pallas_call x0 -> x1, Pallas kernels: none -> 1.71 us  [in_turns(): pl.pallas_call(last_update, out_shape=shape(held, depth, dtype=F32), in_s...]
    pallas_call x9, Pallas kernels: 7.99 us -> 6.28 us  [call(): pl.pallas_call(kernel, out_shape=out_shape, in_specs=[SMEM] * smem + [VME...]
    ppermute x8, waiting for transfers between devices: 22.1 us -> 23.8 us  [send(): return lax.ppermute(x, 'au', perm)]
  transfers between devices with their start and end apart: 24 -> 24, of which waited for: 12 -> 13; matrix products, arithmetic and copies ran while one was open for 0% -> 0% of each run, Pallas kernels for 5% -> 7%
where the time goes in v5:
time: 71.4 us; the launch traced here: 71.2 us
  waiting for transfers between devices  37.2 us (52%)
  starting transfers between devices  19.9 us (28%)
  Pallas kernels  7.99 us (11%)
  local copies, waits for them, and re-layouts  3.66 us (5%)
  between operations  1.41 us (2%)
  other arithmetic  1.08 us (2%)
    ppermute x8, waiting for transfers between devices, send(): return lax.ppermute(x, 'au', perm)  23.8 us
    ppermute x16, waiting for transfers between devices, swap(): return lax.ppermute(x, axis, [(i, i ^ by) for i in range(n)])  13.4 us
    ppermute x8, starting transfers between devices, send(): return lax.ppermute(x, 'au', perm)  11.1 us
    ppermute x16, starting transfers between devices, swap(): return lax.ppermute(x, axis, [(i, i ^ by) for i in range(n)])  8.82 us
    pallas_call x9, Pallas kernels, call(): pl.pallas_call(kernel, out_shape=out_shape, in_specs=[SMEM] * smem + [VME...  6.28 us
    unnamed x14, local copies, waits for them, and re-layouts  3.66 us
    pallas_call x1, Pallas kernels, in_turns(): pl.pallas_call(last_update, out_shape=shape(held, depth, dtype=F32), in_s...  1.71 us
  transfers between devices with their start and end apart: 24, of which 13 were waited for; matrix products, arithmetic and copies ran while one was open for 0% of the time, Pallas kernels for 7%

profile of v5, /device:TPU:0, one launch (start us, length us, event | category | flops | bytes accessed | tf_op | source)
XLA Modules:
  0.0 71.2 jit_solution(510322649191244885)
XLA Ops:
  0.6 1.1 %convert_element_type.3.refs_0_ = bf16[256,512]{1,0:T(8,128)(2,1)S(1)} convert(f32[256,512]{1,0:T(8,128)} %emb.1) | non-fusion elementwise | flops 131072 | bytes 786432 | tf_op jit(solution)/shard_map/convert_element_type | solution.py:207
  1.7 4.1 %collective-permute-start.1 = (bf16[256,512]{1,0:T(8,128)(2,1)S(1)}, bf16[256,512]{1,0:T(8,128)(2,1)S(1)}, u32[]{:S(2)}, u32[]{:S(2)}) collective-permute-start(bf16[256,512]{1,0:T(8,128)(2,1)S(1)} %convert_element_type.3.refs_0_), channel_id=1, source_target_pairs={{0,16},{4,20},{24,8},{28,12},{8,0},{12,4},{16,24},{20,28},{1,17},{... | collective-permute-start | bytes 786440 | tf_op jit(solution)/shard_map/ppermute | solution.py:29
  6.5 1.4 %copy-done.1 = bf16[1,12,256,256]{3,2,1,0:T(8,128)(2,1)S(1)} copy-done((bf16[1,12,256,256]{3,2,1,0:T(8,128)(2,1)S(1)}, bf16[1,12,256,256]{3,2,1,0:T(8,128)(2,1)}, u32[]{:S(2)}) %copy-start.1) | copy-done | bytes 1572888
  9.2 0.8 %shard_map.95.adj = bf16[512,2048]{1,0:T(8,128)(2,1)S(1)} custom-call(s32[1,12]{1,0:T(1,128)S(1)} %copy-done.5, s32[1,12]{1,0:T(1,128)S(1)} %copy-done.6, s32[1,1]{1,0:T(1,128)S(6)} %copy.10.count, bf16[1,12,256,256]{3,2,1,0:T(8,128)(2,1)S(1)} %copy-done.1), custom_call_target="tpu_custom_call" | custom-call | bytes 8388608 | tf_op jit(solution)/shard_map/pallas_call | solution.py:49
  11.0 1.2 %shard_map.96 = (bf16[1024,512]{1,0:T(8,128)(2,1)S(1)}, bf16[1024,512]{1,0:T(8,128)(2,1)S(1)}, f32[128,512]{1,0:T(8,128)S(1)}, bf16[1024,512]{1,0:T(8,128)(2,1)S(1)}, bf16[1024,512]{1,0:T(8,128)(2,1)S(1)}) custom-call(bf16[512,2048]{1,0:T(8,128)(2,1)S(1)} %shard_map.95.adj, f32[512,512]{1,0:T(8,128)S(1)} %copy-done.2, f32[512,512]{1,0:T(8,128)S(1)} %copy-done.3, ...), custom_call_target="tpu_custom_call" | custom-call | bytes 9437184 | tf_op jit(solution)/shard_map/pallas_call | solution.py:49
  12.5 2.3 %collective-permute-start.6 = (bf16[256,512]{1,0:T(8,128)(2,1)S(1)}, bf16[256,512]{1,0:T(8,128)(2,1)S(1)}, u32[]{:S(2)}, u32[]{:S(2)}) collective-permute-start(bf16[256,512]{1,0:T(8,128)(2,1)S(1)} %collective-permute-done.1.refs_2_), channel_id=1, source_target_pairs={{16,24},{20,28},{8,0},{12,4},{24,16},{28,20},{0,8},{4,12},{17,25},... | collective-permute-start | bytes 786440 | tf_op jit(solution)/shard_map/ppermute | solution.py:29
  15.3 4.9 %collective-permute-done.3.refs_4_ = bf16[256,512]{1,0:T(8,128)(2,1)S(1)} collective-permute-done((bf16[256,512]{1,0:T(8,128)(2,1)S(1)}, bf16[256,512]{1,0:T(8,128)(2,1)S(1)}, u32[]{:S(2)}, u32[]{:S(2)}) %collective-permute-start.3) | collective-permute-done | bytes 262176 | tf_op jit(solution)/shard_map/ppermute | solution.py:29
  20.8 3.7 %collective-permute-done.6.ends = bf16[256,512]{1,0:T(8,128)(2,1)S(1)} collective-permute-done((bf16[256,512]{1,0:T(8,128)(2,1)S(1)}, bf16[256,512]{1,0:T(8,128)(2,1)S(1)}, u32[]{:S(2)}, u32[]{:S(2)}) %collective-permute-start.6) | collective-permute-done | bytes 262176 | tf_op jit(solution)/shard_map/ppermute | solution.py:29
  24.5 1.0 %shard_map.97.early = f32[512,512]{1,0:T(8,128)S(1)} custom-call(bf16[512,2048]{1,0:T(8,128)(2,1)S(1)} %shard_map.95.adj, bf16[256,512]{1,0:T(8,128)(2,1)S(1)} %convert_element_type.3.refs_0_, bf16[256,512]{1,0:T(8,128)(2,1)S(1)} %collective-permute-done.refs_1_, bf16[256,512]{1,0:T(8,128)(2,1)S(1)} %collective-permute-done.1.refs_2_, ...), custom_call_target="tpu_custom_call" | custom-call | flops 536870912 | bytes 4194304 | tf_op jit(solution)/shard_map/pallas_call | solution.py:49
  26.7 2.4 %collective-permute-start.10 = (bf16[128,512]{1,0:T(8,128)(2,1)S(1)}, bf16[128,512]{1,0:T(8,128)(2,1)S(1)}, u32[]{:S(2)}, u32[]{:S(2)}) collective-permute-start(bf16[128,512]{1,0:T(8,128)(2,1)S(1)} %get-tuple-element.32), channel_id=1, source_target_pairs={{0,3},{1,2},{2,1},{3,0},{4,7},{5,6},{6,5},{7,4},{8,11},{9,10},{10,... | collective-permute-start | bytes 393224 | tf_op jit(solution)/shard_map/ppermute | solution.py:33
  30.2 3.5 %collective-permute-done.10.refs_0_ = bf16[128,512]{1,0:T(8,128)(2,1)S(1)} collective-permute-done((bf16[128,512]{1,0:T(8,128)(2,1)S(1)}, bf16[128,512]{1,0:T(8,128)(2,1)S(1)}, u32[]{:S(2)}, u32[]{:S(2)}) %collective-permute-start.10) | collective-permute-done | bytes 131104 | tf_op jit(solution)/shard_map/ppermute | solution.py:33
  33.7 2.5 %collective-permute-done.11.refs_1_ = bf16[128,512]{1,0:T(8,128)(2,1)S(1)} collective-permute-done((bf16[128,512]{1,0:T(8,128)(2,1)S(1)}, bf16[128,512]{1,0:T(8,128)(2,1)S(1)}, u32[]{:S(2)}, u32[]{:S(2)}) %collective-permute-start.11) | collective-permute-done | bytes 131104 | tf_op jit(solution)/shard_map/ppermute | solution.py:33
  36.8 1.6 %collective-permute-start.13 = (bf16[128,512]{1,0:T(8,128)(2,1)S(1)}, bf16[128,512]{1,0:T(8,128)(2,1)S(1)}, u32[]{:S(2)}, u32[]{:S(2)}) collective-permute-start(bf16[128,512]{1,0:T(8,128)(2,1)S(1)} %get-tuple-element.36.refs_2_), channel_id=1, source_target_pairs={{0,1},{1,0},{2,3},{3,2},{4,5},{5,4},{6,7},{7,6},{8,9},{9,8},{10,11... | collective-permute-start | bytes 393224 | tf_op jit(solution)/shard_map/ppermute | solution.py:33
  39.1 1.2 %collective-permute-start.15 = (bf16[128,512]{1,0:T(8,128)(2,1)S(1)}, bf16[128,512]{1,0:T(8,128)(2,1)S(1)}, u32[]{:S(2)}, u32[]{:S(2)}) collective-permute-start(bf16[128,512]{1,0:T(8,128)(2,1)S(1)} %get-tuple-element.36.refs_2_), channel_id=1, source_target_pairs={{0,3},{1,2},{2,1},{3,0},{4,7},{5,6},{6,5},{7,4},{8,11},{9,10},{10,... | collective-permute-start | bytes 393224 | tf_op jit(solution)/shard_map/ppermute | solution.py:33
  40.4 2.4 %collective-permute-done.13.refs_3_ = bf16[128,512]{1,0:T(8,128)(2,1)S(1)} collective-permute-done((bf16[128,512]{1,0:T(8,128)(2,1)S(1)}, bf16[128,512]{1,0:T(8,128)(2,1)S(1)}, u32[]{:S(2)}, u32[]{:S(2)}) %collective-permute-start.13) | collective-permute-done | bytes 131104 | tf_op jit(solution)/shard_map/ppermute | solution.py:33
  42.7 3.4 %collective-permute-done.14.refs_4_ = bf16[128,512]{1,0:T(8,128)(2,1)S(1)} collective-permute-done((bf16[128,512]{1,0:T(8,128)(2,1)S(1)}, bf16[128,512]{1,0:T(8,128)(2,1)S(1)}, u32[]{:S(2)}, u32[]{:S(2)}) %collective-permute-start.14) | collective-permute-done | bytes 131104 | tf_op jit(solution)/shard_map/ppermute | solution.py:33
  48.2 1.0 %collective-permute-start.22 = (bf16[256,512]{1,0:T(8,128)(2,1)S(1)}, bf16[256,512]{1,0:T(8,128)(2,1)S(1)}, u32[]{:S(2)}, u32[]{:S(2)}) collective-permute-start(bf16[256,512]{1,0:T(8,128)(2,1)S(1)} %shard_map.100.refs_10_), channel_id=1, source_target_pairs={{24,16},{28,20},{0,8},{4,12},{16,24},{20,28},{8,0},{12,4},{25,17},... | collective-permute-start | bytes 786440 | tf_op jit(solution)/shard_map/ppermute | solution.py:29
  50.0 1.1 %shard_map.102 = (bf16[256,512]{1,0:T(8,128)(2,1)S(1)}, f32[128,512]{1,0:T(8,128)}) custom-call(bf16[1024,512]{1,0:T(8,128)(2,1)S(1)} %get-tuple-element.22.refs_0_, bf16[1024,512]{1,0:T(8,128)(2,1)S(1)} %collective-permute-done.9.refs_1_, bf16[128,512]{1,0:T(8,128)(2,1)S(1)} %get-tuple-element.36.refs_2_, ...), custom_call_target="tpu_custom_call" | custom-call | flops 268435456 | bytes 2097152 | tf_op jit(solution)/shard_map/pallas_call | solution.py:49
  51.1 2.5 %collective-permute-start.21 = (bf16[256,512]{1,0:T(8,128)(2,1)S(1)}, bf16[256,512]{1,0:T(8,128)(2,1)S(1)}, u32[]{:S(2)}, u32[]{:S(2)}) collective-permute-start(bf16[256,512]{1,0:T(8,128)(2,1)S(1)} %get-tuple-element.40), channel_id=1, source_target_pairs={{8,0},{12,4},{16,24},{20,28},{24,8},{28,12},{0,16},{4,20},{9,1},{1... | collective-permute-start | bytes 786440 | tf_op jit(solution)/shard_map/ppermute | solution.py:29
  53.5 3.8 %collective-permute-done.22.handed = bf16[256,512]{1,0:T(8,128)(2,1)S(1)} collective-permute-done((bf16[256,512]{1,0:T(8,128)(2,1)S(1)}, bf16[256,512]{1,0:T(8,128)(2,1)S(1)}, u32[]{:S(2)}, u32[]{:S(2)}) %collective-permute-start.22) | collective-permute-done | bytes 262176 | tf_op jit(solution)/shard_map/ppermute | solution.py:29
  57.4 1.0 %collective-permute-start.23 = (bf16[256,512]{1,0:T(8,128)(2,1)S(1)}, bf16[256,512]{1,0:T(8,128)(2,1)S(1)}, u32[]{:S(2)}, u32[]{:S(2)}) collective-permute-start(bf16[256,512]{1,0:T(8,128)(2,1)S(1)} %shard_map.103), channel_id=1, source_target_pairs={{16,0},{20,4},{8,24},{12,28},{0,8},{4,12},{24,16},{28,20},{17,1},{... | collective-permute-start | bytes 786440 | tf_op jit(solution)/shard_map/ppermute | solution.py:29
  58.5 4.0 %collective-permute-done.21.near = bf16[256,512]{1,0:T(8,128)(2,1)S(1)} collective-permute-done((bf16[256,512]{1,0:T(8,128)(2,1)S(1)}, bf16[256,512]{1,0:T(8,128)(2,1)S(1)}, u32[]{:S(2)}, u32[]{:S(2)}) %collective-permute-start.21) | collective-permute-done | bytes 262176 | tf_op jit(solution)/shard_map/ppermute | solution.py:29
  62.5 7.0 %collective-permute-done.23.onward = bf16[256,512]{1,0:T(8,128)(2,1)S(1)} collective-permute-done((bf16[256,512]{1,0:T(8,128)(2,1)S(1)}, bf16[256,512]{1,0:T(8,128)(2,1)S(1)}, u32[]{:S(2)}, u32[]{:S(2)}) %collective-permute-start.23) | collective-permute-done | bytes 262176 | tf_op jit(solution)/shard_map/ppermute | solution.py:29
  69.5 1.7 %shard_map.104 = f32[256,512]{1,0:T(8,128)} custom-call(f32[256,512]{1,0:T(8,128)S(1)} %copy-done, bf16[1024,512]{1,0:T(8,128)(2,1)S(1)} %get-tuple-element.24.w_hi, bf16[1024,512]{1,0:T(8,128)(2,1)S(1)} %get-tuple-element.31.w_lo, bf16[256,512]{1,0:T(8,128)(2,1)S(1)} %collective-permute-done.20.middle, f32[256,512]{1,0:T(8,128)S(1)} %get-tuple-element.37.refs_10_.own, ...), custom_call_target="tpu_custom_call" | custom-call | flops 805306368 | bytes 4194304 | tf_op jit(solution)/shard_map/pallas_call | solution.py:278
  (49 shorter events, 10.1 us)
Async XLA Ops:
  1.7 10.8 %collective-permute-start.1 = (bf16[256,512]{1,0:T(8,128)(2,1)S(1)}, bf16[256,512]{1,0:T(8,128)(2,1)S(1)}, u32[]{:S(2)}, u32[]{:S(2)}) collective-permute-start(bf16[256,512]{1,0:T(8,128)(2,1)S(1)} %convert_element_type.3.refs_0_), channel_id=1, source_target_pairs={{0,16},{4,20},{24,8},{28,12},{8,0},{12,4},{16,24},{20,28},{1,17},{... | collective-permute-start | bytes 786440 | tf_op jit(solution)/shard_map/ppermute | solution.py:29
  10.0 10.2 %collective-permute-start.3 = (bf16[256,512]{1,0:T(8,128)(2,1)S(1)}, bf16[256,512]{1,0:T(8,128)(2,1)S(1)}, u32[]{:S(2)}, u32[]{:S(2)}) collective-permute-start(bf16[256,512]{1,0:T(8,128)(2,1)S(1)} %convert_element_type.3.refs_0_), channel_id=1, source_target_pairs={{0,8},{4,12},{24,16},{28,20},{8,24},{12,28},{16,0},{20,4},{1,9},{5... | collective-permute-start | bytes 786440 | tf_op jit(solution)/shard_map/ppermute | solution.py:29
  12.2 8.1 %collective-permute-start.5 = (bf16[256,512]{1,0:T(8,128)(2,1)S(1)}, bf16[256,512]{1,0:T(8,128)(2,1)S(1)}, u32[]{:S(2)}, u32[]{:S(2)}) collective-permute-start(bf16[256,512]{1,0:T(8,128)(2,1)S(1)} %convert_element_type.3.refs_0_), channel_id=1, source_target_pairs={{8,16},{12,20},{16,8},{20,12},{0,4},{4,0},{24,28},{28,24},{9,17},{... | collective-permute-start | bytes 786440 | tf_op jit(solution)/shard_map/ppermute | solution.py:29
  12.5 12.0 %collective-permute-start.6 = (bf16[256,512]{1,0:T(8,128)(2,1)S(1)}, bf16[256,512]{1,0:T(8,128)(2,1)S(1)}, u32[]{:S(2)}, u32[]{:S(2)}) collective-permute-start(bf16[256,512]{1,0:T(8,128)(2,1)S(1)} %collective-permute-done.1.refs_2_), channel_id=1, source_target_pairs={{16,24},{20,28},{8,0},{12,4},{24,16},{28,20},{0,8},{4,12},{17,25},... | collective-permute-start | bytes 786440 | tf_op jit(solution)/shard_map/ppermute | solution.py:29
  14.8 9.7 %collective-permute-start = (bf16[256,512]{1,0:T(8,128)(2,1)S(1)}, bf16[256,512]{1,0:T(8,128)(2,1)S(1)}, u32[]{:S(2)}, u32[]{:S(2)}) collective-permute-start(bf16[256,512]{1,0:T(8,128)(2,1)S(1)} %convert_element_type.3.refs_0_), channel_id=1, source_target_pairs={{0,4},{4,0},{8,12},{12,8},{16,20},{20,16},{24,28},{28,24},{1,5},{5... | collective-permute-start | bytes 786440 | tf_op jit(solution)/shard_map/ppermute | solution.py:33
  14.8 9.7 %collective-permute-start.2 = (bf16[256,512]{1,0:T(8,128)(2,1)S(1)}, bf16[256,512]{1,0:T(8,128)(2,1)S(1)}, u32[]{:S(2)}, u32[]{:S(2)}) collective-permute-start(bf16[256,512]{1,0:T(8,128)(2,1)S(1)} %collective-permute-done.1.refs_2_), channel_id=1, source_target_pairs={{0,4},{4,0},{8,12},{12,8},{16,20},{20,16},{24,28},{28,24},{1,5},{5... | collective-permute-start | bytes 786440 | tf_op jit(solution)/shard_map/ppermute | solution.py:33
  20.2 4.3 %collective-permute-start.4 = (bf16[256,512]{1,0:T(8,128)(2,1)S(1)}, bf16[256,512]{1,0:T(8,128)(2,1)S(1)}, u32[]{:S(2)}, u32[]{:S(2)}) collective-permute-start(bf16[256,512]{1,0:T(8,128)(2,1)S(1)} %collective-permute-done.3.refs_4_), channel_id=1, source_target_pairs={{0,4},{4,0},{8,12},{12,8},{16,20},{20,16},{24,28},{28,24},{1,5},{5... | collective-permute-start | bytes 786440 | tf_op jit(solution)/shard_map/ppermute | solution.py:33
  20.2 5.3 %collective-permute-start.7 = (bf16[256,512]{1,0:T(8,128)(2,1)S(1)}, bf16[256,512]{1,0:T(8,128)(2,1)S(1)}, u32[]{:S(2)}, u32[]{:S(2)}) collective-permute-start(bf16[256,512]{1,0:T(8,128)(2,1)S(1)} %collective-permute-done.5.middle), channel_id=1, source_target_pairs={{0,4},{4,0},{8,12},{12,8},{16,20},{20,16},{24,28},{28,24},{1,5},{5... | collective-permute-start | bytes 786440 | tf_op jit(solution)/shard_map/ppermute | solution.py:33
  24.5 1.5 %collective-permute-start.8 = (bf16[256,512]{1,0:T(8,128)(2,1)S(1)}, bf16[256,512]{1,0:T(8,128)(2,1)S(1)}, u32[]{:S(2)}, u32[]{:S(2)}) collective-permute-start(bf16[256,512]{1,0:T(8,128)(2,1)S(1)} %collective-permute-done.6.ends), channel_id=1, source_target_pairs={{0,4},{4,0},{8,12},{12,8},{16,20},{20,16},{24,28},{28,24},{1,5},{5... | collective-permute-start | bytes 786440 | tf_op jit(solution)/shard_map/ppermute | solution.py:33
  26.5 3.7 %collective-permute-start.9 = (bf16[1024,512]{1,0:T(8,128)(2,1)S(1)}, bf16[1024,512]{1,0:T(8,128)(2,1)S(1)}, u32[]{:S(2)}, u32[]{:S(2)}) collective-permute-start(bf16[1024,512]{1,0:T(8,128)(2,1)S(1)} %get-tuple-element.29), channel_id=1, source_target_pairs={{0,4},{4,0},{8,12},{12,8},{16,20},{20,16},{24,28},{28,24},{1,5},{5... | collective-permute-start | bytes 3145736 | tf_op jit(solution)/shard_map/ppermute | solution.py:33
  26.7 7.0 %collective-permute-start.10 = (bf16[128,512]{1,0:T(8,128)(2,1)S(1)}, bf16[128,512]{1,0:T(8,128)(2,1)S(1)}, u32[]{:S(2)}, u32[]{:S(2)}) collective-permute-start(bf16[128,512]{1,0:T(8,128)(2,1)S(1)} %get-tuple-element.32), channel_id=1, source_target_pairs={{0,3},{1,2},{2,1},{3,0},{4,7},{5,6},{6,5},{7,4},{8,11},{9,10},{10,... | collective-permute-start | bytes 393224 | tf_op jit(solution)/shard_map/ppermute | solution.py:33
  29.1 7.1 %collective-permute-start.11 = (bf16[128,512]{1,0:T(8,128)(2,1)S(1)}, bf16[128,512]{1,0:T(8,128)(2,1)S(1)}, u32[]{:S(2)}, u32[]{:S(2)}) collective-permute-start(bf16[128,512]{1,0:T(8,128)(2,1)S(1)} %get-tuple-element.33), channel_id=1, source_target_pairs={{0,2},{1,3},{2,0},{3,1},{4,6},{5,7},{6,4},{7,5},{8,10},{9,11},{10,... | collective-permute-start | bytes 393224 | tf_op jit(solution)/shard_map/ppermute | solution.py:33
  29.6 6.7 %collective-permute-start.12 = (bf16[128,512]{1,0:T(8,128)(2,1)S(1)}, bf16[128,512]{1,0:T(8,128)(2,1)S(1)}, u32[]{:S(2)}, u32[]{:S(2)}) collective-permute-start(bf16[128,512]{1,0:T(8,128)(2,1)S(1)} %get-tuple-element.34), channel_id=1, source_target_pairs={{0,1},{1,0},{2,3},{3,2},{4,5},{5,4},{6,7},{7,6},{8,9},{9,8},{10,11... | collective-permute-start | bytes 393224 | tf_op jit(solution)/shard_map/ppermute | solution.py:33
  36.8 5.9 %collective-permute-start.13 = (bf16[128,512]{1,0:T(8,128)(2,1)S(1)}, bf16[128,512]{1,0:T(8,128)(2,1)S(1)}, u32[]{:S(2)}, u32[]{:S(2)}) collective-permute-start(bf16[128,512]{1,0:T(8,128)(2,1)S(1)} %get-tuple-element.36.refs_2_), channel_id=1, source_target_pairs={{0,1},{1,0},{2,3},{3,2},{4,5},{5,4},{6,7},{7,6},{8,9},{9,8},{10,11... | collective-permute-start | bytes 393224 | tf_op jit(solution)/shard_map/ppermute | solution.py:33
  38.4 7.8 %collective-permute-start.14 = (bf16[128,512]{1,0:T(8,128)(2,1)S(1)}, bf16[128,512]{1,0:T(8,128)(2,1)S(1)}, u32[]{:S(2)}, u32[]{:S(2)}) collective-permute-start(bf16[128,512]{1,0:T(8,128)(2,1)S(1)} %get-tuple-element.36.refs_2_), channel_id=1, source_target_pairs={{0,2},{1,3},{2,0},{3,1},{4,6},{5,7},{6,4},{7,5},{8,10},{9,11},{10,... | collective-permute-start | bytes 393224 | tf_op jit(solution)/shard_map/ppermute | solution.py:33
  39.1 7.0 %collective-permute-start.15 = (bf16[128,512]{1,0:T(8,128)(2,1)S(1)}, bf16[128,512]{1,0:T(8,128)(2,1)S(1)}, u32[]{:S(2)}, u32[]{:S(2)}) collective-permute-start(bf16[128,512]{1,0:T(8,128)(2,1)S(1)} %get-tuple-element.36.refs_2_), channel_id=1, source_target_pairs={{0,3},{1,2},{2,1},{3,0},{4,7},{5,6},{6,5},{7,4},{8,11},{9,10},{10,... | collective-permute-start | bytes 393224 | tf_op jit(solution)/shard_map/ppermute | solution.py:33
  40.4 6.3 %collective-permute-start.16 = (bf16[128,512]{1,0:T(8,128)(2,1)S(1)}, bf16[128,512]{1,0:T(8,128)(2,1)S(1)}, u32[]{:S(2)}, u32[]{:S(2)}) collective-permute-start(bf16[128,512]{1,0:T(8,128)(2,1)S(1)} %get-tuple-element.36.refs_2_), channel_id=1, source_target_pairs={{0,4},{4,0},{8,12},{12,8},{16,20},{20,16},{24,28},{28,24},{1,5},{5... | collective-permute-start | bytes 393224 | tf_op jit(solution)/shard_map/ppermute | solution.py:33
  42.7 4.0 %collective-permute-start.17 = (bf16[128,512]{1,0:T(8,128)(2,1)S(1)}, bf16[128,512]{1,0:T(8,128)(2,1)S(1)}, u32[]{:S(2)}, u32[]{:S(2)}) collective-permute-start(bf16[128,512]{1,0:T(8,128)(2,1)S(1)} %collective-permute-done.13.refs_3_), channel_id=1, source_target_pairs={{0,4},{4,0},{8,12},{12,8},{16,20},{20,16},{24,28},{28,24},{1,5},{5... | collective-permute-start | bytes 393224 | tf_op jit(solution)/shard_map/ppermute | solution.py:33
  46.2 1.3 %collective-permute-start.18 = (bf16[128,512]{1,0:T(8,128)(2,1)S(1)}, bf16[128,512]{1,0:T(8,128)(2,1)S(1)}, u32[]{:S(2)}, u32[]{:S(2)}) collective-permute-start(bf16[128,512]{1,0:T(8,128)(2,1)S(1)} %collective-permute-done.14.refs_4_), channel_id=1, source_target_pairs={{0,4},{4,0},{8,12},{12,8},{16,20},{20,16},{24,28},{28,24},{1,5},{5... | collective-permute-start | bytes 393224 | tf_op jit(solution)/shard_map/ppermute | solution.py:33
  46.2 1.5 %collective-permute-start.19 = (bf16[128,512]{1,0:T(8,128)(2,1)S(1)}, bf16[128,512]{1,0:T(8,128)(2,1)S(1)}, u32[]{:S(2)}, u32[]{:S(2)}) collective-permute-start(bf16[128,512]{1,0:T(8,128)(2,1)S(1)} %collective-permute-done.15.refs_5_), channel_id=1, source_target_pairs={{0,4},{4,0},{8,12},{12,8},{16,20},{20,16},{24,28},{28,24},{1,5},{5... | collective-permute-start | bytes 393224 | tf_op jit(solution)/shard_map/ppermute | solution.py:33
  48.2 9.2 %collective-permute-start.22 = (bf16[256,512]{1,0:T(8,128)(2,1)S(1)}, bf16[256,512]{1,0:T(8,128)(2,1)S(1)}, u32[]{:S(2)}, u32[]{:S(2)}) collective-permute-start(bf16[256,512]{1,0:T(8,128)(2,1)S(1)} %shard_map.100.refs_10_), channel_id=1, source_target_pairs={{24,16},{28,20},{0,8},{4,12},{16,24},{20,28},{8,0},{12,4},{25,17},... | collective-permute-start | bytes 786440 | tf_op jit(solution)/shard_map/ppermute | solution.py:29
  49.2 13.3 %collective-permute-start.20 = (bf16[256,512]{1,0:T(8,128)(2,1)S(1)}, bf16[256,512]{1,0:T(8,128)(2,1)S(1)}, u32[]{:S(2)}, u32[]{:S(2)}) collective-permute-start(bf16[256,512]{1,0:T(8,128)(2,1)S(1)} %shard_map.100.refs_10_), channel_id=1, source_target_pairs={{16,8},{20,12},{8,16},{12,20},{0,4},{4,0},{24,28},{28,24},{17,9},{... | collective-permute-start | bytes 786440 | tf_op jit(solution)/shard_map/ppermute | solution.py:29
  51.1 11.4 %collective-permute-start.21 = (bf16[256,512]{1,0:T(8,128)(2,1)S(1)}, bf16[256,512]{1,0:T(8,128)(2,1)S(1)}, u32[]{:S(2)}, u32[]{:S(2)}) collective-permute-start(bf16[256,512]{1,0:T(8,128)(2,1)S(1)} %get-tuple-element.40), channel_id=1, source_target_pairs={{8,0},{12,4},{16,24},{20,28},{24,8},{28,12},{0,16},{4,20},{9,1},{1... | collective-permute-start | bytes 786440 | tf_op jit(solution)/shard_map/ppermute | solution.py:29
  57.4 12.1 %collective-permute-start.23 = (bf16[256,512]{1,0:T(8,128)(2,1)S(1)}, bf16[256,512]{1,0:T(8,128)(2,1)S(1)}, u32[]{:S(2)}, u32[]{:S(2)}) collective-permute-start(bf16[256,512]{1,0:T(8,128)(2,1)S(1)} %shard_map.103), channel_id=1, source_target_pairs={{16,0},{20,4},{8,24},{12,28},{0,8},{4,12},{24,16},{28,20},{17,1},{... | collective-permute-start | bytes 786440 | tf_op jit(solution)/shard_map/ppermute | solution.py:29
  (7 other events, 26.9 us)

commit v6 on v5

--- a/solution.py
+++ b/solution.py
@@ -122,14 +122,13 @@
 
 
 def early_sums(adj, *refs):
-    *blocks, sums = refs
-    sums[...] = block_sums(adj, 0, [block[...] for block in blocks])
-
-
-def late_sums(adj, early, middle, ends, middle_other, ends_other, *outs):
-    inner = in_middle()
-    blocks = [jnp.where(inner, a[...], b[...]) for a, b in ((middle, ends), (middle_other, ends_other))]
-    sums = early[...] + block_sums(adj, 6, blocks)
+    *blocks, middle, ends, sums = refs
+    blocks = [block[...] for block in blocks] + [jnp.where(in_middle(), middle[...], ends[...])]
+    sums[...] = block_sums(adj, 0, blocks)
+
+
+def late_sums(adj, early, middle, ends, *outs):
+    sums = early[...] + block_sums(adj, 7, [jnp.where(in_middle(), middle[...], ends[...])])
     height = outs[0].shape[0]
     for k, out in enumerate(outs):
         out[...] = sums[k * height : (k + 1) * height].astype(out.dtype)
@@ -227,14 +226,14 @@
     (early,) = call(
         early_sums,
         (shape(users, depth, dtype=F32),),
-        (adj, mine, other(mine), first, other(first), second, other(second)),
+        (adj, mine, other(mine), first, other(first), second, other(second), middle, ends),
         flops=work // 2,
         nbytes=4 << 20,
     )
     own, *others = call(
         late_sums,
         (shape(share, depth, dtype=F32),) + (shape(share, depth),) * 3,
-        (adj, early, middle, ends, other(middle), other(ends)),
+        (adj, early, other(middle), other(ends)),
         flops=work // 2,
         nbytes=4 << 20,
     )
@@ -243,12 +242,13 @@
     new_users, user_half = call(
         functools.partial(update, 4),
         (shape(share, depth, dtype=F32), shape(share, depth)),
-        (own_emb, w_hi, w_lo, *(swap(others[k - 1], "ia", 4, k) for k in (3, 2, 1)), own),
+        (own_emb, w_hi, w_lo, *(swap(others[k - 1], "ia", 4, k) for k in (1, 2, 3)), own),
         flops=12 * share * depth * depth,
         nbytes=3 << 20,
     )
 
     shares = [user_half] + [swap(user_half, "ia", 4, k) for k in (1, 2, 3)]
+    shares[1:3] = lax.optimization_barrier(tuple(shares[1:3]))
     shares += [other(x) for x in shares]
     (far,) = call(
         functools.partial(item_sums, (3,), 4),

time: 71.4 us -> 71 us (level)
  transfers between devices with their start and end apart: 24 -> 24, of which waited for: 13 -> 14; matrix products, arithmetic and copies ran while one was open for 0% -> 0% of each run, Pallas kernels for 7% -> 7%
where the time goes in v6:
time: 71 us; the launch traced here: 70.8 us
  waiting for transfers between devices  36.6 us (52%)
  starting transfers between devices  20 us (28%)
  Pallas kernels  8.08 us (11%)
  local copies, waits for them, and re-layouts  3.57 us (5%)
  between operations  1.41 us (2%)
  other arithmetic  1.08 us (2%)
    ppermute x8, waiting for transfers between devices, send(): return lax.ppermute(x, 'au', perm)  23.4 us
    ppermute x16, waiting for transfers between devices, swap(): return lax.ppermute(x, axis, [(i, i ^ by) for i in range(n)])  13.2 us
    ppermute x8, starting transfers between devices, send(): return lax.ppermute(x, 'au', perm)  11.2 us
    ppermute x16, starting transfers between devices, swap(): return lax.ppermute(x, axis, [(i, i ^ by) for i in range(n)])  8.81 us
    pallas_call x9, Pallas kernels, call(): pl.pallas_call(kernel, out_shape=out_shape, in_specs=[SMEM] * smem + [VME...  6.36 us
    unnamed x14, local copies, waits for them, and re-layouts  3.57 us
    pallas_call x1, Pallas kernels, in_turns(): pl.pallas_call(last_update, out_shape=shape(held, depth, dtype=F32), in_s...  1.72 us
  transfers between devices with their start and end apart: 24, of which 14 were waited for; matrix products, arithmetic and copies ran while one was open for 0% of the time, Pallas kernels for 7%

profile of v6, /device:TPU:0, one launch (start us, length us, event | category | flops | bytes accessed | tf_op | source)
XLA Modules:
  0.0 70.8 jit_solution(15924294422570478063)
XLA Ops:
  0.6 1.1 %convert_element_type.3.refs_0_ = bf16[256,512]{1,0:T(8,128)(2,1)S(1)} convert(f32[256,512]{1,0:T(8,128)} %emb.1) | non-fusion elementwise | flops 131072 | bytes 786432 | tf_op jit(solution)/shard_map/convert_element_type | solution.py:206
  1.7 4.1 %collective-permute-start.1 = (bf16[256,512]{1,0:T(8,128)(2,1)S(1)}, bf16[256,512]{1,0:T(8,128)(2,1)S(1)}, u32[]{:S(2)}, u32[]{:S(2)}) collective-permute-start(bf16[256,512]{1,0:T(8,128)(2,1)S(1)} %convert_element_type.3.refs_0_), channel_id=1, source_target_pairs={{0,16},{4,20},{24,8},{28,12},{8,0},{12,4},{16,24},{20,28},{1,17},{... | collective-permute-start | bytes 786440 | tf_op jit(solution)/shard_map/ppermute | solution.py:29
  6.5 1.4 %copy-done.1 = bf16[1,12,256,256]{3,2,1,0:T(8,128)(2,1)S(1)} copy-done((bf16[1,12,256,256]{3,2,1,0:T(8,128)(2,1)S(1)}, bf16[1,12,256,256]{3,2,1,0:T(8,128)(2,1)}, u32[]{:S(2)}) %copy-start.1) | copy-done | bytes 1572888
  11.0 1.2 %shard_map.96 = (bf16[1024,512]{1,0:T(8,128)(2,1)S(1)}, bf16[1024,512]{1,0:T(8,128)(2,1)S(1)}, f32[128,512]{1,0:T(8,128)S(1)}, bf16[1024,512]{1,0:T(8,128)(2,1)S(1)}, bf16[1024,512]{1,0:T(8,128)(2,1)S(1)}) custom-call(bf16[512,2048]{1,0:T(8,128)(2,1)S(1)} %shard_map.95.adj, f32[512,512]{1,0:T(8,128)S(1)} %copy-done.2, f32[512,512]{1,0:T(8,128)S(1)} %copy-done.3, ...), custom_call_target="tpu_custom_call" | custom-call | bytes 9437184 | tf_op jit(solution)/shard_map/pallas_call | solution.py:49
  12.5 2.4 %collective-permute-start.6 = (bf16[256,512]{1,0:T(8,128)(2,1)S(1)}, bf16[256,512]{1,0:T(8,128)(2,1)S(1)}, u32[]{:S(2)}, u32[]{:S(2)}) collective-permute-start(bf16[256,512]{1,0:T(8,128)(2,1)S(1)} %collective-permute-done.1.refs_2_), channel_id=1, source_target_pairs={{16,24},{20,28},{8,0},{12,4},{24,16},{28,20},{0,8},{4,12},{17,25},... | collective-permute-start | bytes 786440 | tf_op jit(solution)/shard_map/ppermute | solution.py:29
  15.4 4.9 %collective-permute-done.3.refs_4_ = bf16[256,512]{1,0:T(8,128)(2,1)S(1)} collective-permute-done((bf16[256,512]{1,0:T(8,128)(2,1)S(1)}, bf16[256,512]{1,0:T(8,128)(2,1)S(1)}, u32[]{:S(2)}, u32[]{:S(2)}) %collective-permute-start.3) | collective-permute-done | bytes 262176 | tf_op jit(solution)/shard_map/ppermute | solution.py:29
  20.8 3.7 %collective-permute-done.6.refs_7_ = bf16[256,512]{1,0:T(8,128)(2,1)S(1)} collective-permute-done((bf16[256,512]{1,0:T(8,128)(2,1)S(1)}, bf16[256,512]{1,0:T(8,128)(2,1)S(1)}, u32[]{:S(2)}, u32[]{:S(2)}) %collective-permute-start.6) | collective-permute-done | bytes 262176 | tf_op jit(solution)/shard_map/ppermute | solution.py:29
  24.6 1.1 %shard_map.97.early = f32[512,512]{1,0:T(8,128)S(1)} custom-call(bf16[512,2048]{1,0:T(8,128)(2,1)S(1)} %shard_map.95.adj, bf16[256,512]{1,0:T(8,128)(2,1)S(1)} %convert_element_type.3.refs_0_, bf16[256,512]{1,0:T(8,128)(2,1)S(1)} %collective-permute-done.refs_1_, bf16[256,512]{1,0:T(8,128)(2,1)S(1)} %collective-permute-done.1.refs_2_, ...), custom_call_target="tpu_custom_call" | custom-call | flops 536870912 | bytes 4194304 | tf_op jit(solution)/shard_map/pallas_call | solution.py:49
  26.6 1.4 %collective-permute-start.10 = (bf16[128,512]{1,0:T(8,128)(2,1)S(1)}, bf16[128,512]{1,0:T(8,128)(2,1)S(1)}, u32[]{:S(2)}, u32[]{:S(2)}) collective-permute-start(bf16[128,512]{1,0:T(8,128)(2,1)S(1)} %get-tuple-element.34), channel_id=1, source_target_pairs={{0,1},{1,0},{2,3},{3,2},{4,5},{5,4},{6,7},{7,6},{8,9},{9,8},{10,11... | collective-permute-start | bytes 393224 | tf_op jit(solution)/shard_map/ppermute | solution.py:33
  28.0 1.6 %collective-permute-start.11 = (bf16[128,512]{1,0:T(8,128)(2,1)S(1)}, bf16[128,512]{1,0:T(8,128)(2,1)S(1)}, u32[]{:S(2)}, u32[]{:S(2)}) collective-permute-start(bf16[128,512]{1,0:T(8,128)(2,1)S(1)} %get-tuple-element.35), channel_id=1, source_target_pairs={{0,2},{1,3},{2,0},{3,1},{4,6},{5,7},{6,4},{7,5},{8,10},{9,11},{10,... | collective-permute-start | bytes 393224 | tf_op jit(solution)/shard_map/ppermute | solution.py:33
  30.1 2.7 %collective-permute-done.10.refs_0_ = bf16[128,512]{1,0:T(8,128)(2,1)S(1)} collective-permute-done((bf16[128,512]{1,0:T(8,128)(2,1)S(1)}, bf16[128,512]{1,0:T(8,128)(2,1)S(1)}, u32[]{:S(2)}, u32[]{:S(2)}) %collective-permute-start.10) | collective-permute-done | bytes 131104 | tf_op jit(solution)/shard_map/ppermute | solution.py:33
  32.8 3.4 %collective-permute-done.11.refs_1_ = bf16[128,512]{1,0:T(8,128)(2,1)S(1)} collective-permute-done((bf16[128,512]{1,0:T(8,128)(2,1)S(1)}, bf16[128,512]{1,0:T(8,128)(2,1)S(1)}, u32[]{:S(2)}, u32[]{:S(2)}) %collective-permute-start.11) | collective-permute-done | bytes 131104 | tf_op jit(solution)/shard_map/ppermute | solution.py:33
  36.8 1.4 %collective-permute-start.13 = (bf16[128,512]{1,0:T(8,128)(2,1)S(1)}, bf16[128,512]{1,0:T(8,128)(2,1)S(1)}, u32[]{:S(2)}, u32[]{:S(2)}) collective-permute-start(bf16[128,512]{1,0:T(8,128)(2,1)S(1)} %get-tuple-element.38.refs_2_), channel_id=1, source_target_pairs={{0,1},{1,0},{2,3},{3,2},{4,5},{5,4},{6,7},{7,6},{8,9},{9,8},{10,11... | collective-permute-start | bytes 393224 | tf_op jit(solution)/shard_map/ppermute | solution.py:33
  39.0 1.4 %collective-permute-start.15 = (bf16[128,512]{1,0:T(8,128)(2,1)S(1)}, bf16[128,512]{1,0:T(8,128)(2,1)S(1)}, u32[]{:S(2)}, u32[]{:S(2)}) collective-permute-start(bf16[128,512]{1,0:T(8,128)(2,1)S(1)} %get-tuple-element.38.refs_2_), channel_id=1, source_target_pairs={{0,3},{1,2},{2,1},{3,0},{4,7},{5,6},{6,5},{7,4},{8,11},{9,10},{10,... | collective-permute-start | bytes 393224 | tf_op jit(solution)/shard_map/ppermute | solution.py:33
  40.4 2.1 %collective-permute-done.13.refs_3_ = bf16[128,512]{1,0:T(8,128)(2,1)S(1)} collective-permute-done((bf16[128,512]{1,0:T(8,128)(2,1)S(1)}, bf16[128,512]{1,0:T(8,128)(2,1)S(1)}, u32[]{:S(2)}, u32[]{:S(2)}) %collective-permute-start.13) | collective-permute-done | bytes 131104 | tf_op jit(solution)/shard_map/ppermute | solution.py:33
  42.5 3.2 %collective-permute-done.14.refs_4_ = bf16[128,512]{1,0:T(8,128)(2,1)S(1)} collective-permute-done((bf16[128,512]{1,0:T(8,128)(2,1)S(1)}, bf16[128,512]{1,0:T(8,128)(2,1)S(1)}, u32[]{:S(2)}, u32[]{:S(2)}) %collective-permute-start.14) | collective-permute-done | bytes 131104 | tf_op jit(solution)/shard_map/ppermute | solution.py:33
  48.0 1.1 %collective-permute-start.22 = (bf16[256,512]{1,0:T(8,128)(2,1)S(1)}, bf16[256,512]{1,0:T(8,128)(2,1)S(1)}, u32[]{:S(2)}, u32[]{:S(2)}) collective-permute-start(bf16[256,512]{1,0:T(8,128)(2,1)S(1)} %shard_map.100.refs_10_), channel_id=1, source_target_pairs={{24,16},{28,20},{0,8},{4,12},{16,24},{20,28},{8,0},{12,4},{25,17},... | collective-permute-start | bytes 786440 | tf_op jit(solution)/shard_map/ppermute | solution.py:29
  49.8 1.1 %shard_map.102 = (bf16[256,512]{1,0:T(8,128)(2,1)S(1)}, f32[128,512]{1,0:T(8,128)}) custom-call(bf16[1024,512]{1,0:T(8,128)(2,1)S(1)} %get-tuple-element.24.refs_0_, bf16[1024,512]{1,0:T(8,128)(2,1)S(1)} %collective-permute-done.9.refs_1_, bf16[128,512]{1,0:T(8,128)(2,1)S(1)} %get-tuple-element.38.refs_2_, ...), custom_call_target="tpu_custom_call" | custom-call | flops 268435456 | bytes 2097152 | tf_op jit(solution)/shard_map/pallas_call | solution.py:49
  50.9 2.5 %collective-permute-start.21 = (bf16[256,512]{1,0:T(8,128)(2,1)S(1)}, bf16[256,512]{1,0:T(8,128)(2,1)S(1)}, u32[]{:S(2)}, u32[]{:S(2)}) collective-permute-start(bf16[256,512]{1,0:T(8,128)(2,1)S(1)} %get-tuple-element.44), channel_id=1, source_target_pairs={{8,0},{12,4},{16,24},{20,28},{24,8},{28,12},{0,16},{4,20},{9,1},{1... | collective-permute-start | bytes 786440 | tf_op jit(solution)/shard_map/ppermute | solution.py:29
  53.4 3.9 %collective-permute-done.22.handed = bf16[256,512]{1,0:T(8,128)(2,1)S(1)} collective-permute-done((bf16[256,512]{1,0:T(8,128)(2,1)S(1)}, bf16[256,512]{1,0:T(8,128)(2,1)S(1)}, u32[]{:S(2)}, u32[]{:S(2)}) %collective-permute-start.22) | collective-permute-done | bytes 262176 | tf_op jit(solution)/shard_map/ppermute | solution.py:29
  57.3 1.0 %collective-permute-start.23 = (bf16[256,512]{1,0:T(8,128)(2,1)S(1)}, bf16[256,512]{1,0:T(8,128)(2,1)S(1)}, u32[]{:S(2)}, u32[]{:S(2)}) collective-permute-start(bf16[256,512]{1,0:T(8,128)(2,1)S(1)} %shard_map.103), channel_id=1, source_target_pairs={{16,0},{20,4},{8,24},{12,28},{0,8},{4,12},{24,16},{28,20},{17,1},{... | collective-permute-start | bytes 786440 | tf_op jit(solution)/shard_map/ppermute | solution.py:29
  58.4 3.8 %collective-permute-done.21.near = bf16[256,512]{1,0:T(8,128)(2,1)S(1)} collective-permute-done((bf16[256,512]{1,0:T(8,128)(2,1)S(1)}, bf16[256,512]{1,0:T(8,128)(2,1)S(1)}, u32[]{:S(2)}, u32[]{:S(2)}) %collective-permute-start.21) | collective-permute-done | bytes 262176 | tf_op jit(solution)/shard_map/ppermute | solution.py:29
  62.2 6.9 %collective-permute-done.23.onward = bf16[256,512]{1,0:T(8,128)(2,1)S(1)} collective-permute-done((bf16[256,512]{1,0:T(8,128)(2,1)S(1)}, bf16[256,512]{1,0:T(8,128)(2,1)S(1)}, u32[]{:S(2)}, u32[]{:S(2)}) %collective-permute-start.23) | collective-permute-done | bytes 262176 | tf_op jit(solution)/shard_map/ppermute | solution.py:29
  69.1 1.7 %shard_map.104 = f32[256,512]{1,0:T(8,128)} custom-call(f32[256,512]{1,0:T(8,128)S(1)} %copy-done, bf16[1024,512]{1,0:T(8,128)(2,1)S(1)} %get-tuple-element.26.w_hi, bf16[1024,512]{1,0:T(8,128)(2,1)S(1)} %get-tuple-element.33.w_lo, bf16[256,512]{1,0:T(8,128)(2,1)S(1)} %collective-permute-done.20.middle, f32[256,512]{1,0:T(8,128)S(1)} %get-tuple-element.41.refs_10_.own, ...), custom_call_target="tpu_custom_call" | custom-call | flops 805306368 | bytes 4194304 | tf_op jit(solution)/shard_map/pallas_call | solution.py:278
  (49 shorter events, 10.3 us)
Async XLA Ops:
  1.7 10.8 %collective-permute-start.1 = (bf16[256,512]{1,0:T(8,128)(2,1)S(1)}, bf16[256,512]{1,0:T(8,128)(2,1)S(1)}, u32[]{:S(2)}, u32[]{:S(2)}) collective-permute-start(bf16[256,512]{1,0:T(8,128)(2,1)S(1)} %convert_element_type.3.refs_0_), channel_id=1, source_target_pairs={{0,16},{4,20},{24,8},{28,12},{8,0},{12,4},{16,24},{20,28},{1,17},{... | collective-permute-start | bytes 786440 | tf_op jit(solution)/shard_map/ppermute | solution.py:29
  10.1 10.2 %collective-permute-start.3 = (bf16[256,512]{1,0:T(8,128)(2,1)S(1)}, bf16[256,512]{1,0:T(8,128)(2,1)S(1)}, u32[]{:S(2)}, u32[]{:S(2)}) collective-permute-start(bf16[256,512]{1,0:T(8,128)(2,1)S(1)} %convert_element_type.3.refs_0_), channel_id=1, source_target_pairs={{0,8},{4,12},{24,16},{28,20},{8,24},{12,28},{16,0},{20,4},{1,9},{5... | collective-permute-start | bytes 786440 | tf_op jit(solution)/shard_map/ppermute | solution.py:29
  12.2 8.1 %collective-permute-start.5 = (bf16[256,512]{1,0:T(8,128)(2,1)S(1)}, bf16[256,512]{1,0:T(8,128)(2,1)S(1)}, u32[]{:S(2)}, u32[]{:S(2)}) collective-permute-start(bf16[256,512]{1,0:T(8,128)(2,1)S(1)} %convert_element_type.3.refs_0_), channel_id=1, source_target_pairs={{8,16},{12,20},{16,8},{20,12},{0,4},{4,0},{24,28},{28,24},{9,17},{... | collective-permute-start | bytes 786440 | tf_op jit(solution)/shard_map/ppermute | solution.py:29
  12.5 12.0 %collective-permute-start.6 = (bf16[256,512]{1,0:T(8,128)(2,1)S(1)}, bf16[256,512]{1,0:T(8,128)(2,1)S(1)}, u32[]{:S(2)}, u32[]{:S(2)}) collective-permute-start(bf16[256,512]{1,0:T(8,128)(2,1)S(1)} %collective-permute-done.1.refs_2_), channel_id=1, source_target_pairs={{16,24},{20,28},{8,0},{12,4},{24,16},{28,20},{0,8},{4,12},{17,25},... | collective-permute-start | bytes 786440 | tf_op jit(solution)/shard_map/ppermute | solution.py:29
  14.9 9.7 %collective-permute-start = (bf16[256,512]{1,0:T(8,128)(2,1)S(1)}, bf16[256,512]{1,0:T(8,128)(2,1)S(1)}, u32[]{:S(2)}, u32[]{:S(2)}) collective-permute-start(bf16[256,512]{1,0:T(8,128)(2,1)S(1)} %convert_element_type.3.refs_0_), channel_id=1, source_target_pairs={{0,4},{4,0},{8,12},{12,8},{16,20},{20,16},{24,28},{28,24},{1,5},{5... | collective-permute-start | bytes 786440 | tf_op jit(solution)/shard_map/ppermute | solution.py:33
  14.9 9.7 %collective-permute-start.2 = (bf16[256,512]{1,0:T(8,128)(2,1)S(1)}, bf16[256,512]{1,0:T(8,128)(2,1)S(1)}, u32[]{:S(2)}, u32[]{:S(2)}) collective-permute-start(bf16[256,512]{1,0:T(8,128)(2,1)S(1)} %collective-permute-done.1.refs_2_), channel_id=1, source_target_pairs={{0,4},{4,0},{8,12},{12,8},{16,20},{20,16},{24,28},{28,24},{1,5},{5... | collective-permute-start | bytes 786440 | tf_op jit(solution)/shard_map/ppermute | solution.py:33
  20.3 4.2 %collective-permute-start.4 = (bf16[256,512]{1,0:T(8,128)(2,1)S(1)}, bf16[256,512]{1,0:T(8,128)(2,1)S(1)}, u32[]{:S(2)}, u32[]{:S(2)}) collective-permute-start(bf16[256,512]{1,0:T(8,128)(2,1)S(1)} %collective-permute-done.3.refs_4_), channel_id=1, source_target_pairs={{0,4},{4,0},{8,12},{12,8},{16,20},{20,16},{24,28},{28,24},{1,5},{5... | collective-permute-start | bytes 786440 | tf_op jit(solution)/shard_map/ppermute | solution.py:33
  20.3 5.3 %collective-permute-start.7 = (bf16[256,512]{1,0:T(8,128)(2,1)S(1)}, bf16[256,512]{1,0:T(8,128)(2,1)S(1)}, u32[]{:S(2)}, u32[]{:S(2)}) collective-permute-start(bf16[256,512]{1,0:T(8,128)(2,1)S(1)} %collective-permute-done.5.refs_6_), channel_id=1, source_target_pairs={{0,4},{4,0},{8,12},{12,8},{16,20},{20,16},{24,28},{28,24},{1,5},{5... | collective-permute-start | bytes 786440 | tf_op jit(solution)/shard_map/ppermute | solution.py:33
  24.5 1.5 %collective-permute-start.8 = (bf16[256,512]{1,0:T(8,128)(2,1)S(1)}, bf16[256,512]{1,0:T(8,128)(2,1)S(1)}, u32[]{:S(2)}, u32[]{:S(2)}) collective-permute-start(bf16[256,512]{1,0:T(8,128)(2,1)S(1)} %collective-permute-done.6.refs_7_), channel_id=1, source_target_pairs={{0,4},{4,0},{8,12},{12,8},{16,20},{20,16},{24,28},{28,24},{1,5},{5... | collective-permute-start | bytes 786440 | tf_op jit(solution)/shard_map/ppermute | solution.py:33
  26.4 3.7 %collective-permute-start.9 = (bf16[1024,512]{1,0:T(8,128)(2,1)S(1)}, bf16[1024,512]{1,0:T(8,128)(2,1)S(1)}, u32[]{:S(2)}, u32[]{:S(2)}) collective-permute-start(bf16[1024,512]{1,0:T(8,128)(2,1)S(1)} %get-tuple-element.31), channel_id=1, source_target_pairs={{0,4},{4,0},{8,12},{12,8},{16,20},{20,16},{24,28},{28,24},{1,5},{5... | collective-permute-start | bytes 3145736 | tf_op jit(solution)/shard_map/ppermute | solution.py:33
  26.6 6.2 %collective-permute-start.10 = (bf16[128,512]{1,0:T(8,128)(2,1)S(1)}, bf16[128,512]{1,0:T(8,128)(2,1)S(1)}, u32[]{:S(2)}, u32[]{:S(2)}) collective-permute-start(bf16[128,512]{1,0:T(8,128)(2,1)S(1)} %get-tuple-element.34), channel_id=1, source_target_pairs={{0,1},{1,0},{2,3},{3,2},{4,5},{5,4},{6,7},{7,6},{8,9},{9,8},{10,11... | collective-permute-start | bytes 393224 | tf_op jit(solution)/shard_map/ppermute | solution.py:33
  28.0 8.3 %collective-permute-start.11 = (bf16[128,512]{1,0:T(8,128)(2,1)S(1)}, bf16[128,512]{1,0:T(8,128)(2,1)S(1)}, u32[]{:S(2)}, u32[]{:S(2)}) collective-permute-start(bf16[128,512]{1,0:T(8,128)(2,1)S(1)} %get-tuple-element.35), channel_id=1, source_target_pairs={{0,2},{1,3},{2,0},{3,1},{4,6},{5,7},{6,4},{7,5},{8,10},{9,11},{10,... | collective-permute-start | bytes 393224 | tf_op jit(solution)/shard_map/ppermute | solution.py:33
  29.6 6.7 %collective-permute-start.12 = (bf16[128,512]{1,0:T(8,128)(2,1)S(1)}, bf16[128,512]{1,0:T(8,128)(2,1)S(1)}, u32[]{:S(2)}, u32[]{:S(2)}) collective-permute-start(bf16[128,512]{1,0:T(8,128)(2,1)S(1)} %get-tuple-element.36), channel_id=1, source_target_pairs={{0,3},{1,2},{2,1},{3,0},{4,7},{5,6},{6,5},{7,4},{8,11},{9,10},{10,... | collective-permute-start | bytes 393224 | tf_op jit(solution)/shard_map/ppermute | solution.py:33
  36.8 5.6 %collective-permute-start.13 = (bf16[128,512]{1,0:T(8,128)(2,1)S(1)}, bf16[128,512]{1,0:T(8,128)(2,1)S(1)}, u32[]{:S(2)}, u32[]{:S(2)}) collective-permute-start(bf16[128,512]{1,0:T(8,128)(2,1)S(1)} %get-tuple-element.38.refs_2_), channel_id=1, source_target_pairs={{0,1},{1,0},{2,3},{3,2},{4,5},{5,4},{6,7},{7,6},{8,9},{9,8},{10,11... | collective-permute-start | bytes 393224 | tf_op jit(solution)/shard_map/ppermute | solution.py:33
  38.2 7.5 %collective-permute-start.14 = (bf16[128,512]{1,0:T(8,128)(2,1)S(1)}, bf16[128,512]{1,0:T(8,128)(2,1)S(1)}, u32[]{:S(2)}, u32[]{:S(2)}) collective-permute-start(bf16[128,512]{1,0:T(8,128)(2,1)S(1)} %get-tuple-element.38.refs_2_), channel_id=1, source_target_pairs={{0,2},{1,3},{2,0},{3,1},{4,6},{5,7},{6,4},{7,5},{8,10},{9,11},{10,... | collective-permute-start | bytes 393224 | tf_op jit(solution)/shard_map/ppermute | solution.py:33
  39.0 7.3 %collective-permute-start.15 = (bf16[128,512]{1,0:T(8,128)(2,1)S(1)}, bf16[128,512]{1,0:T(8,128)(2,1)S(1)}, u32[]{:S(2)}, u32[]{:S(2)}) collective-permute-start(bf16[128,512]{1,0:T(8,128)(2,1)S(1)} %get-tuple-element.38.refs_2_), channel_id=1, source_target_pairs={{0,3},{1,2},{2,1},{3,0},{4,7},{5,6},{6,5},{7,4},{8,11},{9,10},{10,... | collective-permute-start | bytes 393224 | tf_op jit(solution)/shard_map/ppermute | solution.py:33
  40.4 5.8 %collective-permute-start.16 = (bf16[128,512]{1,0:T(8,128)(2,1)S(1)}, bf16[128,512]{1,0:T(8,128)(2,1)S(1)}, u32[]{:S(2)}, u32[]{:S(2)}) collective-permute-start(bf16[128,512]{1,0:T(8,128)(2,1)S(1)} %get-tuple-element.38.refs_2_), channel_id=1, source_target_pairs={{0,4},{4,0},{8,12},{12,8},{16,20},{20,16},{24,28},{28,24},{1,5},{5... | collective-permute-start | bytes 393224 | tf_op jit(solution)/shard_map/ppermute | solution.py:33
  45.7 1.3 %collective-permute-start.17 = (bf16[128,512]{1,0:T(8,128)(2,1)S(1)}, bf16[128,512]{1,0:T(8,128)(2,1)S(1)}, u32[]{:S(2)}, u32[]{:S(2)}) collective-permute-start(bf16[128,512]{1,0:T(8,128)(2,1)S(1)} %collective-permute-done.13.refs_3_), channel_id=1, source_target_pairs={{0,4},{4,0},{8,12},{12,8},{16,20},{20,16},{24,28},{28,24},{1,5},{5... | collective-permute-start | bytes 393224 | tf_op jit(solution)/shard_map/ppermute | solution.py:33
  45.7 1.5 %collective-permute-start.18 = (bf16[128,512]{1,0:T(8,128)(2,1)S(1)}, bf16[128,512]{1,0:T(8,128)(2,1)S(1)}, u32[]{:S(2)}, u32[]{:S(2)}) collective-permute-start(bf16[128,512]{1,0:T(8,128)(2,1)S(1)} %collective-permute-done.14.refs_4_), channel_id=1, source_target_pairs={{0,4},{4,0},{8,12},{12,8},{16,20},{20,16},{24,28},{28,24},{1,5},{5... | collective-permute-start | bytes 393224 | tf_op jit(solution)/shard_map/ppermute | solution.py:33
  46.2 1.3 %collective-permute-start.19 = (bf16[128,512]{1,0:T(8,128)(2,1)S(1)}, bf16[128,512]{1,0:T(8,128)(2,1)S(1)}, u32[]{:S(2)}, u32[]{:S(2)}) collective-permute-start(bf16[128,512]{1,0:T(8,128)(2,1)S(1)} %collective-permute-done.15.refs_5_), channel_id=1, source_target_pairs={{0,4},{4,0},{8,12},{12,8},{16,20},{20,16},{24,28},{28,24},{1,5},{5... | collective-permute-start | bytes 393224 | tf_op jit(solution)/shard_map/ppermute | solution.py:33
  48.0 9.2 %collective-permute-start.22 = (bf16[256,512]{1,0:T(8,128)(2,1)S(1)}, bf16[256,512]{1,0:T(8,128)(2,1)S(1)}, u32[]{:S(2)}, u32[]{:S(2)}) collective-permute-start(bf16[256,512]{1,0:T(8,128)(2,1)S(1)} %shard_map.100.refs_10_), channel_id=1, source_target_pairs={{24,16},{28,20},{0,8},{4,12},{16,24},{20,28},{8,0},{12,4},{25,17},... | collective-permute-start | bytes 786440 | tf_op jit(solution)/shard_map/ppermute | solution.py:29
  49.1 13.1 %collective-permute-start.20 = (bf16[256,512]{1,0:T(8,128)(2,1)S(1)}, bf16[256,512]{1,0:T(8,128)(2,1)S(1)}, u32[]{:S(2)}, u32[]{:S(2)}) collective-permute-start(bf16[256,512]{1,0:T(8,128)(2,1)S(1)} %shard_map.100.refs_10_), channel_id=1, source_target_pairs={{16,8},{20,12},{8,16},{12,20},{0,4},{4,0},{24,28},{28,24},{17,9},{... | collective-permute-start | bytes 786440 | tf_op jit(solution)/shard_map/ppermute | solution.py:29
  50.9 11.3 %collective-permute-start.21 = (bf16[256,512]{1,0:T(8,128)(2,1)S(1)}, bf16[256,512]{1,0:T(8,128)(2,1)S(1)}, u32[]{:S(2)}, u32[]{:S(2)}) collective-permute-start(bf16[256,512]{1,0:T(8,128)(2,1)S(1)} %get-tuple-element.44), channel_id=1, source_target_pairs={{8,0},{12,4},{16,24},{20,28},{24,8},{28,12},{0,16},{4,20},{9,1},{1... | collective-permute-start | bytes 786440 | tf_op jit(solution)/shard_map/ppermute | solution.py:29
  57.3 11.7 %collective-permute-start.23 = (bf16[256,512]{1,0:T(8,128)(2,1)S(1)}, bf16[256,512]{1,0:T(8,128)(2,1)S(1)}, u32[]{:S(2)}, u32[]{:S(2)}) collective-permute-start(bf16[256,512]{1,0:T(8,128)(2,1)S(1)} %shard_map.103), channel_id=1, source_target_pairs={{16,0},{20,4},{8,24},{12,28},{0,8},{4,12},{24,16},{28,20},{17,1},{... | collective-permute-start | bytes 786440 | tf_op jit(solution)/shard_map/ppermute | solution.py:29
  (7 other events, 26.6 us)

commit v7 on v6

--- a/solution.py
+++ b/solution.py
@@ -175,14 +175,16 @@
         out[...] = mixed.astype(out.dtype)
 
 
-def last_update(emb, w_hi, w_lo, middle, own, near, onward, out, ready, sems):
-    inner = in_middle()
+def arrived(own, near, middle, out):
+    out[...] = own[...] + near[...].astype(F32) + jnp.where(in_middle(), middle[...].astype(F32), 0)
+
+
+def last_update(emb, w_hi, w_lo, sums, onward, out, ready, sems):
     n = sems.shape[0]
     copies = []
     for k in range(n):
         rows = slice(k * (out.shape[0] // n), (k + 1) * (out.shape[0] // n))
-        side = own[rows, :] + near[rows, :].astype(F32) + onward[rows, :].astype(F32)
-        side = side + jnp.where(inner, middle[rows, :].astype(F32), 0)
+        side = sums[rows, :] + onward[rows, :].astype(F32)
         ready[rows, :] = mix(side, emb[rows, :], w_hi[...], w_lo[...])
         copies.append(pltpu.make_async_copy(ready.at[rows, :], out.at[rows, :], sems.at[k]))
         copies[k].start()
@@ -275,15 +277,16 @@
     )
     near = send(near, back(TURN_2))
     (onward,) = call(pass_on, (shape(held, depth),), (onward, handed), nbytes=1 << 19)
+    (own,) = call(arrived, (shape(held, depth, dtype=F32),), (own, near, middle), nbytes=1 << 20)
     new_items = pl.pallas_call(
         last_update,
         out_shape=shape(held, depth, dtype=F32),
-        in_specs=[VMEM] * 7,
+        in_specs=[VMEM] * 5,
         out_specs=pl.BlockSpec(memory_space=pl.ANY),
         scratch_shapes=(pltpu.VMEM((held, depth), F32), pltpu.SemaphoreType.DMA((2,))),
         compiler_params=PARAMS,
         cost_estimate=pl.CostEstimate(flops=12 * held * depth * depth, bytes_accessed=4 << 20, transcendentals=0),
-    )(item_emb, w_hi, w_lo, middle, own, near, send(onward, back(TURN_1)))
+    )(item_emb, w_hi, w_lo, own, send(onward, back(TURN_1)))
     return (new_users, new_items)
 
 

time: 71 us -> 71 us (level)
    pallas_call x9 -> x10, Pallas kernels: 6.36 us -> 6.48 us  [call(): pl.pallas_call(kernel, out_shape=out_shape, in_specs=[SMEM] * smem + [VME...]
where the time goes in v7:
time: 71 us; the launch traced here: 70.8 us
  waiting for transfers between devices  36.5 us (51%)
  starting transfers between devices  20 us (28%)
  Pallas kernels  8.19 us (12%)
  local copies, waits for them, and re-layouts  3.54 us (5%)
  between operations  1.41 us (2%)
  other arithmetic  1.08 us (2%)
    ppermute x8, waiting for transfers between devices, send(): return lax.ppermute(x, 'au', perm)  23.2 us
    ppermute x16, waiting for transfers between devices, swap(): return lax.ppermute(x, axis, [(i, i ^ by) for i in range(n)])  13.3 us
    ppermute x8, starting transfers between devices, send(): return lax.ppermute(x, 'au', perm)  11.2 us
    ppermute x16, starting transfers between devices, swap(): return lax.ppermute(x, axis, [(i, i ^ by) for i in range(n)])  8.81 us
    pallas_call x10, Pallas kernels, call(): pl.pallas_call(kernel, out_shape=out_shape, in_specs=[SMEM] * smem + [VME...  6.48 us
    unnamed x14, local copies, waits for them, and re-layouts  3.54 us
    pallas_call x1, Pallas kernels, in_turns(): pl.pallas_call(last_update, out_shape=shape(held, depth, dtype=F32), in_s...  1.71 us
  transfers between devices with their start and end apart: 24, of which 14 were waited for; matrix products, arithmetic and copies ran while one was open for 0% of the time, Pallas kernels for 7%

profile of v7, /device:TPU:0, one launch (start us, length us, event | category | flops | bytes accessed | tf_op | source)
XLA Modules:
  0.0 70.8 jit_solution(13152099506118040627)
XLA Ops:
  0.6 1.1 %convert_element_type.3.refs_0_ = bf16[256,512]{1,0:T(8,128)(2,1)S(1)} convert(f32[256,512]{1,0:T(8,128)} %emb.1) | non-fusion elementwise | flops 131072 | bytes 786432 | tf_op jit(solution)/shard_map/convert_element_type | solution.py:208
  1.7 4.1 %collective-permute-start.1 = (bf16[256,512]{1,0:T(8,128)(2,1)S(1)}, bf16[256,512]{1,0:T(8,128)(2,1)S(1)}, u32[]{:S(2)}, u32[]{:S(2)}) collective-permute-start(bf16[256,512]{1,0:T(8,128)(2,1)S(1)} %convert_element_type.3.refs_0_), channel_id=1, source_target_pairs={{0,16},{4,20},{24,8},{28,12},{8,0},{12,4},{16,24},{20,28},{1,17},{... | collective-permute-start | bytes 786440 | tf_op jit(solution)/shard_map/ppermute | solution.py:29
  6.5 1.4 %copy-done.1 = bf16[1,12,256,256]{3,2,1,0:T(8,128)(2,1)S(1)} copy-done((bf16[1,12,256,256]{3,2,1,0:T(8,128)(2,1)S(1)}, bf16[1,12,256,256]{3,2,1,0:T(8,128)(2,1)}, u32[]{:S(2)}) %copy-start.1) | copy-done | bytes 1572888
  11.0 1.2 %shard_map.96 = (bf16[1024,512]{1,0:T(8,128)(2,1)S(1)}, bf16[1024,512]{1,0:T(8,128)(2,1)S(1)}, f32[128,512]{1,0:T(8,128)S(1)}, bf16[1024,512]{1,0:T(8,128)(2,1)S(1)}, bf16[1024,512]{1,0:T(8,128)(2,1)S(1)}) custom-call(bf16[512,2048]{1,0:T(8,128)(2,1)S(1)} %shard_map.95.adj, f32[512,512]{1,0:T(8,128)S(1)} %copy-done.2, f32[512,512]{1,0:T(8,128)S(1)} %copy-done.3, ...), custom_call_target="tpu_custom_call" | custom-call | bytes 9437184 | tf_op jit(solution)/shard_map/pallas_call | solution.py:49
  12.5 2.4 %collective-permute-start.6 = (bf16[256,512]{1,0:T(8,128)(2,1)S(1)}, bf16[256,512]{1,0:T(8,128)(2,1)S(1)}, u32[]{:S(2)}, u32[]{:S(2)}) collective-permute-start(bf16[256,512]{1,0:T(8,128)(2,1)S(1)} %collective-permute-done.1.refs_2_), channel_id=1, source_target_pairs={{16,24},{20,28},{8,0},{12,4},{24,16},{28,20},{0,8},{4,12},{17,25},... | collective-permute-start | bytes 786440 | tf_op jit(solution)/shard_map/ppermute | solution.py:29
  15.4 4.9 %collective-permute-done.3.refs_4_ = bf16[256,512]{1,0:T(8,128)(2,1)S(1)} collective-permute-done((bf16[256,512]{1,0:T(8,128)(2,1)S(1)}, bf16[256,512]{1,0:T(8,128)(2,1)S(1)}, u32[]{:S(2)}, u32[]{:S(2)}) %collective-permute-start.3) | collective-permute-done | bytes 262176 | tf_op jit(solution)/shard_map/ppermute | solution.py:29
  20.9 3.5 %collective-permute-done.6.refs_7_ = bf16[256,512]{1,0:T(8,128)(2,1)S(1)} collective-permute-done((bf16[256,512]{1,0:T(8,128)(2,1)S(1)}, bf16[256,512]{1,0:T(8,128)(2,1)S(1)}, u32[]{:S(2)}, u32[]{:S(2)}) %collective-permute-start.6) | collective-permute-done | bytes 262176 | tf_op jit(solution)/shard_map/ppermute | solution.py:29
  24.4 1.1 %shard_map.97.early = f32[512,512]{1,0:T(8,128)S(1)} custom-call(bf16[512,2048]{1,0:T(8,128)(2,1)S(1)} %shard_map.95.adj, bf16[256,512]{1,0:T(8,128)(2,1)S(1)} %convert_element_type.3.refs_0_, bf16[256,512]{1,0:T(8,128)(2,1)S(1)} %collective-permute-done.refs_1_, bf16[256,512]{1,0:T(8,128)(2,1)S(1)} %collective-permute-done.1.refs_2_, ...), custom_call_target="tpu_custom_call" | custom-call | flops 536870912 | bytes 4194304 | tf_op jit(solution)/shard_map/pallas_call | solution.py:49
  26.5 1.6 %collective-permute-start.10 = (bf16[128,512]{1,0:T(8,128)(2,1)S(1)}, bf16[128,512]{1,0:T(8,128)(2,1)S(1)}, u32[]{:S(2)}, u32[]{:S(2)}) collective-permute-start(bf16[128,512]{1,0:T(8,128)(2,1)S(1)} %get-tuple-element.34), channel_id=1, source_target_pairs={{0,1},{1,0},{2,3},{3,2},{4,5},{5,4},{6,7},{7,6},{8,9},{9,8},{10,11... | collective-permute-start | bytes 393224 | tf_op jit(solution)/shard_map/ppermute | solution.py:33
  28.1 1.4 %collective-permute-start.11 = (bf16[128,512]{1,0:T(8,128)(2,1)S(1)}, bf16[128,512]{1,0:T(8,128)(2,1)S(1)}, u32[]{:S(2)}, u32[]{:S(2)}) collective-permute-start(bf16[128,512]{1,0:T(8,128)(2,1)S(1)} %get-tuple-element.35), channel_id=1, source_target_pairs={{0,2},{1,3},{2,0},{3,1},{4,6},{5,7},{6,4},{7,5},{8,10},{9,11},{10,... | collective-permute-start | bytes 393224 | tf_op jit(solution)/shard_map/ppermute | solution.py:33
  30.0 2.5 %collective-permute-done.10.refs_0_ = bf16[128,512]{1,0:T(8,128)(2,1)S(1)} collective-permute-done((bf16[128,512]{1,0:T(8,128)(2,1)S(1)}, bf16[128,512]{1,0:T(8,128)(2,1)S(1)}, u32[]{:S(2)}, u32[]{:S(2)}) %collective-permute-start.10) | collective-permute-done | bytes 131104 | tf_op jit(solution)/shard_map/ppermute | solution.py:33
  32.5 3.9 %collective-permute-done.11.refs_1_ = bf16[128,512]{1,0:T(8,128)(2,1)S(1)} collective-permute-done((bf16[128,512]{1,0:T(8,128)(2,1)S(1)}, bf16[128,512]{1,0:T(8,128)(2,1)S(1)}, u32[]{:S(2)}, u32[]{:S(2)}) %collective-permute-start.11) | collective-permute-done | bytes 131104 | tf_op jit(solution)/shard_map/ppermute | solution.py:33
  37.0 1.2 %collective-permute-start.13 = (bf16[128,512]{1,0:T(8,128)(2,1)S(1)}, bf16[128,512]{1,0:T(8,128)(2,1)S(1)}, u32[]{:S(2)}, u32[]{:S(2)}) collective-permute-start(bf16[128,512]{1,0:T(8,128)(2,1)S(1)} %get-tuple-element.38.refs_2_), channel_id=1, source_target_pairs={{0,1},{1,0},{2,3},{3,2},{4,5},{5,4},{6,7},{7,6},{8,9},{9,8},{10,11... | collective-permute-start | bytes 393224 | tf_op jit(solution)/shard_map/ppermute | solution.py:33
  39.0 1.5 %collective-permute-start.15 = (bf16[128,512]{1,0:T(8,128)(2,1)S(1)}, bf16[128,512]{1,0:T(8,128)(2,1)S(1)}, u32[]{:S(2)}, u32[]{:S(2)}) collective-permute-start(bf16[128,512]{1,0:T(8,128)(2,1)S(1)} %get-tuple-element.38.refs_2_), channel_id=1, source_target_pairs={{0,3},{1,2},{2,1},{3,0},{4,7},{5,6},{6,5},{7,4},{8,11},{9,10},{10,... | collective-permute-start | bytes 393224 | tf_op jit(solution)/shard_map/ppermute | solution.py:33
  40.5 2.3 %collective-permute-done.13.refs_3_ = bf16[128,512]{1,0:T(8,128)(2,1)S(1)} collective-permute-done((bf16[128,512]{1,0:T(8,128)(2,1)S(1)}, bf16[128,512]{1,0:T(8,128)(2,1)S(1)}, u32[]{:S(2)}, u32[]{:S(2)}) %collective-permute-start.13) | collective-permute-done | bytes 131104 | tf_op jit(solution)/shard_map/ppermute | solution.py:33
  42.8 2.9 %collective-permute-done.14.refs_4_ = bf16[128,512]{1,0:T(8,128)(2,1)S(1)} collective-permute-done((bf16[128,512]{1,0:T(8,128)(2,1)S(1)}, bf16[128,512]{1,0:T(8,128)(2,1)S(1)}, u32[]{:S(2)}, u32[]{:S(2)}) %collective-permute-start.14) | collective-permute-done | bytes 131104 | tf_op jit(solution)/shard_map/ppermute | solution.py:33
  48.0 1.0 %collective-permute-start.22 = (bf16[256,512]{1,0:T(8,128)(2,1)S(1)}, bf16[256,512]{1,0:T(8,128)(2,1)S(1)}, u32[]{:S(2)}, u32[]{:S(2)}) collective-permute-start(bf16[256,512]{1,0:T(8,128)(2,1)S(1)} %shard_map.100.refs_10_), channel_id=1, source_target_pairs={{24,16},{28,20},{0,8},{4,12},{16,24},{20,28},{8,0},{12,4},{25,17},... | collective-permute-start | bytes 786440 | tf_op jit(solution)/shard_map/ppermute | solution.py:29
  49.7 1.1 %shard_map.102 = (bf16[256,512]{1,0:T(8,128)(2,1)S(1)}, f32[128,512]{1,0:T(8,128)}) custom-call(bf16[1024,512]{1,0:T(8,128)(2,1)S(1)} %get-tuple-element.24.refs_0_, bf16[1024,512]{1,0:T(8,128)(2,1)S(1)} %collective-permute-done.9.refs_1_, bf16[128,512]{1,0:T(8,128)(2,1)S(1)} %get-tuple-element.38.refs_2_, ...), custom_call_target="tpu_custom_call" | custom-call | flops 268435456 | bytes 2097152 | tf_op jit(solution)/shard_map/pallas_call | solution.py:49
  50.8 2.5 %collective-permute-start.20 = (bf16[256,512]{1,0:T(8,128)(2,1)S(1)}, bf16[256,512]{1,0:T(8,128)(2,1)S(1)}, u32[]{:S(2)}, u32[]{:S(2)}) collective-permute-start(bf16[256,512]{1,0:T(8,128)(2,1)S(1)} %get-tuple-element.44), channel_id=1, source_target_pairs={{8,0},{12,4},{16,24},{20,28},{24,8},{28,12},{0,16},{4,20},{9,1},{1... | collective-permute-start | bytes 786440 | tf_op jit(solution)/shard_map/ppermute | solution.py:29
  53.3 3.9 %collective-permute-done.22.handed = bf16[256,512]{1,0:T(8,128)(2,1)S(1)} collective-permute-done((bf16[256,512]{1,0:T(8,128)(2,1)S(1)}, bf16[256,512]{1,0:T(8,128)(2,1)S(1)}, u32[]{:S(2)}, u32[]{:S(2)}) %collective-permute-start.22) | collective-permute-done | bytes 262176 | tf_op jit(solution)/shard_map/ppermute | solution.py:29
  57.3 1.0 %collective-permute-start.23 = (bf16[256,512]{1,0:T(8,128)(2,1)S(1)}, bf16[256,512]{1,0:T(8,128)(2,1)S(1)}, u32[]{:S(2)}, u32[]{:S(2)}) collective-permute-start(bf16[256,512]{1,0:T(8,128)(2,1)S(1)} %shard_map.104), channel_id=1, source_target_pairs={{16,0},{20,4},{8,24},{12,28},{0,8},{4,12},{24,16},{28,20},{17,1},{... | collective-permute-start | bytes 786440 | tf_op jit(solution)/shard_map/ppermute | solution.py:29
  58.3 3.9 %collective-permute-done.20.near = bf16[256,512]{1,0:T(8,128)(2,1)S(1)} collective-permute-done((bf16[256,512]{1,0:T(8,128)(2,1)S(1)}, bf16[256,512]{1,0:T(8,128)(2,1)S(1)}, u32[]{:S(2)}, u32[]{:S(2)}) %collective-permute-start.20) | collective-permute-done | bytes 262176 | tf_op jit(solution)/shard_map/ppermute | solution.py:29
  62.3 6.8 %collective-permute-done.23.onward = bf16[256,512]{1,0:T(8,128)(2,1)S(1)} collective-permute-done((bf16[256,512]{1,0:T(8,128)(2,1)S(1)}, bf16[256,512]{1,0:T(8,128)(2,1)S(1)}, u32[]{:S(2)}, u32[]{:S(2)}) %collective-permute-start.23) | collective-permute-done | bytes 262176 | tf_op jit(solution)/shard_map/ppermute | solution.py:29
  69.1 1.7 %shard_map.105 = f32[256,512]{1,0:T(8,128)} custom-call(f32[256,512]{1,0:T(8,128)S(1)} %copy-done, bf16[1024,512]{1,0:T(8,128)(2,1)S(1)} %get-tuple-element.26.w_hi, bf16[1024,512]{1,0:T(8,128)(2,1)S(1)} %get-tuple-element.33.w_lo, f32[256,512]{1,0:T(8,128)S(1)} %shard_map.103.sums, bf16[256,512]{1,0:T(8,128)(2,1)S(1)} %collective-permute-done.23.onward), custom_call_target="tpu_custom_call" | custom-call | flops 805306368 | bytes 4194304 | tf_op jit(solution)/shard_map/pallas_call | solution.py:281
  (50 shorter events, 10.4 us)
Async XLA Ops:
  1.7 10.8 %collective-permute-start.1 = (bf16[256,512]{1,0:T(8,128)(2,1)S(1)}, bf16[256,512]{1,0:T(8,128)(2,1)S(1)}, u32[]{:S(2)}, u32[]{:S(2)}) collective-permute-start(bf16[256,512]{1,0:T(8,128)(2,1)S(1)} %convert_element_type.3.refs_0_), channel_id=1, source_target_pairs={{0,16},{4,20},{24,8},{28,12},{8,0},{12,4},{16,24},{20,28},{1,17},{... | collective-permute-start | bytes 786440 | tf_op jit(solution)/shard_map/ppermute | solution.py:29
  10.1 10.2 %collective-permute-start.3 = (bf16[256,512]{1,0:T(8,128)(2,1)S(1)}, bf16[256,512]{1,0:T(8,128)(2,1)S(1)}, u32[]{:S(2)}, u32[]{:S(2)}) collective-permute-start(bf16[256,512]{1,0:T(8,128)(2,1)S(1)} %convert_element_type.3.refs_0_), channel_id=1, source_target_pairs={{0,8},{4,12},{24,16},{28,20},{8,24},{12,28},{16,0},{20,4},{1,9},{5... | collective-permute-start | bytes 786440 | tf_op jit(solution)/shard_map/ppermute | solution.py:29
  12.2 8.2 %collective-permute-start.5 = (bf16[256,512]{1,0:T(8,128)(2,1)S(1)}, bf16[256,512]{1,0:T(8,128)(2,1)S(1)}, u32[]{:S(2)}, u32[]{:S(2)}) collective-permute-start(bf16[256,512]{1,0:T(8,128)(2,1)S(1)} %convert_element_type.3.refs_0_), channel_id=1, source_target_pairs={{8,16},{12,20},{16,8},{20,12},{0,4},{4,0},{24,28},{28,24},{9,17},{... | collective-permute-start | bytes 786440 | tf_op jit(solution)/shard_map/ppermute | solution.py:29
  12.5 11.9 %collective-permute-start.6 = (bf16[256,512]{1,0:T(8,128)(2,1)S(1)}, bf16[256,512]{1,0:T(8,128)(2,1)S(1)}, u32[]{:S(2)}, u32[]{:S(2)}) collective-permute-start(bf16[256,512]{1,0:T(8,128)(2,1)S(1)} %collective-permute-done.1.refs_2_), channel_id=1, source_target_pairs={{16,24},{20,28},{8,0},{12,4},{24,16},{28,20},{0,8},{4,12},{17,25},... | collective-permute-start | bytes 786440 | tf_op jit(solution)/shard_map/ppermute | solution.py:29
  14.9 9.5 %collective-permute-start = (bf16[256,512]{1,0:T(8,128)(2,1)S(1)}, bf16[256,512]{1,0:T(8,128)(2,1)S(1)}, u32[]{:S(2)}, u32[]{:S(2)}) collective-permute-start(bf16[256,512]{1,0:T(8,128)(2,1)S(1)} %convert_element_type.3.refs_0_), channel_id=1, source_target_pairs={{0,4},{4,0},{8,12},{12,8},{16,20},{20,16},{24,28},{28,24},{1,5},{5... | collective-permute-start | bytes 786440 | tf_op jit(solution)/shard_map/ppermute | solution.py:33
  14.9 9.5 %collective-permute-start.2 = (bf16[256,512]{1,0:T(8,128)(2,1)S(1)}, bf16[256,512]{1,0:T(8,128)(2,1)S(1)}, u32[]{:S(2)}, u32[]{:S(2)}) collective-permute-start(bf16[256,512]{1,0:T(8,128)(2,1)S(1)} %collective-permute-done.1.refs_2_), channel_id=1, source_target_pairs={{0,4},{4,0},{8,12},{12,8},{16,20},{20,16},{24,28},{28,24},{1,5},{5... | collective-permute-start | bytes 786440 | tf_op jit(solution)/shard_map/ppermute | solution.py:33
  20.4 4.1 %collective-permute-start.4 = (bf16[256,512]{1,0:T(8,128)(2,1)S(1)}, bf16[256,512]{1,0:T(8,128)(2,1)S(1)}, u32[]{:S(2)}, u32[]{:S(2)}) collective-permute-start(bf16[256,512]{1,0:T(8,128)(2,1)S(1)} %collective-permute-done.3.refs_4_), channel_id=1, source_target_pairs={{0,4},{4,0},{8,12},{12,8},{16,20},{20,16},{24,28},{28,24},{1,5},{5... | collective-permute-start | bytes 786440 | tf_op jit(solution)/shard_map/ppermute | solution.py:33
  20.4 5.2 %collective-permute-start.7 = (bf16[256,512]{1,0:T(8,128)(2,1)S(1)}, bf16[256,512]{1,0:T(8,128)(2,1)S(1)}, u32[]{:S(2)}, u32[]{:S(2)}) collective-permute-start(bf16[256,512]{1,0:T(8,128)(2,1)S(1)} %collective-permute-done.5.refs_6_), channel_id=1, source_target_pairs={{0,4},{4,0},{8,12},{12,8},{16,20},{20,16},{24,28},{28,24},{1,5},{5... | collective-permute-start | bytes 786440 | tf_op jit(solution)/shard_map/ppermute | solution.py:33
  24.4 1.5 %collective-permute-start.8 = (bf16[256,512]{1,0:T(8,128)(2,1)S(1)}, bf16[256,512]{1,0:T(8,128)(2,1)S(1)}, u32[]{:S(2)}, u32[]{:S(2)}) collective-permute-start(bf16[256,512]{1,0:T(8,128)(2,1)S(1)} %collective-permute-done.6.refs_7_), channel_id=1, source_target_pairs={{0,4},{4,0},{8,12},{12,8},{16,20},{20,16},{24,28},{28,24},{1,5},{5... | collective-permute-start | bytes 786440 | tf_op jit(solution)/shard_map/ppermute | solution.py:33
  26.3 3.7 %collective-permute-start.9 = (bf16[1024,512]{1,0:T(8,128)(2,1)S(1)}, bf16[1024,512]{1,0:T(8,128)(2,1)S(1)}, u32[]{:S(2)}, u32[]{:S(2)}) collective-permute-start(bf16[1024,512]{1,0:T(8,128)(2,1)S(1)} %get-tuple-element.31), channel_id=1, source_target_pairs={{0,4},{4,0},{8,12},{12,8},{16,20},{20,16},{24,28},{28,24},{1,5},{5... | collective-permute-start | bytes 3145736 | tf_op jit(solution)/shard_map/ppermute | solution.py:33
  26.5 6.0 %collective-permute-start.10 = (bf16[128,512]{1,0:T(8,128)(2,1)S(1)}, bf16[128,512]{1,0:T(8,128)(2,1)S(1)}, u32[]{:S(2)}, u32[]{:S(2)}) collective-permute-start(bf16[128,512]{1,0:T(8,128)(2,1)S(1)} %get-tuple-element.34), channel_id=1, source_target_pairs={{0,1},{1,0},{2,3},{3,2},{4,5},{5,4},{6,7},{7,6},{8,9},{9,8},{10,11... | collective-permute-start | bytes 393224 | tf_op jit(solution)/shard_map/ppermute | solution.py:33
  28.1 8.3 %collective-permute-start.11 = (bf16[128,512]{1,0:T(8,128)(2,1)S(1)}, bf16[128,512]{1,0:T(8,128)(2,1)S(1)}, u32[]{:S(2)}, u32[]{:S(2)}) collective-permute-start(bf16[128,512]{1,0:T(8,128)(2,1)S(1)} %get-tuple-element.35), channel_id=1, source_target_pairs={{0,2},{1,3},{2,0},{3,1},{4,6},{5,7},{6,4},{7,5},{8,10},{9,11},{10,... | collective-permute-start | bytes 393224 | tf_op jit(solution)/shard_map/ppermute | solution.py:33
  29.5 6.9 %collective-permute-start.12 = (bf16[128,512]{1,0:T(8,128)(2,1)S(1)}, bf16[128,512]{1,0:T(8,128)(2,1)S(1)}, u32[]{:S(2)}, u32[]{:S(2)}) collective-permute-start(bf16[128,512]{1,0:T(8,128)(2,1)S(1)} %get-tuple-element.36), channel_id=1, source_target_pairs={{0,3},{1,2},{2,1},{3,0},{4,7},{5,6},{6,5},{7,4},{8,11},{9,10},{10,... | collective-permute-start | bytes 393224 | tf_op jit(solution)/shard_map/ppermute | solution.py:33
  37.0 5.8 %collective-permute-start.13 = (bf16[128,512]{1,0:T(8,128)(2,1)S(1)}, bf16[128,512]{1,0:T(8,128)(2,1)S(1)}, u32[]{:S(2)}, u32[]{:S(2)}) collective-permute-start(bf16[128,512]{1,0:T(8,128)(2,1)S(1)} %get-tuple-element.38.refs_2_), channel_id=1, source_target_pairs={{0,1},{1,0},{2,3},{3,2},{4,5},{5,4},{6,7},{7,6},{8,9},{9,8},{10,11... | collective-permute-start | bytes 393224 | tf_op jit(solution)/shard_map/ppermute | solution.py:33
  38.2 7.5 %collective-permute-start.14 = (bf16[128,512]{1,0:T(8,128)(2,1)S(1)}, bf16[128,512]{1,0:T(8,128)(2,1)S(1)}, u32[]{:S(2)}, u32[]{:S(2)}) collective-permute-start(bf16[128,512]{1,0:T(8,128)(2,1)S(1)} %get-tuple-element.38.refs_2_), channel_id=1, source_target_pairs={{0,2},{1,3},{2,0},{3,1},{4,6},{5,7},{6,4},{7,5},{8,10},{9,11},{10,... | collective-permute-start | bytes 393224 | tf_op jit(solution)/shard_map/ppermute | solution.py:33
  39.0 7.2 %collective-permute-start.15 = (bf16[128,512]{1,0:T(8,128)(2,1)S(1)}, bf16[128,512]{1,0:T(8,128)(2,1)S(1)}, u32[]{:S(2)}, u32[]{:S(2)}) collective-permute-start(bf16[128,512]{1,0:T(8,128)(2,1)S(1)} %get-tuple-element.38.refs_2_), channel_id=1, source_target_pairs={{0,3},{1,2},{2,1},{3,0},{4,7},{5,6},{6,5},{7,4},{8,11},{9,10},{10,... | collective-permute-start | bytes 393224 | tf_op jit(solution)/shard_map/ppermute | solution.py:33
  40.5 5.7 %collective-permute-start.16 = (bf16[128,512]{1,0:T(8,128)(2,1)S(1)}, bf16[128,512]{1,0:T(8,128)(2,1)S(1)}, u32[]{:S(2)}, u32[]{:S(2)}) collective-permute-start(bf16[128,512]{1,0:T(8,128)(2,1)S(1)} %get-tuple-element.38.refs_2_), channel_id=1, source_target_pairs={{0,4},{4,0},{8,12},{12,8},{16,20},{20,16},{24,28},{28,24},{1,5},{5... | collective-permute-start | bytes 393224 | tf_op jit(solution)/shard_map/ppermute | solution.py:33
  45.7 1.3 %collective-permute-start.17 = (bf16[128,512]{1,0:T(8,128)(2,1)S(1)}, bf16[128,512]{1,0:T(8,128)(2,1)S(1)}, u32[]{:S(2)}, u32[]{:S(2)}) collective-permute-start(bf16[128,512]{1,0:T(8,128)(2,1)S(1)} %collective-permute-done.13.refs_3_), channel_id=1, source_target_pairs={{0,4},{4,0},{8,12},{12,8},{16,20},{20,16},{24,28},{28,24},{1,5},{5... | collective-permute-start | bytes 393224 | tf_op jit(solution)/shard_map/ppermute | solution.py:33
  45.7 1.5 %collective-permute-start.18 = (bf16[128,512]{1,0:T(8,128)(2,1)S(1)}, bf16[128,512]{1,0:T(8,128)(2,1)S(1)}, u32[]{:S(2)}, u32[]{:S(2)}) collective-permute-start(bf16[128,512]{1,0:T(8,128)(2,1)S(1)} %collective-permute-done.14.refs_4_), channel_id=1, source_target_pairs={{0,4},{4,0},{8,12},{12,8},{16,20},{20,16},{24,28},{28,24},{1,5},{5... | collective-permute-start | bytes 393224 | tf_op jit(solution)/shard_map/ppermute | solution.py:33
  46.2 1.3 %collective-permute-start.19 = (bf16[128,512]{1,0:T(8,128)(2,1)S(1)}, bf16[128,512]{1,0:T(8,128)(2,1)S(1)}, u32[]{:S(2)}, u32[]{:S(2)}) collective-permute-start(bf16[128,512]{1,0:T(8,128)(2,1)S(1)} %collective-permute-done.15.refs_5_), channel_id=1, source_target_pairs={{0,4},{4,0},{8,12},{12,8},{16,20},{20,16},{24,28},{28,24},{1,5},{5... | collective-permute-start | bytes 393224 | tf_op jit(solution)/shard_map/ppermute | solution.py:33
  48.0 9.2 %collective-permute-start.22 = (bf16[256,512]{1,0:T(8,128)(2,1)S(1)}, bf16[256,512]{1,0:T(8,128)(2,1)S(1)}, u32[]{:S(2)}, u32[]{:S(2)}) collective-permute-start(bf16[256,512]{1,0:T(8,128)(2,1)S(1)} %shard_map.100.refs_10_), channel_id=1, source_target_pairs={{24,16},{28,20},{0,8},{4,12},{16,24},{20,28},{8,0},{12,4},{25,17},... | collective-permute-start | bytes 786440 | tf_op jit(solution)/shard_map/ppermute | solution.py:29
  49.0 13.1 %collective-permute-start.21 = (bf16[256,512]{1,0:T(8,128)(2,1)S(1)}, bf16[256,512]{1,0:T(8,128)(2,1)S(1)}, u32[]{:S(2)}, u32[]{:S(2)}) collective-permute-start(bf16[256,512]{1,0:T(8,128)(2,1)S(1)} %shard_map.100.refs_10_), channel_id=1, source_target_pairs={{16,8},{20,12},{8,16},{12,20},{0,4},{4,0},{24,28},{28,24},{17,9},{... | collective-permute-start | bytes 786440 | tf_op jit(solution)/shard_map/ppermute | solution.py:29
  50.8 11.3 %collective-permute-start.20 = (bf16[256,512]{1,0:T(8,128)(2,1)S(1)}, bf16[256,512]{1,0:T(8,128)(2,1)S(1)}, u32[]{:S(2)}, u32[]{:S(2)}) collective-permute-start(bf16[256,512]{1,0:T(8,128)(2,1)S(1)} %get-tuple-element.44), channel_id=1, source_target_pairs={{8,0},{12,4},{16,24},{20,28},{24,8},{28,12},{0,16},{4,20},{9,1},{1... | collective-permute-start | bytes 786440 | tf_op jit(solution)/shard_map/ppermute | solution.py:29
  57.3 11.8 %collective-permute-start.23 = (bf16[256,512]{1,0:T(8,128)(2,1)S(1)}, bf16[256,512]{1,0:T(8,128)(2,1)S(1)}, u32[]{:S(2)}, u32[]{:S(2)}) collective-permute-start(bf16[256,512]{1,0:T(8,128)(2,1)S(1)} %shard_map.104), channel_id=1, source_target_pairs={{16,0},{20,4},{8,24},{12,28},{0,8},{4,12},{24,16},{28,20},{17,1},{... | collective-permute-start | bytes 786440 | tf_op jit(solution)/shard_map/ppermute | solution.py:29
  (7 other events, 25.6 us)

commit v8 on v6

--- a/solution.py
+++ b/solution.py
@@ -222,7 +222,7 @@
     )
     middle = send(after(mine, w_hi), MIDDLE)
     first = after(first, w_hi)
-    ends = send(first, HANDED)
+    ends = lax.ppermute(first, "au", [(2 * a + core, 2 * b + core) for a, b in HANDED[:2] for core in (0, 1)])
     (early,) = call(
         early_sums,
         (shape(users, depth, dtype=F32),),

time: 71 us -> 71 us (level)
  starting transfers between devices: 20 us -> 18.9 us
  waiting for transfers between devices: 36.6 us -> 37.7 us
    ppermute x0 -> x1, waiting for transfers between devices: none -> 3.63 us  [in_turns(): lax.ppermute(first, 'au', [(2 * a + core, 2 * b + core) for a, b in HANDE...]
    ppermute x8 -> x7, waiting for transfers between devices: 23.4 us -> 20.7 us  [send(): return lax.ppermute(x, 'au', perm)]
    ppermute x8 -> x7, starting transfers between devices: 11.2 us -> 8.76 us  [send(): return lax.ppermute(x, 'au', perm)]
    ppermute x0 -> x1, starting transfers between devices: none -> 1.28 us  [in_turns(): lax.ppermute(first, 'au', [(2 * a + core, 2 * b + core) for a, b in HANDE...]
where the time goes in v8:
time: 71 us; the launch traced here: 70.8 us
  waiting for transfers between devices  37.7 us (53%)
  starting transfers between devices  18.9 us (27%)
  Pallas kernels  8.03 us (11%)
  local copies, waits for them, and re-layouts  3.63 us (5%)
  between operations  1.43 us (2%)
  other arithmetic  1.08 us (2%)
    ppermute x7, waiting for transfers between devices, send(): return lax.ppermute(x, 'au', perm)  20.7 us
    ppermute x16, waiting for transfers between devices, swap(): return lax.ppermute(x, axis, [(i, i ^ by) for i in range(n)])  13.4 us
    ppermute x16, starting transfers between devices, swap(): return lax.ppermute(x, axis, [(i, i ^ by) for i in range(n)])  8.86 us
    ppermute x7, starting transfers between devices, send(): return lax.ppermute(x, 'au', perm)  8.76 us
    pallas_call x9, Pallas kernels, call(): pl.pallas_call(kernel, out_shape=out_shape, in_specs=[SMEM] * smem + [VME...  6.31 us
    ppermute x1, waiting for transfers between devices, in_turns(): lax.ppermute(first, 'au', [(2 * a + core, 2 * b + core) for a, b in HANDE...  3.63 us
    unnamed x14, local copies, waits for them, and re-layouts  3.63 us
    pallas_call x1, Pallas kernels, in_turns(): pl.pallas_call(last_update, out_shape=shape(held, depth, dtype=F32), in_s...  1.72 us
  transfers between devices with their start and end apart: 24, of which 14 were waited for; matrix products, arithmetic and copies ran while one was open for 0% of the time, Pallas kernels for 7%

profile of v8, /device:TPU:0, one launch (start us, length us, event | category | flops | bytes accessed | tf_op | source)
XLA Modules:
  0.0 70.8 jit_solution(4019685440777074455)
XLA Ops:
  0.6 1.1 %convert_element_type.3.refs_0_ = bf16[256,512]{1,0:T(8,128)(2,1)S(1)} convert(f32[256,512]{1,0:T(8,128)} %emb.1) | non-fusion elementwise | flops 131072 | bytes 786432 | tf_op jit(solution)/shard_map/convert_element_type | solution.py:206
  1.7 4.1 %collective-permute-start.1 = (bf16[256,512]{1,0:T(8,128)(2,1)S(1)}, bf16[256,512]{1,0:T(8,128)(2,1)S(1)}, u32[]{:S(2)}, u32[]{:S(2)}) collective-permute-start(bf16[256,512]{1,0:T(8,128)(2,1)S(1)} %convert_element_type.3.refs_0_), channel_id=1, source_target_pairs={{0,16},{4,20},{24,8},{28,12},{8,0},{12,4},{16,24},{20,28},{1,17},{... | collective-permute-start | bytes 786440 | tf_op jit(solution)/shard_map/ppermute | solution.py:29
  6.5 1.4 %copy-done.1 = bf16[1,12,256,256]{3,2,1,0:T(8,128)(2,1)S(1)} copy-done((bf16[1,12,256,256]{3,2,1,0:T(8,128)(2,1)S(1)}, bf16[1,12,256,256]{3,2,1,0:T(8,128)(2,1)}, u32[]{:S(2)}) %copy-start.1) | copy-done | bytes 1572888
  11.0 1.2 %shard_map.96 = (bf16[1024,512]{1,0:T(8,128)(2,1)S(1)}, bf16[1024,512]{1,0:T(8,128)(2,1)S(1)}, f32[128,512]{1,0:T(8,128)S(1)}, bf16[1024,512]{1,0:T(8,128)(2,1)S(1)}, bf16[1024,512]{1,0:T(8,128)(2,1)S(1)}) custom-call(bf16[512,2048]{1,0:T(8,128)(2,1)S(1)} %shard_map.95.adj, f32[512,512]{1,0:T(8,128)S(1)} %copy-done.2, f32[512,512]{1,0:T(8,128)S(1)} %copy-done.3, ...), custom_call_target="tpu_custom_call" | custom-call | bytes 9437184 | tf_op jit(solution)/shard_map/pallas_call | solution.py:49
  12.5 1.3 %collective-permute-start.6 = (bf16[256,512]{1,0:T(8,128)(2,1)S(1)}, bf16[256,512]{1,0:T(8,128)(2,1)S(1)}, u32[]{:S(2)}, u32[]{:S(2)}) collective-permute-start(bf16[256,512]{1,0:T(8,128)(2,1)S(1)} %collective-permute-done.1.refs_2_), channel_id=1, source_target_pairs={{16,24},{20,28},{8,0},{12,4},{17,25},{21,29},{9,1},{13,5},{18,26},... | collective-permute-start | bytes 786440 | tf_op jit(solution)/shard_map/ppermute | solution.py:225
  14.4 5.9 %collective-permute-done.3.refs_4_ = bf16[256,512]{1,0:T(8,128)(2,1)S(1)} collective-permute-done((bf16[256,512]{1,0:T(8,128)(2,1)S(1)}, bf16[256,512]{1,0:T(8,128)(2,1)S(1)}, u32[]{:S(2)}, u32[]{:S(2)}) %collective-permute-start.3) | collective-permute-done | bytes 262176 | tf_op jit(solution)/shard_map/ppermute | solution.py:29
  20.8 3.6 %collective-permute-done.6.refs_7_ = bf16[256,512]{1,0:T(8,128)(2,1)S(1)} collective-permute-done((bf16[256,512]{1,0:T(8,128)(2,1)S(1)}, bf16[256,512]{1,0:T(8,128)(2,1)S(1)}, u32[]{:S(2)}, u32[]{:S(2)}) %collective-permute-start.6) | collective-permute-done | bytes 262176 | tf_op jit(solution)/shard_map/ppermute | solution.py:225
  24.4 1.1 %shard_map.97.early = f32[512,512]{1,0:T(8,128)S(1)} custom-call(bf16[512,2048]{1,0:T(8,128)(2,1)S(1)} %shard_map.95.adj, bf16[256,512]{1,0:T(8,128)(2,1)S(1)} %convert_element_type.3.refs_0_, bf16[256,512]{1,0:T(8,128)(2,1)S(1)} %collective-permute-done.refs_1_, bf16[256,512]{1,0:T(8,128)(2,1)S(1)} %collective-permute-done.1.refs_2_, ...), custom_call_target="tpu_custom_call" | custom-call | flops 536870912 | bytes 4194304 | tf_op jit(solution)/shard_map/pallas_call | solution.py:49
  26.5 1.5 %collective-permute-start.10 = (bf16[128,512]{1,0:T(8,128)(2,1)S(1)}, bf16[128,512]{1,0:T(8,128)(2,1)S(1)}, u32[]{:S(2)}, u32[]{:S(2)}) collective-permute-start(bf16[128,512]{1,0:T(8,128)(2,1)S(1)} %get-tuple-element.34), channel_id=1, source_target_pairs={{0,1},{1,0},{2,3},{3,2},{4,5},{5,4},{6,7},{7,6},{8,9},{9,8},{10,11... | collective-permute-start | bytes 393224 | tf_op jit(solution)/shard_map/ppermute | solution.py:33
  28.0 1.6 %collective-permute-start.11 = (bf16[128,512]{1,0:T(8,128)(2,1)S(1)}, bf16[128,512]{1,0:T(8,128)(2,1)S(1)}, u32[]{:S(2)}, u32[]{:S(2)}) collective-permute-start(bf16[128,512]{1,0:T(8,128)(2,1)S(1)} %get-tuple-element.35), channel_id=1, source_target_pairs={{0,2},{1,3},{2,0},{3,1},{4,6},{5,7},{6,4},{7,5},{8,10},{9,11},{10,... | collective-permute-start | bytes 393224 | tf_op jit(solution)/shard_map/ppermute | solution.py:33
  30.0 2.6 %collective-permute-done.10.refs_0_ = bf16[128,512]{1,0:T(8,128)(2,1)S(1)} collective-permute-done((bf16[128,512]{1,0:T(8,128)(2,1)S(1)}, bf16[128,512]{1,0:T(8,128)(2,1)S(1)}, u32[]{:S(2)}, u32[]{:S(2)}) %collective-permute-start.10) | collective-permute-done | bytes 131104 | tf_op jit(solution)/shard_map/ppermute | solution.py:33
  32.6 3.7 %collective-permute-done.11.refs_1_ = bf16[128,512]{1,0:T(8,128)(2,1)S(1)} collective-permute-done((bf16[128,512]{1,0:T(8,128)(2,1)S(1)}, bf16[128,512]{1,0:T(8,128)(2,1)S(1)}, u32[]{:S(2)}, u32[]{:S(2)}) %collective-permute-start.11) | collective-permute-done | bytes 131104 | tf_op jit(solution)/shard_map/ppermute | solution.py:33
  36.9 1.4 %collective-permute-start.13 = (bf16[128,512]{1,0:T(8,128)(2,1)S(1)}, bf16[128,512]{1,0:T(8,128)(2,1)S(1)}, u32[]{:S(2)}, u32[]{:S(2)}) collective-permute-start(bf16[128,512]{1,0:T(8,128)(2,1)S(1)} %get-tuple-element.38.refs_2_), channel_id=1, source_target_pairs={{0,1},{1,0},{2,3},{3,2},{4,5},{5,4},{6,7},{7,6},{8,9},{9,8},{10,11... | collective-permute-start | bytes 393224 | tf_op jit(solution)/shard_map/ppermute | solution.py:33
  39.0 1.4 %collective-permute-start.15 = (bf16[128,512]{1,0:T(8,128)(2,1)S(1)}, bf16[128,512]{1,0:T(8,128)(2,1)S(1)}, u32[]{:S(2)}, u32[]{:S(2)}) collective-permute-start(bf16[128,512]{1,0:T(8,128)(2,1)S(1)} %get-tuple-element.38.refs_2_), channel_id=1, source_target_pairs={{0,3},{1,2},{2,1},{3,0},{4,7},{5,6},{6,5},{7,4},{8,11},{9,10},{10,... | collective-permute-start | bytes 393224 | tf_op jit(solution)/shard_map/ppermute | solution.py:33
  40.4 2.1 %collective-permute-done.13.refs_3_ = bf16[128,512]{1,0:T(8,128)(2,1)S(1)} collective-permute-done((bf16[128,512]{1,0:T(8,128)(2,1)S(1)}, bf16[128,512]{1,0:T(8,128)(2,1)S(1)}, u32[]{:S(2)}, u32[]{:S(2)}) %collective-permute-start.13) | collective-permute-done | bytes 131104 | tf_op jit(solution)/shard_map/ppermute | solution.py:33
  42.5 3.3 %collective-permute-done.14.refs_4_ = bf16[128,512]{1,0:T(8,128)(2,1)S(1)} collective-permute-done((bf16[128,512]{1,0:T(8,128)(2,1)S(1)}, bf16[128,512]{1,0:T(8,128)(2,1)S(1)}, u32[]{:S(2)}, u32[]{:S(2)}) %collective-permute-start.14) | collective-permute-done | bytes 131104 | tf_op jit(solution)/shard_map/ppermute | solution.py:33
  48.1 1.0 %collective-permute-start.22 = (bf16[256,512]{1,0:T(8,128)(2,1)S(1)}, bf16[256,512]{1,0:T(8,128)(2,1)S(1)}, u32[]{:S(2)}, u32[]{:S(2)}) collective-permute-start(bf16[256,512]{1,0:T(8,128)(2,1)S(1)} %shard_map.100.refs_10_), channel_id=1, source_target_pairs={{24,16},{28,20},{0,8},{4,12},{16,24},{20,28},{8,0},{12,4},{25,17},... | collective-permute-start | bytes 786440 | tf_op jit(solution)/shard_map/ppermute | solution.py:29
  49.8 1.1 %shard_map.102 = (bf16[256,512]{1,0:T(8,128)(2,1)S(1)}, f32[128,512]{1,0:T(8,128)}) custom-call(bf16[1024,512]{1,0:T(8,128)(2,1)S(1)} %get-tuple-element.24.refs_0_, bf16[1024,512]{1,0:T(8,128)(2,1)S(1)} %collective-permute-done.9.refs_1_, bf16[128,512]{1,0:T(8,128)(2,1)S(1)} %get-tuple-element.38.refs_2_, ...), custom_call_target="tpu_custom_call" | custom-call | flops 268435456 | bytes 2097152 | tf_op jit(solution)/shard_map/pallas_call | solution.py:49
  50.9 2.5 %collective-permute-start.21 = (bf16[256,512]{1,0:T(8,128)(2,1)S(1)}, bf16[256,512]{1,0:T(8,128)(2,1)S(1)}, u32[]{:S(2)}, u32[]{:S(2)}) collective-permute-start(bf16[256,512]{1,0:T(8,128)(2,1)S(1)} %get-tuple-element.44), channel_id=1, source_target_pairs={{8,0},{12,4},{16,24},{20,28},{24,8},{28,12},{0,16},{4,20},{9,1},{1... | collective-permute-start | bytes 786440 | tf_op jit(solution)/shard_map/ppermute | solution.py:29
  53.4 3.9 %collective-permute-done.22.handed = bf16[256,512]{1,0:T(8,128)(2,1)S(1)} collective-permute-done((bf16[256,512]{1,0:T(8,128)(2,1)S(1)}, bf16[256,512]{1,0:T(8,128)(2,1)S(1)}, u32[]{:S(2)}, u32[]{:S(2)}) %collective-permute-start.22) | collective-permute-done | bytes 262176 | tf_op jit(solution)/shard_map/ppermute | solution.py:29
  57.4 1.0 %collective-permute-start.23 = (bf16[256,512]{1,0:T(8,128)(2,1)S(1)}, bf16[256,512]{1,0:T(8,128)(2,1)S(1)}, u32[]{:S(2)}, u32[]{:S(2)}) collective-permute-start(bf16[256,512]{1,0:T(8,128)(2,1)S(1)} %shard_map.103), channel_id=1, source_target_pairs={{16,0},{20,4},{8,24},{12,28},{0,8},{4,12},{24,16},{28,20},{17,1},{... | collective-permute-start | bytes 786440 | tf_op jit(solution)/shard_map/ppermute | solution.py:29
  58.3 3.9 %collective-permute-done.21.near = bf16[256,512]{1,0:T(8,128)(2,1)S(1)} collective-permute-done((bf16[256,512]{1,0:T(8,128)(2,1)S(1)}, bf16[256,512]{1,0:T(8,128)(2,1)S(1)}, u32[]{:S(2)}, u32[]{:S(2)}) %collective-permute-start.21) | collective-permute-done | bytes 262176 | tf_op jit(solution)/shard_map/ppermute | solution.py:29
  62.2 6.8 %collective-permute-done.23.onward = bf16[256,512]{1,0:T(8,128)(2,1)S(1)} collective-permute-done((bf16[256,512]{1,0:T(8,128)(2,1)S(1)}, bf16[256,512]{1,0:T(8,128)(2,1)S(1)}, u32[]{:S(2)}, u32[]{:S(2)}) %collective-permute-start.23) | collective-permute-done | bytes 262176 | tf_op jit(solution)/shard_map/ppermute | solution.py:29
  69.1 1.7 %shard_map.104 = f32[256,512]{1,0:T(8,128)} custom-call(f32[256,512]{1,0:T(8,128)S(1)} %copy-done, bf16[1024,512]{1,0:T(8,128)(2,1)S(1)} %get-tuple-element.26.w_hi, bf16[1024,512]{1,0:T(8,128)(2,1)S(1)} %get-tuple-element.33.w_lo, bf16[256,512]{1,0:T(8,128)(2,1)S(1)} %collective-permute-done.20.middle, f32[256,512]{1,0:T(8,128)S(1)} %get-tuple-element.41.refs_10_.own, ...), custom_call_target="tpu_custom_call" | custom-call | flops 805306368 | bytes 4194304 | tf_op jit(solution)/shard_map/pallas_call | solution.py:278
  (49 shorter events, 10.2 us)
Async XLA Ops:
  1.7 10.8 %collective-permute-start.1 = (bf16[256,512]{1,0:T(8,128)(2,1)S(1)}, bf16[256,512]{1,0:T(8,128)(2,1)S(1)}, u32[]{:S(2)}, u32[]{:S(2)}) collective-permute-start(bf16[256,512]{1,0:T(8,128)(2,1)S(1)} %convert_element_type.3.refs_0_), channel_id=1, source_target_pairs={{0,16},{4,20},{24,8},{28,12},{8,0},{12,4},{16,24},{20,28},{1,17},{... | collective-permute-start | bytes 786440 | tf_op jit(solution)/shard_map/ppermute | solution.py:29
  10.1 10.2 %collective-permute-start.3 = (bf16[256,512]{1,0:T(8,128)(2,1)S(1)}, bf16[256,512]{1,0:T(8,128)(2,1)S(1)}, u32[]{:S(2)}, u32[]{:S(2)}) collective-permute-start(bf16[256,512]{1,0:T(8,128)(2,1)S(1)} %convert_element_type.3.refs_0_), channel_id=1, source_target_pairs={{0,8},{4,12},{24,16},{28,20},{8,24},{12,28},{16,0},{20,4},{1,9},{5... | collective-permute-start | bytes 786440 | tf_op jit(solution)/shard_map/ppermute | solution.py:29
  12.2 8.1 %collective-permute-start.5 = (bf16[256,512]{1,0:T(8,128)(2,1)S(1)}, bf16[256,512]{1,0:T(8,128)(2,1)S(1)}, u32[]{:S(2)}, u32[]{:S(2)}) collective-permute-start(bf16[256,512]{1,0:T(8,128)(2,1)S(1)} %convert_element_type.3.refs_0_), channel_id=1, source_target_pairs={{8,16},{12,20},{16,8},{20,12},{0,4},{4,0},{24,28},{28,24},{9,17},{... | collective-permute-start | bytes 786440 | tf_op jit(solution)/shard_map/ppermute | solution.py:29
  12.5 11.9 %collective-permute-start.6 = (bf16[256,512]{1,0:T(8,128)(2,1)S(1)}, bf16[256,512]{1,0:T(8,128)(2,1)S(1)}, u32[]{:S(2)}, u32[]{:S(2)}) collective-permute-start(bf16[256,512]{1,0:T(8,128)(2,1)S(1)} %collective-permute-done.1.refs_2_), channel_id=1, source_target_pairs={{16,24},{20,28},{8,0},{12,4},{17,25},{21,29},{9,1},{13,5},{18,26},... | collective-permute-start | bytes 786440 | tf_op jit(solution)/shard_map/ppermute | solution.py:225
  13.8 10.6 %collective-permute-start = (bf16[256,512]{1,0:T(8,128)(2,1)S(1)}, bf16[256,512]{1,0:T(8,128)(2,1)S(1)}, u32[]{:S(2)}, u32[]{:S(2)}) collective-permute-start(bf16[256,512]{1,0:T(8,128)(2,1)S(1)} %convert_element_type.3.refs_0_), channel_id=1, source_target_pairs={{0,4},{4,0},{8,12},{12,8},{16,20},{20,16},{24,28},{28,24},{1,5},{5... | collective-permute-start | bytes 786440 | tf_op jit(solution)/shard_map/ppermute | solution.py:33
  14.1 10.3 %collective-permute-start.2 = (bf16[256,512]{1,0:T(8,128)(2,1)S(1)}, bf16[256,512]{1,0:T(8,128)(2,1)S(1)}, u32[]{:S(2)}, u32[]{:S(2)}) collective-permute-start(bf16[256,512]{1,0:T(8,128)(2,1)S(1)} %collective-permute-done.1.refs_2_), channel_id=1, source_target_pairs={{0,4},{4,0},{8,12},{12,8},{16,20},{20,16},{24,28},{28,24},{1,5},{5... | collective-permute-start | bytes 786440 | tf_op jit(solution)/shard_map/ppermute | solution.py:33
  20.3 4.2 %collective-permute-start.4 = (bf16[256,512]{1,0:T(8,128)(2,1)S(1)}, bf16[256,512]{1,0:T(8,128)(2,1)S(1)}, u32[]{:S(2)}, u32[]{:S(2)}) collective-permute-start(bf16[256,512]{1,0:T(8,128)(2,1)S(1)} %collective-permute-done.3.refs_4_), channel_id=1, source_target_pairs={{0,4},{4,0},{8,12},{12,8},{16,20},{20,16},{24,28},{28,24},{1,5},{5... | collective-permute-start | bytes 786440 | tf_op jit(solution)/shard_map/ppermute | solution.py:33
  20.3 5.3 %collective-permute-start.7 = (bf16[256,512]{1,0:T(8,128)(2,1)S(1)}, bf16[256,512]{1,0:T(8,128)(2,1)S(1)}, u32[]{:S(2)}, u32[]{:S(2)}) collective-permute-start(bf16[256,512]{1,0:T(8,128)(2,1)S(1)} %collective-permute-done.5.refs_6_), channel_id=1, source_target_pairs={{0,4},{4,0},{8,12},{12,8},{16,20},{20,16},{24,28},{28,24},{1,5},{5... | collective-permute-start | bytes 786440 | tf_op jit(solution)/shard_map/ppermute | solution.py:33
  24.4 1.5 %collective-permute-start.8 = (bf16[256,512]{1,0:T(8,128)(2,1)S(1)}, bf16[256,512]{1,0:T(8,128)(2,1)S(1)}, u32[]{:S(2)}, u32[]{:S(2)}) collective-permute-start(bf16[256,512]{1,0:T(8,128)(2,1)S(1)} %collective-permute-done.6.refs_7_), channel_id=1, source_target_pairs={{0,4},{4,0},{8,12},{12,8},{16,20},{20,16},{24,28},{28,24},{1,5},{5... | collective-permute-start | bytes 786440 | tf_op jit(solution)/shard_map/ppermute | solution.py:33
  26.3 3.7 %collective-permute-start.9 = (bf16[1024,512]{1,0:T(8,128)(2,1)S(1)}, bf16[1024,512]{1,0:T(8,128)(2,1)S(1)}, u32[]{:S(2)}, u32[]{:S(2)}) collective-permute-start(bf16[1024,512]{1,0:T(8,128)(2,1)S(1)} %get-tuple-element.31), channel_id=1, source_target_pairs={{0,4},{4,0},{8,12},{12,8},{16,20},{20,16},{24,28},{28,24},{1,5},{5... | collective-permute-start | bytes 3145736 | tf_op jit(solution)/shard_map/ppermute | solution.py:33
  26.5 6.1 %collective-permute-start.10 = (bf16[128,512]{1,0:T(8,128)(2,1)S(1)}, bf16[128,512]{1,0:T(8,128)(2,1)S(1)}, u32[]{:S(2)}, u32[]{:S(2)}) collective-permute-start(bf16[128,512]{1,0:T(8,128)(2,1)S(1)} %get-tuple-element.34), channel_id=1, source_target_pairs={{0,1},{1,0},{2,3},{3,2},{4,5},{5,4},{6,7},{7,6},{8,9},{9,8},{10,11... | collective-permute-start | bytes 393224 | tf_op jit(solution)/shard_map/ppermute | solution.py:33
  28.0 8.3 %collective-permute-start.11 = (bf16[128,512]{1,0:T(8,128)(2,1)S(1)}, bf16[128,512]{1,0:T(8,128)(2,1)S(1)}, u32[]{:S(2)}, u32[]{:S(2)}) collective-permute-start(bf16[128,512]{1,0:T(8,128)(2,1)S(1)} %get-tuple-element.35), channel_id=1, source_target_pairs={{0,2},{1,3},{2,0},{3,1},{4,6},{5,7},{6,4},{7,5},{8,10},{9,11},{10,... | collective-permute-start | bytes 393224 | tf_op jit(solution)/shard_map/ppermute | solution.py:33
  29.6 6.7 %collective-permute-start.12 = (bf16[128,512]{1,0:T(8,128)(2,1)S(1)}, bf16[128,512]{1,0:T(8,128)(2,1)S(1)}, u32[]{:S(2)}, u32[]{:S(2)}) collective-permute-start(bf16[128,512]{1,0:T(8,128)(2,1)S(1)} %get-tuple-element.36), channel_id=1, source_target_pairs={{0,3},{1,2},{2,1},{3,0},{4,7},{5,6},{6,5},{7,4},{8,11},{9,10},{10,... | collective-permute-start | bytes 393224 | tf_op jit(solution)/shard_map/ppermute | solution.py:33
  36.9 5.6 %collective-permute-start.13 = (bf16[128,512]{1,0:T(8,128)(2,1)S(1)}, bf16[128,512]{1,0:T(8,128)(2,1)S(1)}, u32[]{:S(2)}, u32[]{:S(2)}) collective-permute-start(bf16[128,512]{1,0:T(8,128)(2,1)S(1)} %get-tuple-element.38.refs_2_), channel_id=1, source_target_pairs={{0,1},{1,0},{2,3},{3,2},{4,5},{5,4},{6,7},{7,6},{8,9},{9,8},{10,11... | collective-permute-start | bytes 393224 | tf_op jit(solution)/shard_map/ppermute | solution.py:33
  38.3 7.5 %collective-permute-start.14 = (bf16[128,512]{1,0:T(8,128)(2,1)S(1)}, bf16[128,512]{1,0:T(8,128)(2,1)S(1)}, u32[]{:S(2)}, u32[]{:S(2)}) collective-permute-start(bf16[128,512]{1,0:T(8,128)(2,1)S(1)} %get-tuple-element.38.refs_2_), channel_id=1, source_target_pairs={{0,2},{1,3},{2,0},{3,1},{4,6},{5,7},{6,4},{7,5},{8,10},{9,11},{10,... | collective-permute-start | bytes 393224 | tf_op jit(solution)/shard_map/ppermute | solution.py:33
  39.0 7.3 %collective-permute-start.15 = (bf16[128,512]{1,0:T(8,128)(2,1)S(1)}, bf16[128,512]{1,0:T(8,128)(2,1)S(1)}, u32[]{:S(2)}, u32[]{:S(2)}) collective-permute-start(bf16[128,512]{1,0:T(8,128)(2,1)S(1)} %get-tuple-element.38.refs_2_), channel_id=1, source_target_pairs={{0,3},{1,2},{2,1},{3,0},{4,7},{5,6},{6,5},{7,4},{8,11},{9,10},{10,... | collective-permute-start | bytes 393224 | tf_op jit(solution)/shard_map/ppermute | solution.py:33
  40.4 5.9 %collective-permute-start.16 = (bf16[128,512]{1,0:T(8,128)(2,1)S(1)}, bf16[128,512]{1,0:T(8,128)(2,1)S(1)}, u32[]{:S(2)}, u32[]{:S(2)}) collective-permute-start(bf16[128,512]{1,0:T(8,128)(2,1)S(1)} %get-tuple-element.38.refs_2_), channel_id=1, source_target_pairs={{0,4},{4,0},{8,12},{12,8},{16,20},{20,16},{24,28},{28,24},{1,5},{5... | collective-permute-start | bytes 393224 | tf_op jit(solution)/shard_map/ppermute | solution.py:33
  45.8 1.3 %collective-permute-start.17 = (bf16[128,512]{1,0:T(8,128)(2,1)S(1)}, bf16[128,512]{1,0:T(8,128)(2,1)S(1)}, u32[]{:S(2)}, u32[]{:S(2)}) collective-permute-start(bf16[128,512]{1,0:T(8,128)(2,1)S(1)} %collective-permute-done.13.refs_3_), channel_id=1, source_target_pairs={{0,4},{4,0},{8,12},{12,8},{16,20},{20,16},{24,28},{28,24},{1,5},{5... | collective-permute-start | bytes 393224 | tf_op jit(solution)/shard_map/ppermute | solution.py:33
  45.8 1.5 %collective-permute-start.18 = (bf16[128,512]{1,0:T(8,128)(2,1)S(1)}, bf16[128,512]{1,0:T(8,128)(2,1)S(1)}, u32[]{:S(2)}, u32[]{:S(2)}) collective-permute-start(bf16[128,512]{1,0:T(8,128)(2,1)S(1)} %collective-permute-done.14.refs_4_), channel_id=1, source_target_pairs={{0,4},{4,0},{8,12},{12,8},{16,20},{20,16},{24,28},{28,24},{1,5},{5... | collective-permute-start | bytes 393224 | tf_op jit(solution)/shard_map/ppermute | solution.py:33
  46.3 1.3 %collective-permute-start.19 = (bf16[128,512]{1,0:T(8,128)(2,1)S(1)}, bf16[128,512]{1,0:T(8,128)(2,1)S(1)}, u32[]{:S(2)}, u32[]{:S(2)}) collective-permute-start(bf16[128,512]{1,0:T(8,128)(2,1)S(1)} %collective-permute-done.15.refs_5_), channel_id=1, source_target_pairs={{0,4},{4,0},{8,12},{12,8},{16,20},{20,16},{24,28},{28,24},{1,5},{5... | collective-permute-start | bytes 393224 | tf_op jit(solution)/shard_map/ppermute | solution.py:33
  48.1 9.2 %collective-permute-start.22 = (bf16[256,512]{1,0:T(8,128)(2,1)S(1)}, bf16[256,512]{1,0:T(8,128)(2,1)S(1)}, u32[]{:S(2)}, u32[]{:S(2)}) collective-permute-start(bf16[256,512]{1,0:T(8,128)(2,1)S(1)} %shard_map.100.refs_10_), channel_id=1, source_target_pairs={{24,16},{28,20},{0,8},{4,12},{16,24},{20,28},{8,0},{12,4},{25,17},... | collective-permute-start | bytes 786440 | tf_op jit(solution)/shard_map/ppermute | solution.py:29
  49.1 13.2 %collective-permute-start.20 = (bf16[256,512]{1,0:T(8,128)(2,1)S(1)}, bf16[256,512]{1,0:T(8,128)(2,1)S(1)}, u32[]{:S(2)}, u32[]{:S(2)}) collective-permute-start(bf16[256,512]{1,0:T(8,128)(2,1)S(1)} %shard_map.100.refs_10_), channel_id=1, source_target_pairs={{16,8},{20,12},{8,16},{12,20},{0,4},{4,0},{24,28},{28,24},{17,9},{... | collective-permute-start | bytes 786440 | tf_op jit(solution)/shard_map/ppermute | solution.py:29
  50.9 11.4 %collective-permute-start.21 = (bf16[256,512]{1,0:T(8,128)(2,1)S(1)}, bf16[256,512]{1,0:T(8,128)(2,1)S(1)}, u32[]{:S(2)}, u32[]{:S(2)}) collective-permute-start(bf16[256,512]{1,0:T(8,128)(2,1)S(1)} %get-tuple-element.44), channel_id=1, source_target_pairs={{8,0},{12,4},{16,24},{20,28},{24,8},{28,12},{0,16},{4,20},{9,1},{1... | collective-permute-start | bytes 786440 | tf_op jit(solution)/shard_map/ppermute | solution.py:29
  57.4 11.7 %collective-permute-start.23 = (bf16[256,512]{1,0:T(8,128)(2,1)S(1)}, bf16[256,512]{1,0:T(8,128)(2,1)S(1)}, u32[]{:S(2)}, u32[]{:S(2)}) collective-permute-start(bf16[256,512]{1,0:T(8,128)(2,1)S(1)} %shard_map.103), channel_id=1, source_target_pairs={{16,0},{20,4},{8,24},{12,28},{0,8},{4,12},{24,16},{28,20},{17,1},{... | collective-permute-start | bytes 786440 | tf_op jit(solution)/shard_map/ppermute | solution.py:29
  (7 other events, 26.6 us)

commit v9 on v8

--- a/solution.py
+++ b/solution.py
@@ -237,8 +237,6 @@
         flops=work // 2,
         nbytes=4 << 20,
     )
-    others_t = other(after(others_t, own))
-    own = after(own, others_t)
     new_users, user_half = call(
         functools.partial(update, 4),
         (shape(share, depth, dtype=F32), shape(share, depth)),
@@ -247,6 +245,7 @@
         nbytes=3 << 20,
     )
 
+    others_t = other(after(others_t, user_half))
     shares = [user_half] + [swap(user_half, "ia", 4, k) for k in (1, 2, 3)]
     shares[1:3] = lax.optimization_barrier(tuple(shares[1:3]))
     shares += [other(x) for x in shares]

time: 71 us -> 71 us (level)
  transfers between devices with their start and end apart: 24 -> 24, of which waited for: 14 -> 13; matrix products, arithmetic and copies ran while one was open for 0% -> 0% of each run, Pallas kernels for 7% -> 7%
where the time goes in v9:
time: 71 us; the launch traced here: 70.8 us
  waiting for transfers between devices  37.8 us (53%)
  starting transfers between devices  18.8 us (26%)
  Pallas kernels  7.91 us (11%)
  local copies, waits for them, and re-layouts  3.74 us (5%)
  between operations  1.44 us (2%)
  other arithmetic  1.08 us (2%)
    ppermute x7, waiting for transfers between devices, send(): return lax.ppermute(x, 'au', perm)  20.6 us
    ppermute x16, waiting for transfers between devices, swap(): return lax.ppermute(x, axis, [(i, i ^ by) for i in range(n)])  13.4 us
    ppermute x16, starting transfers between devices, swap(): return lax.ppermute(x, axis, [(i, i ^ by) for i in range(n)])  8.78 us
    ppermute x7, starting transfers between devices, send(): return lax.ppermute(x, 'au', perm)  8.76 us
    pallas_call x9, Pallas kernels, call(): pl.pallas_call(kernel, out_shape=out_shape, in_specs=[SMEM] * smem + [VME...  6.19 us
    ppermute x1, waiting for transfers between devices, in_turns(): lax.ppermute(first, 'au', [(2 * a + core, 2 * b + core) for a, b in HANDE...  3.77 us
    unnamed x14, local copies, waits for them, and re-layouts  3.74 us
    pallas_call x1, Pallas kernels, in_turns(): pl.pallas_call(last_update, out_shape=shape(held, depth, dtype=F32), in_s...  1.72 us
  transfers between devices with their start and end apart: 24, of which 13 were waited for; matrix products, arithmetic and copies ran while one was open for 0% of the time, Pallas kernels for 7%

profile of v9, /device:TPU:0, one launch (start us, length us, event | category | flops | bytes accessed | tf_op | source)
XLA Modules:
  0.0 70.8 jit_solution(18252529145100807175)
XLA Ops:
  0.6 1.1 %convert_element_type.3.refs_0_ = bf16[256,512]{1,0:T(8,128)(2,1)S(1)} convert(f32[256,512]{1,0:T(8,128)} %emb.1) | non-fusion elementwise | flops 131072 | bytes 786432 | tf_op jit(solution)/shard_map/convert_element_type | solution.py:206
  1.7 4.1 %collective-permute-start.1 = (bf16[256,512]{1,0:T(8,128)(2,1)S(1)}, bf16[256,512]{1,0:T(8,128)(2,1)S(1)}, u32[]{:S(2)}, u32[]{:S(2)}) collective-permute-start(bf16[256,512]{1,0:T(8,128)(2,1)S(1)} %convert_element_type.3.refs_0_), channel_id=1, source_target_pairs={{0,16},{4,20},{24,8},{28,12},{8,0},{12,4},{16,24},{20,28},{1,17},{... | collective-permute-start | bytes 786440 | tf_op jit(solution)/shard_map/ppermute | solution.py:29
  6.5 1.4 %copy-done.1 = bf16[1,12,256,256]{3,2,1,0:T(8,128)(2,1)S(1)} copy-done((bf16[1,12,256,256]{3,2,1,0:T(8,128)(2,1)S(1)}, bf16[1,12,256,256]{3,2,1,0:T(8,128)(2,1)}, u32[]{:S(2)}) %copy-start.1) | copy-done | bytes 1572888
  11.0 1.2 %shard_map.96 = (bf16[1024,512]{1,0:T(8,128)(2,1)S(1)}, bf16[1024,512]{1,0:T(8,128)(2,1)S(1)}, f32[128,512]{1,0:T(8,128)S(1)}, bf16[1024,512]{1,0:T(8,128)(2,1)S(1)}, bf16[1024,512]{1,0:T(8,128)(2,1)S(1)}) custom-call(bf16[512,2048]{1,0:T(8,128)(2,1)S(1)} %shard_map.95.adj, f32[512,512]{1,0:T(8,128)S(1)} %copy-done.2, f32[512,512]{1,0:T(8,128)S(1)} %copy-done.3, ...), custom_call_target="tpu_custom_call" | custom-call | bytes 9437184 | tf_op jit(solution)/shard_map/pallas_call | solution.py:49
  12.5 1.3 %collective-permute-start.6 = (bf16[256,512]{1,0:T(8,128)(2,1)S(1)}, bf16[256,512]{1,0:T(8,128)(2,1)S(1)}, u32[]{:S(2)}, u32[]{:S(2)}) collective-permute-start(bf16[256,512]{1,0:T(8,128)(2,1)S(1)} %collective-permute-done.1.refs_2_), channel_id=1, source_target_pairs={{16,24},{20,28},{8,0},{12,4},{17,25},{21,29},{9,1},{13,5},{18,26},... | collective-permute-start | bytes 786440 | tf_op jit(solution)/shard_map/ppermute | solution.py:225
  14.4 5.7 %collective-permute-done.3.refs_4_ = bf16[256,512]{1,0:T(8,128)(2,1)S(1)} collective-permute-done((bf16[256,512]{1,0:T(8,128)(2,1)S(1)}, bf16[256,512]{1,0:T(8,128)(2,1)S(1)}, u32[]{:S(2)}, u32[]{:S(2)}) %collective-permute-start.3) | collective-permute-done | bytes 262176 | tf_op jit(solution)/shard_map/ppermute | solution.py:29
  20.6 3.8 %collective-permute-done.6.refs_7_ = bf16[256,512]{1,0:T(8,128)(2,1)S(1)} collective-permute-done((bf16[256,512]{1,0:T(8,128)(2,1)S(1)}, bf16[256,512]{1,0:T(8,128)(2,1)S(1)}, u32[]{:S(2)}, u32[]{:S(2)}) %collective-permute-start.6) | collective-permute-done | bytes 262176 | tf_op jit(solution)/shard_map/ppermute | solution.py:225
  24.4 1.1 %shard_map.97.early = f32[512,512]{1,0:T(8,128)S(1)} custom-call(bf16[512,2048]{1,0:T(8,128)(2,1)S(1)} %shard_map.95.adj, bf16[256,512]{1,0:T(8,128)(2,1)S(1)} %convert_element_type.3.refs_0_, bf16[256,512]{1,0:T(8,128)(2,1)S(1)} %collective-permute-done.refs_1_, bf16[256,512]{1,0:T(8,128)(2,1)S(1)} %collective-permute-done.1.refs_2_, ...), custom_call_target="tpu_custom_call" | custom-call | flops 536870912 | bytes 4194304 | tf_op jit(solution)/shard_map/pallas_call | solution.py:49
  26.2 1.7 %collective-permute-start.9 = (bf16[128,512]{1,0:T(8,128)(2,1)S(1)}, bf16[128,512]{1,0:T(8,128)(2,1)S(1)}, u32[]{:S(2)}, u32[]{:S(2)}) collective-permute-start(bf16[128,512]{1,0:T(8,128)(2,1)S(1)} %get-tuple-element.31), channel_id=1, source_target_pairs={{0,1},{1,0},{2,3},{3,2},{4,5},{5,4},{6,7},{7,6},{8,9},{9,8},{10,11... | collective-permute-start | bytes 393224 | tf_op jit(solution)/shard_map/ppermute | solution.py:33
  27.9 1.4 %collective-permute-start.10 = (bf16[128,512]{1,0:T(8,128)(2,1)S(1)}, bf16[128,512]{1,0:T(8,128)(2,1)S(1)}, u32[]{:S(2)}, u32[]{:S(2)}) collective-permute-start(bf16[128,512]{1,0:T(8,128)(2,1)S(1)} %get-tuple-element.32), channel_id=1, source_target_pairs={{0,2},{1,3},{2,0},{3,1},{4,6},{5,7},{6,4},{7,5},{8,10},{9,11},{10,... | collective-permute-start | bytes 393224 | tf_op jit(solution)/shard_map/ppermute | solution.py:33
  29.8 2.3 %collective-permute-done.9.refs_0_ = bf16[128,512]{1,0:T(8,128)(2,1)S(1)} collective-permute-done((bf16[128,512]{1,0:T(8,128)(2,1)S(1)}, bf16[128,512]{1,0:T(8,128)(2,1)S(1)}, u32[]{:S(2)}, u32[]{:S(2)}) %collective-permute-start.9) | collective-permute-done | bytes 131104 | tf_op jit(solution)/shard_map/ppermute | solution.py:33
  32.1 3.9 %collective-permute-done.10.refs_1_ = bf16[128,512]{1,0:T(8,128)(2,1)S(1)} collective-permute-done((bf16[128,512]{1,0:T(8,128)(2,1)S(1)}, bf16[128,512]{1,0:T(8,128)(2,1)S(1)}, u32[]{:S(2)}, u32[]{:S(2)}) %collective-permute-start.10) | collective-permute-done | bytes 131104 | tf_op jit(solution)/shard_map/ppermute | solution.py:33
  36.7 1.2 %collective-permute-start.13 = (bf16[128,512]{1,0:T(8,128)(2,1)S(1)}, bf16[128,512]{1,0:T(8,128)(2,1)S(1)}, u32[]{:S(2)}, u32[]{:S(2)}) collective-permute-start(bf16[128,512]{1,0:T(8,128)(2,1)S(1)} %get-tuple-element.35.refs_2_), channel_id=1, source_target_pairs={{0,1},{1,0},{2,3},{3,2},{4,5},{5,4},{6,7},{7,6},{8,9},{9,8},{10,11... | collective-permute-start | bytes 393224 | tf_op jit(solution)/shard_map/ppermute | solution.py:33
  38.7 1.5 %collective-permute-start.15 = (bf16[128,512]{1,0:T(8,128)(2,1)S(1)}, bf16[128,512]{1,0:T(8,128)(2,1)S(1)}, u32[]{:S(2)}, u32[]{:S(2)}) collective-permute-start(bf16[128,512]{1,0:T(8,128)(2,1)S(1)} %get-tuple-element.35.refs_2_), channel_id=1, source_target_pairs={{0,3},{1,2},{2,1},{3,0},{4,7},{5,6},{6,5},{7,4},{8,11},{9,10},{10,... | collective-permute-start | bytes 393224 | tf_op jit(solution)/shard_map/ppermute | solution.py:33
  40.2 2.8 %collective-permute-done.13.refs_3_ = bf16[128,512]{1,0:T(8,128)(2,1)S(1)} collective-permute-done((bf16[128,512]{1,0:T(8,128)(2,1)S(1)}, bf16[128,512]{1,0:T(8,128)(2,1)S(1)}, u32[]{:S(2)}, u32[]{:S(2)}) %collective-permute-start.13) | collective-permute-done | bytes 131104 | tf_op jit(solution)/shard_map/ppermute | solution.py:33
  44.4 1.9 %collective-permute-done.15.refs_5_ = bf16[128,512]{1,0:T(8,128)(2,1)S(1)} collective-permute-done((bf16[128,512]{1,0:T(8,128)(2,1)S(1)}, bf16[128,512]{1,0:T(8,128)(2,1)S(1)}, u32[]{:S(2)}, u32[]{:S(2)}) %collective-permute-start.15) | collective-permute-done | bytes 131104 | tf_op jit(solution)/shard_map/ppermute | solution.py:33
  46.2 1.3 %collective-permute-done.19.refs_9_ = bf16[128,512]{1,0:T(8,128)(2,1)S(1)} collective-permute-done((bf16[128,512]{1,0:T(8,128)(2,1)S(1)}, bf16[128,512]{1,0:T(8,128)(2,1)S(1)}, u32[]{:S(2)}, u32[]{:S(2)}) %collective-permute-start.19) | collective-permute-done | bytes 131104 | tf_op jit(solution)/shard_map/ppermute | solution.py:33
  48.0 1.0 %collective-permute-start.22 = (bf16[256,512]{1,0:T(8,128)(2,1)S(1)}, bf16[256,512]{1,0:T(8,128)(2,1)S(1)}, u32[]{:S(2)}, u32[]{:S(2)}) collective-permute-start(bf16[256,512]{1,0:T(8,128)(2,1)S(1)} %shard_map.100.refs_10_), channel_id=1, source_target_pairs={{24,16},{28,20},{0,8},{4,12},{16,24},{20,28},{8,0},{12,4},{25,17},... | collective-permute-start | bytes 786440 | tf_op jit(solution)/shard_map/ppermute | solution.py:29
  49.7 1.1 %shard_map.102 = (bf16[256,512]{1,0:T(8,128)(2,1)S(1)}, f32[128,512]{1,0:T(8,128)}) custom-call(bf16[1024,512]{1,0:T(8,128)(2,1)S(1)} %get-tuple-element.23.refs_0_, bf16[1024,512]{1,0:T(8,128)(2,1)S(1)} %collective-permute-done.12.refs_1_, bf16[128,512]{1,0:T(8,128)(2,1)S(1)} %get-tuple-element.35.refs_2_, ...), custom_call_target="tpu_custom_call" | custom-call | flops 268435456 | bytes 2097152 | tf_op jit(solution)/shard_map/pallas_call | solution.py:49
  50.8 2.5 %collective-permute-start.21 = (bf16[256,512]{1,0:T(8,128)(2,1)S(1)}, bf16[256,512]{1,0:T(8,128)(2,1)S(1)}, u32[]{:S(2)}, u32[]{:S(2)}) collective-permute-start(bf16[256,512]{1,0:T(8,128)(2,1)S(1)} %get-tuple-element.42), channel_id=1, source_target_pairs={{8,0},{12,4},{16,24},{20,28},{24,8},{28,12},{0,16},{4,20},{9,1},{1... | collective-permute-start | bytes 786440 | tf_op jit(solution)/shard_map/ppermute | solution.py:29
  53.4 3.9 %collective-permute-done.22.handed = bf16[256,512]{1,0:T(8,128)(2,1)S(1)} collective-permute-done((bf16[256,512]{1,0:T(8,128)(2,1)S(1)}, bf16[256,512]{1,0:T(8,128)(2,1)S(1)}, u32[]{:S(2)}, u32[]{:S(2)}) %collective-permute-start.22) | collective-permute-done | bytes 262176 | tf_op jit(solution)/shard_map/ppermute | solution.py:29
  58.3 3.9 %collective-permute-done.21.near = bf16[256,512]{1,0:T(8,128)(2,1)S(1)} collective-permute-done((bf16[256,512]{1,0:T(8,128)(2,1)S(1)}, bf16[256,512]{1,0:T(8,128)(2,1)S(1)}, u32[]{:S(2)}, u32[]{:S(2)}) %collective-permute-start.21) | collective-permute-done | bytes 262176 | tf_op jit(solution)/shard_map/ppermute | solution.py:29
  62.2 6.9 %collective-permute-done.23.onward = bf16[256,512]{1,0:T(8,128)(2,1)S(1)} collective-permute-done((bf16[256,512]{1,0:T(8,128)(2,1)S(1)}, bf16[256,512]{1,0:T(8,128)(2,1)S(1)}, u32[]{:S(2)}, u32[]{:S(2)}) %collective-permute-start.23) | collective-permute-done | bytes 262176 | tf_op jit(solution)/shard_map/ppermute | solution.py:29
  69.1 1.7 %shard_map.104 = f32[256,512]{1,0:T(8,128)} custom-call(f32[256,512]{1,0:T(8,128)S(1)} %copy-done, bf16[1024,512]{1,0:T(8,128)(2,1)S(1)} %get-tuple-element.26.w_hi, bf16[1024,512]{1,0:T(8,128)(2,1)S(1)} %get-tuple-element.27.w_lo, bf16[256,512]{1,0:T(8,128)(2,1)S(1)} %collective-permute-done.20.middle, f32[256,512]{1,0:T(8,128)S(1)} %get-tuple-element.39.refs_10_.own, ...), custom_call_target="tpu_custom_call" | custom-call | flops 805306368 | bytes 4194304 | tf_op jit(solution)/shard_map/pallas_call | solution.py:277
  (49 shorter events, 10.8 us)
Async XLA Ops:
  1.7 10.8 %collective-permute-start.1 = (bf16[256,512]{1,0:T(8,128)(2,1)S(1)}, bf16[256,512]{1,0:T(8,128)(2,1)S(1)}, u32[]{:S(2)}, u32[]{:S(2)}) collective-permute-start(bf16[256,512]{1,0:T(8,128)(2,1)S(1)} %convert_element_type.3.refs_0_), channel_id=1, source_target_pairs={{0,16},{4,20},{24,8},{28,12},{8,0},{12,4},{16,24},{20,28},{1,17},{... | collective-permute-start | bytes 786440 | tf_op jit(solution)/shard_map/ppermute | solution.py:29
  9.9 10.2 %collective-permute-start.3 = (bf16[256,512]{1,0:T(8,128)(2,1)S(1)}, bf16[256,512]{1,0:T(8,128)(2,1)S(1)}, u32[]{:S(2)}, u32[]{:S(2)}) collective-permute-start(bf16[256,512]{1,0:T(8,128)(2,1)S(1)} %convert_element_type.3.refs_0_), channel_id=1, source_target_pairs={{0,8},{4,12},{24,16},{28,20},{8,24},{12,28},{16,0},{20,4},{1,9},{5... | collective-permute-start | bytes 786440 | tf_op jit(solution)/shard_map/ppermute | solution.py:29
  12.2 7.9 %collective-permute-start.5 = (bf16[256,512]{1,0:T(8,128)(2,1)S(1)}, bf16[256,512]{1,0:T(8,128)(2,1)S(1)}, u32[]{:S(2)}, u32[]{:S(2)}) collective-permute-start(bf16[256,512]{1,0:T(8,128)(2,1)S(1)} %convert_element_type.3.refs_0_), channel_id=1, source_target_pairs={{8,16},{12,20},{16,8},{20,12},{0,4},{4,0},{24,28},{28,24},{9,17},{... | collective-permute-start | bytes 786440 | tf_op jit(solution)/shard_map/ppermute | solution.py:29
  12.5 11.9 %collective-permute-start.6 = (bf16[256,512]{1,0:T(8,128)(2,1)S(1)}, bf16[256,512]{1,0:T(8,128)(2,1)S(1)}, u32[]{:S(2)}, u32[]{:S(2)}) collective-permute-start(bf16[256,512]{1,0:T(8,128)(2,1)S(1)} %collective-permute-done.1.refs_2_), channel_id=1, source_target_pairs={{16,24},{20,28},{8,0},{12,4},{17,25},{21,29},{9,1},{13,5},{18,26},... | collective-permute-start | bytes 786440 | tf_op jit(solution)/shard_map/ppermute | solution.py:225
  13.8 10.6 %collective-permute-start = (bf16[256,512]{1,0:T(8,128)(2,1)S(1)}, bf16[256,512]{1,0:T(8,128)(2,1)S(1)}, u32[]{:S(2)}, u32[]{:S(2)}) collective-permute-start(bf16[256,512]{1,0:T(8,128)(2,1)S(1)} %convert_element_type.3.refs_0_), channel_id=1, source_target_pairs={{0,4},{4,0},{8,12},{12,8},{16,20},{20,16},{24,28},{28,24},{1,5},{5... | collective-permute-start | bytes 786440 | tf_op jit(solution)/shard_map/ppermute | solution.py:33
  14.1 10.3 %collective-permute-start.2 = (bf16[256,512]{1,0:T(8,128)(2,1)S(1)}, bf16[256,512]{1,0:T(8,128)(2,1)S(1)}, u32[]{:S(2)}, u32[]{:S(2)}) collective-permute-start(bf16[256,512]{1,0:T(8,128)(2,1)S(1)} %collective-permute-done.1.refs_2_), channel_id=1, source_target_pairs={{0,4},{4,0},{8,12},{12,8},{16,20},{20,16},{24,28},{28,24},{1,5},{5... | collective-permute-start | bytes 786440 | tf_op jit(solution)/shard_map/ppermute | solution.py:33
  20.1 4.3 %collective-permute-start.4 = (bf16[256,512]{1,0:T(8,128)(2,1)S(1)}, bf16[256,512]{1,0:T(8,128)(2,1)S(1)}, u32[]{:S(2)}, u32[]{:S(2)}) collective-permute-start(bf16[256,512]{1,0:T(8,128)(2,1)S(1)} %collective-permute-done.3.refs_4_), channel_id=1, source_target_pairs={{0,4},{4,0},{8,12},{12,8},{16,20},{20,16},{24,28},{28,24},{1,5},{5... | collective-permute-start | bytes 786440 | tf_op jit(solution)/shard_map/ppermute | solution.py:33
  20.1 5.4 %collective-permute-start.7 = (bf16[256,512]{1,0:T(8,128)(2,1)S(1)}, bf16[256,512]{1,0:T(8,128)(2,1)S(1)}, u32[]{:S(2)}, u32[]{:S(2)}) collective-permute-start(bf16[256,512]{1,0:T(8,128)(2,1)S(1)} %collective-permute-done.5.refs_6_), channel_id=1, source_target_pairs={{0,4},{4,0},{8,12},{12,8},{16,20},{20,16},{24,28},{28,24},{1,5},{5... | collective-permute-start | bytes 786440 | tf_op jit(solution)/shard_map/ppermute | solution.py:33
  24.4 1.5 %collective-permute-start.8 = (bf16[256,512]{1,0:T(8,128)(2,1)S(1)}, bf16[256,512]{1,0:T(8,128)(2,1)S(1)}, u32[]{:S(2)}, u32[]{:S(2)}) collective-permute-start(bf16[256,512]{1,0:T(8,128)(2,1)S(1)} %collective-permute-done.6.refs_7_), channel_id=1, source_target_pairs={{0,4},{4,0},{8,12},{12,8},{16,20},{20,16},{24,28},{28,24},{1,5},{5... | collective-permute-start | bytes 786440 | tf_op jit(solution)/shard_map/ppermute | solution.py:33
  26.2 5.9 %collective-permute-start.9 = (bf16[128,512]{1,0:T(8,128)(2,1)S(1)}, bf16[128,512]{1,0:T(8,128)(2,1)S(1)}, u32[]{:S(2)}, u32[]{:S(2)}) collective-permute-start(bf16[128,512]{1,0:T(8,128)(2,1)S(1)} %get-tuple-element.31), channel_id=1, source_target_pairs={{0,1},{1,0},{2,3},{3,2},{4,5},{5,4},{6,7},{7,6},{8,9},{9,8},{10,11... | collective-permute-start | bytes 393224 | tf_op jit(solution)/shard_map/ppermute | solution.py:33
  27.9 8.1 %collective-permute-start.10 = (bf16[128,512]{1,0:T(8,128)(2,1)S(1)}, bf16[128,512]{1,0:T(8,128)(2,1)S(1)}, u32[]{:S(2)}, u32[]{:S(2)}) collective-permute-start(bf16[128,512]{1,0:T(8,128)(2,1)S(1)} %get-tuple-element.32), channel_id=1, source_target_pairs={{0,2},{1,3},{2,0},{3,1},{4,6},{5,7},{6,4},{7,5},{8,10},{9,11},{10,... | collective-permute-start | bytes 393224 | tf_op jit(solution)/shard_map/ppermute | solution.py:33
  29.3 6.7 %collective-permute-start.11 = (bf16[128,512]{1,0:T(8,128)(2,1)S(1)}, bf16[128,512]{1,0:T(8,128)(2,1)S(1)}, u32[]{:S(2)}, u32[]{:S(2)}) collective-permute-start(bf16[128,512]{1,0:T(8,128)(2,1)S(1)} %get-tuple-element.33), channel_id=1, source_target_pairs={{0,3},{1,2},{2,1},{3,0},{4,7},{5,6},{6,5},{7,4},{8,11},{9,10},{10,... | collective-permute-start | bytes 393224 | tf_op jit(solution)/shard_map/ppermute | solution.py:33
  36.6 11.0 %collective-permute-start.12 = (bf16[1024,512]{1,0:T(8,128)(2,1)S(1)}, bf16[1024,512]{1,0:T(8,128)(2,1)S(1)}, u32[]{:S(2)}, u32[]{:S(2)}) collective-permute-start(bf16[1024,512]{1,0:T(8,128)(2,1)S(1)} %get-tuple-element.36), channel_id=1, source_target_pairs={{0,4},{4,0},{8,12},{12,8},{16,20},{20,16},{24,28},{28,24},{1,5},{5... | collective-permute-start | bytes 3145736 | tf_op jit(solution)/shard_map/ppermute | solution.py:33
  36.7 6.4 %collective-permute-start.13 = (bf16[128,512]{1,0:T(8,128)(2,1)S(1)}, bf16[128,512]{1,0:T(8,128)(2,1)S(1)}, u32[]{:S(2)}, u32[]{:S(2)}) collective-permute-start(bf16[128,512]{1,0:T(8,128)(2,1)S(1)} %get-tuple-element.35.refs_2_), channel_id=1, source_target_pairs={{0,1},{1,0},{2,3},{3,2},{4,5},{5,4},{6,7},{7,6},{8,9},{9,8},{10,11... | collective-permute-start | bytes 393224 | tf_op jit(solution)/shard_map/ppermute | solution.py:33
  37.8 6.0 %collective-permute-start.14 = (bf16[128,512]{1,0:T(8,128)(2,1)S(1)}, bf16[128,512]{1,0:T(8,128)(2,1)S(1)}, u32[]{:S(2)}, u32[]{:S(2)}) collective-permute-start(bf16[128,512]{1,0:T(8,128)(2,1)S(1)} %get-tuple-element.35.refs_2_), channel_id=1, source_target_pairs={{0,2},{1,3},{2,0},{3,1},{4,6},{5,7},{6,4},{7,5},{8,10},{9,11},{10,... | collective-permute-start | bytes 393224 | tf_op jit(solution)/shard_map/ppermute | solution.py:33
  38.7 7.6 %collective-permute-start.15 = (bf16[128,512]{1,0:T(8,128)(2,1)S(1)}, bf16[128,512]{1,0:T(8,128)(2,1)S(1)}, u32[]{:S(2)}, u32[]{:S(2)}) collective-permute-start(bf16[128,512]{1,0:T(8,128)(2,1)S(1)} %get-tuple-element.35.refs_2_), channel_id=1, source_target_pairs={{0,3},{1,2},{2,1},{3,0},{4,7},{5,6},{6,5},{7,4},{8,11},{9,10},{10,... | collective-permute-start | bytes 393224 | tf_op jit(solution)/shard_map/ppermute | solution.py:33
  40.2 6.0 %collective-permute-start.16 = (bf16[128,512]{1,0:T(8,128)(2,1)S(1)}, bf16[128,512]{1,0:T(8,128)(2,1)S(1)}, u32[]{:S(2)}, u32[]{:S(2)}) collective-permute-start(bf16[128,512]{1,0:T(8,128)(2,1)S(1)} %get-tuple-element.35.refs_2_), channel_id=1, source_target_pairs={{0,4},{4,0},{8,12},{12,8},{16,20},{20,16},{24,28},{28,24},{1,5},{5... | collective-permute-start | bytes 393224 | tf_op jit(solution)/shard_map/ppermute | solution.py:33
  43.9 2.4 %collective-permute-start.17 = (bf16[128,512]{1,0:T(8,128)(2,1)S(1)}, bf16[128,512]{1,0:T(8,128)(2,1)S(1)}, u32[]{:S(2)}, u32[]{:S(2)}) collective-permute-start(bf16[128,512]{1,0:T(8,128)(2,1)S(1)} %collective-permute-done.13.refs_3_), channel_id=1, source_target_pairs={{0,4},{4,0},{8,12},{12,8},{16,20},{20,16},{24,28},{28,24},{1,5},{5... | collective-permute-start | bytes 393224 | tf_op jit(solution)/shard_map/ppermute | solution.py:33
  43.9 2.4 %collective-permute-start.18 = (bf16[128,512]{1,0:T(8,128)(2,1)S(1)}, bf16[128,512]{1,0:T(8,128)(2,1)S(1)}, u32[]{:S(2)}, u32[]{:S(2)}) collective-permute-start(bf16[128,512]{1,0:T(8,128)(2,1)S(1)} %collective-permute-done.14.refs_4_), channel_id=1, source_target_pairs={{0,4},{4,0},{8,12},{12,8},{16,20},{20,16},{24,28},{28,24},{1,5},{5... | collective-permute-start | bytes 393224 | tf_op jit(solution)/shard_map/ppermute | solution.py:33
  46.2 1.3 %collective-permute-start.19 = (bf16[128,512]{1,0:T(8,128)(2,1)S(1)}, bf16[128,512]{1,0:T(8,128)(2,1)S(1)}, u32[]{:S(2)}, u32[]{:S(2)}) collective-permute-start(bf16[128,512]{1,0:T(8,128)(2,1)S(1)} %collective-permute-done.15.refs_5_), channel_id=1, source_target_pairs={{0,4},{4,0},{8,12},{12,8},{16,20},{20,16},{24,28},{28,24},{1,5},{5... | collective-permute-start | bytes 393224 | tf_op jit(solution)/shard_map/ppermute | solution.py:33
  48.0 9.2 %collective-permute-start.22 = (bf16[256,512]{1,0:T(8,128)(2,1)S(1)}, bf16[256,512]{1,0:T(8,128)(2,1)S(1)}, u32[]{:S(2)}, u32[]{:S(2)}) collective-permute-start(bf16[256,512]{1,0:T(8,128)(2,1)S(1)} %shard_map.100.refs_10_), channel_id=1, source_target_pairs={{24,16},{28,20},{0,8},{4,12},{16,24},{20,28},{8,0},{12,4},{25,17},... | collective-permute-start | bytes 786440 | tf_op jit(solution)/shard_map/ppermute | solution.py:29
  49.0 9.3 %collective-permute-start.20 = (bf16[256,512]{1,0:T(8,128)(2,1)S(1)}, bf16[256,512]{1,0:T(8,128)(2,1)S(1)}, u32[]{:S(2)}, u32[]{:S(2)}) collective-permute-start(bf16[256,512]{1,0:T(8,128)(2,1)S(1)} %shard_map.100.refs_10_), channel_id=1, source_target_pairs={{16,8},{20,12},{8,16},{12,20},{0,4},{4,0},{24,28},{28,24},{17,9},{... | collective-permute-start | bytes 786440 | tf_op jit(solution)/shard_map/ppermute | solution.py:29
  50.8 11.3 %collective-permute-start.21 = (bf16[256,512]{1,0:T(8,128)(2,1)S(1)}, bf16[256,512]{1,0:T(8,128)(2,1)S(1)}, u32[]{:S(2)}, u32[]{:S(2)}) collective-permute-start(bf16[256,512]{1,0:T(8,128)(2,1)S(1)} %get-tuple-element.42), channel_id=1, source_target_pairs={{8,0},{12,4},{16,24},{20,28},{24,8},{28,12},{0,16},{4,20},{9,1},{1... | collective-permute-start | bytes 786440 | tf_op jit(solution)/shard_map/ppermute | solution.py:29
  57.3 11.8 %collective-permute-start.23 = (bf16[256,512]{1,0:T(8,128)(2,1)S(1)}, bf16[256,512]{1,0:T(8,128)(2,1)S(1)}, u32[]{:S(2)}, u32[]{:S(2)}) collective-permute-start(bf16[256,512]{1,0:T(8,128)(2,1)S(1)} %shard_map.103), channel_id=1, source_target_pairs={{16,0},{20,4},{8,24},{12,28},{0,8},{4,12},{24,16},{28,20},{17,1},{... | collective-permute-start | bytes 786440 | tf_op jit(solution)/shard_map/ppermute | solution.py:29
  (7 other events, 26.7 us)

commit v10 on v8

--- a/solution.py
+++ b/solution.py
@@ -212,7 +212,7 @@
         smem=3,
         nbytes=8 << 20,
     )
-    second = send(after(mine, adj), TURN_2)
+    second = send(mine, TURN_2)
     w_hi, w_lo, own_emb, adj_t, others_t = call(
         functools.partial(ready, held),
         (shape(2 * depth, depth), shape(2 * depth, depth), shape(share, depth, dtype=F32))

time: 71 us -> 71 us (level)
    ppermute x1, waiting for transfers between devices: 3.63 us -> 4.99 us  [in_turns(): lax.ppermute(first, 'au', [(2 * a + core, 2 * b + core) for a, b in HANDE...]
    ppermute x7, waiting for transfers between devices: 20.7 us -> 19.4 us  [send(): return lax.ppermute(x, 'au', perm)]
where the time goes in v10:
time: 71 us; the launch traced here: 70.7 us
  waiting for transfers between devices  37.7 us (53%)
  starting transfers between devices  18.9 us (27%)
  Pallas kernels  7.94 us (11%)
  local copies, waits for them, and re-layouts  3.78 us (5%)
  between operations  1.41 us (2%)
  other arithmetic  1.08 us (2%)
    ppermute x7, waiting for transfers between devices, send(): return lax.ppermute(x, 'au', perm)  19.4 us
    ppermute x16, waiting for transfers between devices, swap(): return lax.ppermute(x, axis, [(i, i ^ by) for i in range(n)])  13.3 us
    ppermute x16, starting transfers between devices, swap(): return lax.ppermute(x, axis, [(i, i ^ by) for i in range(n)])  8.87 us
    ppermute x7, starting transfers between devices, send(): return lax.ppermute(x, 'au', perm)  8.71 us
    pallas_call x9, Pallas kernels, call(): pl.pallas_call(kernel, out_shape=out_shape, in_specs=[SMEM] * smem + [VME...  6.23 us
    ppermute x1, waiting for transfers between devices, in_turns(): lax.ppermute(first, 'au', [(2 * a + core, 2 * b + core) for a, b in HANDE...  4.99 us
    unnamed x14, local copies, waits for them, and re-layouts  3.78 us
    pallas_call x1, Pallas kernels, in_turns(): pl.pallas_call(last_update, out_shape=shape(held, depth, dtype=F32), in_s...  1.72 us
  transfers between devices with their start and end apart: 24, of which 14 were waited for; matrix products, arithmetic and copies ran while one was open for 0% of the time, Pallas kernels for 7%

profile of v10, /device:TPU:0, one launch (start us, length us, event | category | flops | bytes accessed | tf_op | source)
XLA Modules:
  0.0 70.7 jit_solution(9748043917666337319)
XLA Ops:
  0.6 1.1 %convert_element_type.3.refs_0_ = bf16[256,512]{1,0:T(8,128)(2,1)S(1)} convert(f32[256,512]{1,0:T(8,128)} %emb.1) | non-fusion elementwise | flops 131072 | bytes 786432 | tf_op jit(solution)/shard_map/convert_element_type | solution.py:206
  1.7 4.1 %collective-permute-start.1 = (bf16[256,512]{1,0:T(8,128)(2,1)S(1)}, bf16[256,512]{1,0:T(8,128)(2,1)S(1)}, u32[]{:S(2)}, u32[]{:S(2)}) collective-permute-start(bf16[256,512]{1,0:T(8,128)(2,1)S(1)} %convert_element_type.3.refs_0_), channel_id=1, source_target_pairs={{0,16},{4,20},{24,8},{28,12},{8,0},{12,4},{16,24},{20,28},{1,17},{... | collective-permute-start | bytes 786440 | tf_op jit(solution)/shard_map/ppermute | solution.py:29
  6.5 1.4 %copy-done.1 = bf16[1,12,256,256]{3,2,1,0:T(8,128)(2,1)S(1)} copy-done((bf16[1,12,256,256]{3,2,1,0:T(8,128)(2,1)S(1)}, bf16[1,12,256,256]{3,2,1,0:T(8,128)(2,1)}, u32[]{:S(2)}) %copy-start.1) | copy-done | bytes 1572888
  11.0 1.2 %shard_map.96 = (bf16[1024,512]{1,0:T(8,128)(2,1)S(1)}, bf16[1024,512]{1,0:T(8,128)(2,1)S(1)}, f32[128,512]{1,0:T(8,128)S(1)}, bf16[1024,512]{1,0:T(8,128)(2,1)S(1)}, bf16[1024,512]{1,0:T(8,128)(2,1)S(1)}) custom-call(bf16[512,2048]{1,0:T(8,128)(2,1)S(1)} %shard_map.95.adj, f32[512,512]{1,0:T(8,128)S(1)} %copy-done.2, f32[512,512]{1,0:T(8,128)S(1)} %copy-done.3, ...), custom_call_target="tpu_custom_call" | custom-call | bytes 9437184 | tf_op jit(solution)/shard_map/pallas_call | solution.py:49
  12.6 1.3 %collective-permute-start.6 = (bf16[256,512]{1,0:T(8,128)(2,1)S(1)}, bf16[256,512]{1,0:T(8,128)(2,1)S(1)}, u32[]{:S(2)}, u32[]{:S(2)}) collective-permute-start(bf16[256,512]{1,0:T(8,128)(2,1)S(1)} %collective-permute-done.1.refs_2_), channel_id=1, source_target_pairs={{16,24},{20,28},{8,0},{12,4},{17,25},{21,29},{9,1},{13,5},{18,26},... | collective-permute-start | bytes 786440 | tf_op jit(solution)/shard_map/ppermute | solution.py:225
  14.4 4.5 %collective-permute-done.3.refs_4_ = bf16[256,512]{1,0:T(8,128)(2,1)S(1)} collective-permute-done((bf16[256,512]{1,0:T(8,128)(2,1)S(1)}, bf16[256,512]{1,0:T(8,128)(2,1)S(1)}, u32[]{:S(2)}, u32[]{:S(2)}) %collective-permute-start.3) | collective-permute-done | bytes 262176 | tf_op jit(solution)/shard_map/ppermute | solution.py:29
  19.4 5.0 %collective-permute-done.6.refs_7_ = bf16[256,512]{1,0:T(8,128)(2,1)S(1)} collective-permute-done((bf16[256,512]{1,0:T(8,128)(2,1)S(1)}, bf16[256,512]{1,0:T(8,128)(2,1)S(1)}, u32[]{:S(2)}, u32[]{:S(2)}) %collective-permute-start.6) | collective-permute-done | bytes 262176 | tf_op jit(solution)/shard_map/ppermute | solution.py:225
  24.4 1.1 %shard_map.97.early = f32[512,512]{1,0:T(8,128)S(1)} custom-call(bf16[512,2048]{1,0:T(8,128)(2,1)S(1)} %shard_map.95.adj, bf16[256,512]{1,0:T(8,128)(2,1)S(1)} %convert_element_type.3.refs_0_, bf16[256,512]{1,0:T(8,128)(2,1)S(1)} %collective-permute-done.refs_1_, bf16[256,512]{1,0:T(8,128)(2,1)S(1)} %collective-permute-done.1.refs_2_, ...), custom_call_target="tpu_custom_call" | custom-call | flops 536870912 | bytes 4194304 | tf_op jit(solution)/shard_map/pallas_call | solution.py:49
  26.5 1.5 %collective-permute-start.10 = (bf16[128,512]{1,0:T(8,128)(2,1)S(1)}, bf16[128,512]{1,0:T(8,128)(2,1)S(1)}, u32[]{:S(2)}, u32[]{:S(2)}) collective-permute-start(bf16[128,512]{1,0:T(8,128)(2,1)S(1)} %get-tuple-element.32), channel_id=1, source_target_pairs={{0,1},{1,0},{2,3},{3,2},{4,5},{5,4},{6,7},{7,6},{8,9},{9,8},{10,11... | collective-permute-start | bytes 393224 | tf_op jit(solution)/shard_map/ppermute | solution.py:33
  28.0 1.5 %collective-permute-start.11 = (bf16[128,512]{1,0:T(8,128)(2,1)S(1)}, bf16[128,512]{1,0:T(8,128)(2,1)S(1)}, u32[]{:S(2)}, u32[]{:S(2)}) collective-permute-start(bf16[128,512]{1,0:T(8,128)(2,1)S(1)} %get-tuple-element.33), channel_id=1, source_target_pairs={{0,2},{1,3},{2,0},{3,1},{4,6},{5,7},{6,4},{7,5},{8,10},{9,11},{10,... | collective-permute-start | bytes 393224 | tf_op jit(solution)/shard_map/ppermute | solution.py:33
  30.0 2.6 %collective-permute-done.10.refs_0_ = bf16[128,512]{1,0:T(8,128)(2,1)S(1)} collective-permute-done((bf16[128,512]{1,0:T(8,128)(2,1)S(1)}, bf16[128,512]{1,0:T(8,128)(2,1)S(1)}, u32[]{:S(2)}, u32[]{:S(2)}) %collective-permute-start.10) | collective-permute-done | bytes 131104 | tf_op jit(solution)/shard_map/ppermute | solution.py:33
  32.6 3.7 %collective-permute-done.11.refs_1_ = bf16[128,512]{1,0:T(8,128)(2,1)S(1)} collective-permute-done((bf16[128,512]{1,0:T(8,128)(2,1)S(1)}, bf16[128,512]{1,0:T(8,128)(2,1)S(1)}, u32[]{:S(2)}, u32[]{:S(2)}) %collective-permute-start.11) | collective-permute-done | bytes 131104 | tf_op jit(solution)/shard_map/ppermute | solution.py:33
  36.8 1.3 %collective-permute-start.13 = (bf16[128,512]{1,0:T(8,128)(2,1)S(1)}, bf16[128,512]{1,0:T(8,128)(2,1)S(1)}, u32[]{:S(2)}, u32[]{:S(2)}) collective-permute-start(bf16[128,512]{1,0:T(8,128)(2,1)S(1)} %get-tuple-element.36.refs_2_), channel_id=1, source_target_pairs={{0,1},{1,0},{2,3},{3,2},{4,5},{5,4},{6,7},{7,6},{8,9},{9,8},{10,11... | collective-permute-start | bytes 393224 | tf_op jit(solution)/shard_map/ppermute | solution.py:33
  39.0 1.4 %collective-permute-start.15 = (bf16[128,512]{1,0:T(8,128)(2,1)S(1)}, bf16[128,512]{1,0:T(8,128)(2,1)S(1)}, u32[]{:S(2)}, u32[]{:S(2)}) collective-permute-start(bf16[128,512]{1,0:T(8,128)(2,1)S(1)} %get-tuple-element.36.refs_2_), channel_id=1, source_target_pairs={{0,3},{1,2},{2,1},{3,0},{4,7},{5,6},{6,5},{7,4},{8,11},{9,10},{10,... | collective-permute-start | bytes 393224 | tf_op jit(solution)/shard_map/ppermute | solution.py:33
  40.4 2.2 %collective-permute-done.13.refs_3_ = bf16[128,512]{1,0:T(8,128)(2,1)S(1)} collective-permute-done((bf16[128,512]{1,0:T(8,128)(2,1)S(1)}, bf16[128,512]{1,0:T(8,128)(2,1)S(1)}, u32[]{:S(2)}, u32[]{:S(2)}) %collective-permute-start.13) | collective-permute-done | bytes 131104 | tf_op jit(solution)/shard_map/ppermute | solution.py:33
  42.6 3.0 %collective-permute-done.14.refs_4_ = bf16[128,512]{1,0:T(8,128)(2,1)S(1)} collective-permute-done((bf16[128,512]{1,0:T(8,128)(2,1)S(1)}, bf16[128,512]{1,0:T(8,128)(2,1)S(1)}, u32[]{:S(2)}, u32[]{:S(2)}) %collective-permute-start.14) | collective-permute-done | bytes 131104 | tf_op jit(solution)/shard_map/ppermute | solution.py:33
  47.9 1.0 %collective-permute-start.22 = (bf16[256,512]{1,0:T(8,128)(2,1)S(1)}, bf16[256,512]{1,0:T(8,128)(2,1)S(1)}, u32[]{:S(2)}, u32[]{:S(2)}) collective-permute-start(bf16[256,512]{1,0:T(8,128)(2,1)S(1)} %shard_map.100.refs_10_), channel_id=1, source_target_pairs={{24,16},{28,20},{0,8},{4,12},{16,24},{20,28},{8,0},{12,4},{25,17},... | collective-permute-start | bytes 786440 | tf_op jit(solution)/shard_map/ppermute | solution.py:29
  49.7 1.1 %shard_map.102 = (bf16[256,512]{1,0:T(8,128)(2,1)S(1)}, f32[128,512]{1,0:T(8,128)}) custom-call(bf16[1024,512]{1,0:T(8,128)(2,1)S(1)} %get-tuple-element.23.refs_0_, bf16[1024,512]{1,0:T(8,128)(2,1)S(1)} %collective-permute-done.9.refs_1_, bf16[128,512]{1,0:T(8,128)(2,1)S(1)} %get-tuple-element.36.refs_2_, ...), custom_call_target="tpu_custom_call" | custom-call | flops 268435456 | bytes 2097152 | tf_op jit(solution)/shard_map/pallas_call | solution.py:49
  50.7 2.5 %collective-permute-start.21 = (bf16[256,512]{1,0:T(8,128)(2,1)S(1)}, bf16[256,512]{1,0:T(8,128)(2,1)S(1)}, u32[]{:S(2)}, u32[]{:S(2)}) collective-permute-start(bf16[256,512]{1,0:T(8,128)(2,1)S(1)} %get-tuple-element.42), channel_id=1, source_target_pairs={{8,0},{12,4},{16,24},{20,28},{24,8},{28,12},{0,16},{4,20},{9,1},{1... | collective-permute-start | bytes 786440 | tf_op jit(solution)/shard_map/ppermute | solution.py:29
  53.3 3.9 %collective-permute-done.22.handed = bf16[256,512]{1,0:T(8,128)(2,1)S(1)} collective-permute-done((bf16[256,512]{1,0:T(8,128)(2,1)S(1)}, bf16[256,512]{1,0:T(8,128)(2,1)S(1)}, u32[]{:S(2)}, u32[]{:S(2)}) %collective-permute-start.22) | collective-permute-done | bytes 262176 | tf_op jit(solution)/shard_map/ppermute | solution.py:29
  57.2 1.0 %collective-permute-start.23 = (bf16[256,512]{1,0:T(8,128)(2,1)S(1)}, bf16[256,512]{1,0:T(8,128)(2,1)S(1)}, u32[]{:S(2)}, u32[]{:S(2)}) collective-permute-start(bf16[256,512]{1,0:T(8,128)(2,1)S(1)} %shard_map.103), channel_id=1, source_target_pairs={{16,0},{20,4},{8,24},{12,28},{0,8},{4,12},{24,16},{28,20},{17,1},{... | collective-permute-start | bytes 786440 | tf_op jit(solution)/shard_map/ppermute | solution.py:29
  58.2 3.9 %collective-permute-done.21.near = bf16[256,512]{1,0:T(8,128)(2,1)S(1)} collective-permute-done((bf16[256,512]{1,0:T(8,128)(2,1)S(1)}, bf16[256,512]{1,0:T(8,128)(2,1)S(1)}, u32[]{:S(2)}, u32[]{:S(2)}) %collective-permute-start.21) | collective-permute-done | bytes 262176 | tf_op jit(solution)/shard_map/ppermute | solution.py:29
  62.1 6.9 %collective-permute-done.23.onward = bf16[256,512]{1,0:T(8,128)(2,1)S(1)} collective-permute-done((bf16[256,512]{1,0:T(8,128)(2,1)S(1)}, bf16[256,512]{1,0:T(8,128)(2,1)S(1)}, u32[]{:S(2)}, u32[]{:S(2)}) %collective-permute-start.23) | collective-permute-done | bytes 262176 | tf_op jit(solution)/shard_map/ppermute | solution.py:29
  69.0 1.7 %shard_map.104 = f32[256,512]{1,0:T(8,128)} custom-call(f32[256,512]{1,0:T(8,128)S(1)} %copy-done, bf16[1024,512]{1,0:T(8,128)(2,1)S(1)} %get-tuple-element.25.w_hi, bf16[1024,512]{1,0:T(8,128)(2,1)S(1)} %get-tuple-element.31.w_lo, bf16[256,512]{1,0:T(8,128)(2,1)S(1)} %collective-permute-done.20.middle, f32[256,512]{1,0:T(8,128)S(1)} %get-tuple-element.39.refs_10_.own, ...), custom_call_target="tpu_custom_call" | custom-call | flops 805306368 | bytes 4194304 | tf_op jit(solution)/shard_map/pallas_call | solution.py:278
  (49 shorter events, 10.5 us)
Async XLA Ops:
  1.7 10.8 %collective-permute-start.1 = (bf16[256,512]{1,0:T(8,128)(2,1)S(1)}, bf16[256,512]{1,0:T(8,128)(2,1)S(1)}, u32[]{:S(2)}, u32[]{:S(2)}) collective-permute-start(bf16[256,512]{1,0:T(8,128)(2,1)S(1)} %convert_element_type.3.refs_0_), channel_id=1, source_target_pairs={{0,16},{4,20},{24,8},{28,12},{8,0},{12,4},{16,24},{20,28},{1,17},{... | collective-permute-start | bytes 786440 | tf_op jit(solution)/shard_map/ppermute | solution.py:29
  5.8 13.1 %collective-permute-start.3 = (bf16[256,512]{1,0:T(8,128)(2,1)S(1)}, bf16[256,512]{1,0:T(8,128)(2,1)S(1)}, u32[]{:S(2)}, u32[]{:S(2)}) collective-permute-start(bf16[256,512]{1,0:T(8,128)(2,1)S(1)} %convert_element_type.3.refs_0_), channel_id=1, source_target_pairs={{0,8},{4,12},{24,16},{28,20},{8,24},{12,28},{16,0},{20,4},{1,9},{5... | collective-permute-start | bytes 786440 | tf_op jit(solution)/shard_map/ppermute | solution.py:29
  12.2 6.7 %collective-permute-start.5 = (bf16[256,512]{1,0:T(8,128)(2,1)S(1)}, bf16[256,512]{1,0:T(8,128)(2,1)S(1)}, u32[]{:S(2)}, u32[]{:S(2)}) collective-permute-start(bf16[256,512]{1,0:T(8,128)(2,1)S(1)} %convert_element_type.3.refs_0_), channel_id=1, source_target_pairs={{8,16},{12,20},{16,8},{20,12},{0,4},{4,0},{24,28},{28,24},{9,17},{... | collective-permute-start | bytes 786440 | tf_op jit(solution)/shard_map/ppermute | solution.py:29
  12.6 11.8 %collective-permute-start.6 = (bf16[256,512]{1,0:T(8,128)(2,1)S(1)}, bf16[256,512]{1,0:T(8,128)(2,1)S(1)}, u32[]{:S(2)}, u32[]{:S(2)}) collective-permute-start(bf16[256,512]{1,0:T(8,128)(2,1)S(1)} %collective-permute-done.1.refs_2_), channel_id=1, source_target_pairs={{16,24},{20,28},{8,0},{12,4},{17,25},{21,29},{9,1},{13,5},{18,26},... | collective-permute-start | bytes 786440 | tf_op jit(solution)/shard_map/ppermute | solution.py:225
  13.8 10.6 %collective-permute-start = (bf16[256,512]{1,0:T(8,128)(2,1)S(1)}, bf16[256,512]{1,0:T(8,128)(2,1)S(1)}, u32[]{:S(2)}, u32[]{:S(2)}) collective-permute-start(bf16[256,512]{1,0:T(8,128)(2,1)S(1)} %convert_element_type.3.refs_0_), channel_id=1, source_target_pairs={{0,4},{4,0},{8,12},{12,8},{16,20},{20,16},{24,28},{28,24},{1,5},{5... | collective-permute-start | bytes 786440 | tf_op jit(solution)/shard_map/ppermute | solution.py:33
  14.1 10.3 %collective-permute-start.2 = (bf16[256,512]{1,0:T(8,128)(2,1)S(1)}, bf16[256,512]{1,0:T(8,128)(2,1)S(1)}, u32[]{:S(2)}, u32[]{:S(2)}) collective-permute-start(bf16[256,512]{1,0:T(8,128)(2,1)S(1)} %collective-permute-done.1.refs_2_), channel_id=1, source_target_pairs={{0,4},{4,0},{8,12},{12,8},{16,20},{20,16},{24,28},{28,24},{1,5},{5... | collective-permute-start | bytes 786440 | tf_op jit(solution)/shard_map/ppermute | solution.py:33
  18.9 5.5 %collective-permute-start.4 = (bf16[256,512]{1,0:T(8,128)(2,1)S(1)}, bf16[256,512]{1,0:T(8,128)(2,1)S(1)}, u32[]{:S(2)}, u32[]{:S(2)}) collective-permute-start(bf16[256,512]{1,0:T(8,128)(2,1)S(1)} %collective-permute-done.3.refs_4_), channel_id=1, source_target_pairs={{0,4},{4,0},{8,12},{12,8},{16,20},{20,16},{24,28},{28,24},{1,5},{5... | collective-permute-start | bytes 786440 | tf_op jit(solution)/shard_map/ppermute | solution.py:33
  18.9 6.6 %collective-permute-start.7 = (bf16[256,512]{1,0:T(8,128)(2,1)S(1)}, bf16[256,512]{1,0:T(8,128)(2,1)S(1)}, u32[]{:S(2)}, u32[]{:S(2)}) collective-permute-start(bf16[256,512]{1,0:T(8,128)(2,1)S(1)} %collective-permute-done.5.refs_6_), channel_id=1, source_target_pairs={{0,4},{4,0},{8,12},{12,8},{16,20},{20,16},{24,28},{28,24},{1,5},{5... | collective-permute-start | bytes 786440 | tf_op jit(solution)/shard_map/ppermute | solution.py:33
  24.4 1.5 %collective-permute-start.8 = (bf16[256,512]{1,0:T(8,128)(2,1)S(1)}, bf16[256,512]{1,0:T(8,128)(2,1)S(1)}, u32[]{:S(2)}, u32[]{:S(2)}) collective-permute-start(bf16[256,512]{1,0:T(8,128)(2,1)S(1)} %collective-permute-done.6.refs_7_), channel_id=1, source_target_pairs={{0,4},{4,0},{8,12},{12,8},{16,20},{20,16},{24,28},{28,24},{1,5},{5... | collective-permute-start | bytes 786440 | tf_op jit(solution)/shard_map/ppermute | solution.py:33
  26.3 3.7 %collective-permute-start.9 = (bf16[1024,512]{1,0:T(8,128)(2,1)S(1)}, bf16[1024,512]{1,0:T(8,128)(2,1)S(1)}, u32[]{:S(2)}, u32[]{:S(2)}) collective-permute-start(bf16[1024,512]{1,0:T(8,128)(2,1)S(1)} %get-tuple-element.29), channel_id=1, source_target_pairs={{0,4},{4,0},{8,12},{12,8},{16,20},{20,16},{24,28},{28,24},{1,5},{5... | collective-permute-start | bytes 3145736 | tf_op jit(solution)/shard_map/ppermute | solution.py:33
  26.5 6.1 %collective-permute-start.10 = (bf16[128,512]{1,0:T(8,128)(2,1)S(1)}, bf16[128,512]{1,0:T(8,128)(2,1)S(1)}, u32[]{:S(2)}, u32[]{:S(2)}) collective-permute-start(bf16[128,512]{1,0:T(8,128)(2,1)S(1)} %get-tuple-element.32), channel_id=1, source_target_pairs={{0,1},{1,0},{2,3},{3,2},{4,5},{5,4},{6,7},{7,6},{8,9},{9,8},{10,11... | collective-permute-start | bytes 393224 | tf_op jit(solution)/shard_map/ppermute | solution.py:33
  28.0 8.3 %collective-permute-start.11 = (bf16[128,512]{1,0:T(8,128)(2,1)S(1)}, bf16[128,512]{1,0:T(8,128)(2,1)S(1)}, u32[]{:S(2)}, u32[]{:S(2)}) collective-permute-start(bf16[128,512]{1,0:T(8,128)(2,1)S(1)} %get-tuple-element.33), channel_id=1, source_target_pairs={{0,2},{1,3},{2,0},{3,1},{4,6},{5,7},{6,4},{7,5},{8,10},{9,11},{10,... | collective-permute-start | bytes 393224 | tf_op jit(solution)/shard_map/ppermute | solution.py:33
  29.5 6.8 %collective-permute-start.12 = (bf16[128,512]{1,0:T(8,128)(2,1)S(1)}, bf16[128,512]{1,0:T(8,128)(2,1)S(1)}, u32[]{:S(2)}, u32[]{:S(2)}) collective-permute-start(bf16[128,512]{1,0:T(8,128)(2,1)S(1)} %get-tuple-element.34), channel_id=1, source_target_pairs={{0,3},{1,2},{2,1},{3,0},{4,7},{5,6},{6,5},{7,4},{8,11},{9,10},{10,... | collective-permute-start | bytes 393224 | tf_op jit(solution)/shard_map/ppermute | solution.py:33
  36.8 5.8 %collective-permute-start.13 = (bf16[128,512]{1,0:T(8,128)(2,1)S(1)}, bf16[128,512]{1,0:T(8,128)(2,1)S(1)}, u32[]{:S(2)}, u32[]{:S(2)}) collective-permute-start(bf16[128,512]{1,0:T(8,128)(2,1)S(1)} %get-tuple-element.36.refs_2_), channel_id=1, source_target_pairs={{0,1},{1,0},{2,3},{3,2},{4,5},{5,4},{6,7},{7,6},{8,9},{9,8},{10,11... | collective-permute-start | bytes 393224 | tf_op jit(solution)/shard_map/ppermute | solution.py:33
  38.1 7.5 %collective-permute-start.14 = (bf16[128,512]{1,0:T(8,128)(2,1)S(1)}, bf16[128,512]{1,0:T(8,128)(2,1)S(1)}, u32[]{:S(2)}, u32[]{:S(2)}) collective-permute-start(bf16[128,512]{1,0:T(8,128)(2,1)S(1)} %get-tuple-element.36.refs_2_), channel_id=1, source_target_pairs={{0,2},{1,3},{2,0},{3,1},{4,6},{5,7},{6,4},{7,5},{8,10},{9,11},{10,... | collective-permute-start | bytes 393224 | tf_op jit(solution)/shard_map/ppermute | solution.py:33
  39.0 7.2 %collective-permute-start.15 = (bf16[128,512]{1,0:T(8,128)(2,1)S(1)}, bf16[128,512]{1,0:T(8,128)(2,1)S(1)}, u32[]{:S(2)}, u32[]{:S(2)}) collective-permute-start(bf16[128,512]{1,0:T(8,128)(2,1)S(1)} %get-tuple-element.36.refs_2_), channel_id=1, source_target_pairs={{0,3},{1,2},{2,1},{3,0},{4,7},{5,6},{6,5},{7,4},{8,11},{9,10},{10,... | collective-permute-start | bytes 393224 | tf_op jit(solution)/shard_map/ppermute | solution.py:33
  40.4 5.8 %collective-permute-start.16 = (bf16[128,512]{1,0:T(8,128)(2,1)S(1)}, bf16[128,512]{1,0:T(8,128)(2,1)S(1)}, u32[]{:S(2)}, u32[]{:S(2)}) collective-permute-start(bf16[128,512]{1,0:T(8,128)(2,1)S(1)} %get-tuple-element.36.refs_2_), channel_id=1, source_target_pairs={{0,4},{4,0},{8,12},{12,8},{16,20},{20,16},{24,28},{28,24},{1,5},{5... | collective-permute-start | bytes 393224 | tf_op jit(solution)/shard_map/ppermute | solution.py:33
  45.6 1.3 %collective-permute-start.17 = (bf16[128,512]{1,0:T(8,128)(2,1)S(1)}, bf16[128,512]{1,0:T(8,128)(2,1)S(1)}, u32[]{:S(2)}, u32[]{:S(2)}) collective-permute-start(bf16[128,512]{1,0:T(8,128)(2,1)S(1)} %collective-permute-done.13.refs_3_), channel_id=1, source_target_pairs={{0,4},{4,0},{8,12},{12,8},{16,20},{20,16},{24,28},{28,24},{1,5},{5... | collective-permute-start | bytes 393224 | tf_op jit(solution)/shard_map/ppermute | solution.py:33
  45.6 1.5 %collective-permute-start.18 = (bf16[128,512]{1,0:T(8,128)(2,1)S(1)}, bf16[128,512]{1,0:T(8,128)(2,1)S(1)}, u32[]{:S(2)}, u32[]{:S(2)}) collective-permute-start(bf16[128,512]{1,0:T(8,128)(2,1)S(1)} %collective-permute-done.14.refs_4_), channel_id=1, source_target_pairs={{0,4},{4,0},{8,12},{12,8},{16,20},{20,16},{24,28},{28,24},{1,5},{5... | collective-permute-start | bytes 393224 | tf_op jit(solution)/shard_map/ppermute | solution.py:33
  46.1 1.3 %collective-permute-start.19 = (bf16[128,512]{1,0:T(8,128)(2,1)S(1)}, bf16[128,512]{1,0:T(8,128)(2,1)S(1)}, u32[]{:S(2)}, u32[]{:S(2)}) collective-permute-start(bf16[128,512]{1,0:T(8,128)(2,1)S(1)} %collective-permute-done.15.refs_5_), channel_id=1, source_target_pairs={{0,4},{4,0},{8,12},{12,8},{16,20},{20,16},{24,28},{28,24},{1,5},{5... | collective-permute-start | bytes 393224 | tf_op jit(solution)/shard_map/ppermute | solution.py:33
  47.9 9.2 %collective-permute-start.22 = (bf16[256,512]{1,0:T(8,128)(2,1)S(1)}, bf16[256,512]{1,0:T(8,128)(2,1)S(1)}, u32[]{:S(2)}, u32[]{:S(2)}) collective-permute-start(bf16[256,512]{1,0:T(8,128)(2,1)S(1)} %shard_map.100.refs_10_), channel_id=1, source_target_pairs={{24,16},{28,20},{0,8},{4,12},{16,24},{20,28},{8,0},{12,4},{25,17},... | collective-permute-start | bytes 786440 | tf_op jit(solution)/shard_map/ppermute | solution.py:29
  48.9 13.2 %collective-permute-start.20 = (bf16[256,512]{1,0:T(8,128)(2,1)S(1)}, bf16[256,512]{1,0:T(8,128)(2,1)S(1)}, u32[]{:S(2)}, u32[]{:S(2)}) collective-permute-start(bf16[256,512]{1,0:T(8,128)(2,1)S(1)} %shard_map.100.refs_10_), channel_id=1, source_target_pairs={{16,8},{20,12},{8,16},{12,20},{0,4},{4,0},{24,28},{28,24},{17,9},{... | collective-permute-start | bytes 786440 | tf_op jit(solution)/shard_map/ppermute | solution.py:29
  50.7 11.4 %collective-permute-start.21 = (bf16[256,512]{1,0:T(8,128)(2,1)S(1)}, bf16[256,512]{1,0:T(8,128)(2,1)S(1)}, u32[]{:S(2)}, u32[]{:S(2)}) collective-permute-start(bf16[256,512]{1,0:T(8,128)(2,1)S(1)} %get-tuple-element.42), channel_id=1, source_target_pairs={{8,0},{12,4},{16,24},{20,28},{24,8},{28,12},{0,16},{4,20},{9,1},{1... | collective-permute-start | bytes 786440 | tf_op jit(solution)/shard_map/ppermute | solution.py:29
  57.2 11.8 %collective-permute-start.23 = (bf16[256,512]{1,0:T(8,128)(2,1)S(1)}, bf16[256,512]{1,0:T(8,128)(2,1)S(1)}, u32[]{:S(2)}, u32[]{:S(2)}) collective-permute-start(bf16[256,512]{1,0:T(8,128)(2,1)S(1)} %shard_map.103), channel_id=1, source_target_pairs={{16,0},{20,4},{8,24},{12,28},{0,8},{4,12},{24,16},{28,20},{17,1},{... | collective-permute-start | bytes 786440 | tf_op jit(solution)/shard_map/ppermute | solution.py:29
  (7 other events, 26.7 us)
